TPU v7x, 256 devices: a whole 4x4x8 slice. The times are simulated.
256 devices in a mesh: member: 4 (over y), grid: 16 (over z_lo, x, core), dp: 4 (over z_hi).
Axes of the slice: x: 4, y: 4, z: 8 (z_hi: 4, z_lo: 2; z = z_hi * 2 + z_lo), core: 2. Of those that a mesh axis runs over, the one named last changes fastest.
Arguments:
- latents: bfloat16 [4, 16, 4096, 1024], P('dp', 'member', 'grid'), may hold values from -10 to 10
- w_in: bfloat16 [1024, 1024], replicated, may hold values from -0.1875 to 0.1875
- b_in: float32 [1024], replicated, may hold values from -4 to 4
- w_out: bfloat16 [1024, 100], replicated, may hold values from -0.1875 to 0.1875
- b_out: float32 [100], replicated, may hold values from -4 to 4
- targets: float32 [4, 100, 4096], P('dp', None, ('grid', 'member')), may hold values from -6 to 6
- area: float32 [4096], P(('grid', 'member')), may hold values from 0.3 to 9
- var_weight: float32 [100], replicated, may hold values from 0.3 to 3
- member_rank: int32 [4, 16, 100, 4096], P('dp', None, None, ('grid', 'member')), may hold values from 0 to 15, as said below
- obs_rank: int32 [4, 100, 4096], P('dp', None, ('grid', 'member')), may hold values from 0 to 16
Outputs:
- loss: float32 [4], P('dp')
- grad_w_in: float32 [1024, 1024], P(('member', 'grid', 'dp'))
- grad_w_out: float32 [1024, 100], replicated
- grad_b_in: float32 [1024], replicated
- grad_b_out: float32 [100], replicated
Inputs may be any that keep to these rules, and one draw needn't show every extreme that they name: For each sample, variable and point, member_rank over the 16 members is a permutation of 0 to 15.
All inputs are finite; a program needn't handle non-finite values.
Results may differ from a plain program's by a relative error of at most 0.0031.
Values may be sent and summed in bfloat16 or wider, within the bound.
No kernel may reach another device: no remote copies, remote signals or barrier semaphores. Data moves between devices by JAX's collectives and lax.ppermute only.
A program may use at most 64 MiB of HBM per device.

v0:
```python
import math

import jax
import jax.numpy as jnp
from jax import lax
from jax.sharding import PartitionSpec as P

ALPHA = 0.95


def per_device(latents, w_in, b_in, w_out, b_out, targets, area, var_weight, member_rank, obs_rank):
    mem_dev = latents.shape[1]
    pts_dev = latents.shape[2]
    width = latents.shape[3]
    hid_width = w_in.shape[1]
    n_vars = w_out.shape[1]
    rows_x = latents.reshape(mem_dev * pts_dev, width)
    pre = jnp.dot(rows_x, w_in, preferred_element_type=jnp.float32) + b_in
    hidden = jax.nn.gelu(pre).astype(jnp.bfloat16)
    hidden3 = hidden.reshape(mem_dev, pts_dev, hid_width)
    values = (
        jnp.einsum("mph,hv->mvp", hidden3, w_out, preferred_element_type=jnp.float32)
        + b_out[None, :, None]
    ).astype(jnp.bfloat16)
    ensemble = lax.all_to_all(values, "member", split_axis=2, concat_axis=0, tiled=True)
    n_mem = ensemble.shape[0]
    ens = ensemble.astype(jnp.float32)
    epsil = (1.0 - ALPHA) / n_mem
    truth = targets[0]
    skill = jnp.sum(jnp.abs(ens - truth[None]), axis=0)
    spread = jnp.zeros_like(skill)
    for first in range(n_mem):
        spread = spread + jnp.sum(jnp.abs(ens[first : first + 1] - ens), axis=0)
    weight = area[None, :] * var_weight[:, None]
    local_loss = jnp.sum(
        weight * (skill / n_mem - (1.0 - epsil) / (2.0 * n_mem * (n_mem - 1)) * spread)
    )
    total = lax.psum(local_loss, ("member", "grid"))
    n_points = pts_dev * lax.axis_size("grid")
    loss = (total / (n_points * n_vars)).reshape(1)
    ranks = member_rank[0]
    sign = jnp.where(ranks >= obs_rank[0][None], 1.0, -1.0).astype(jnp.float32)
    centred = (2 * ranks - n_mem + 1).astype(jnp.float32)
    cotangent = (weight[None] * (sign - (1.0 - epsil) / (n_mem - 1) * centred)).astype(jnp.bfloat16)
    back = lax.all_to_all(cotangent, "member", split_axis=0, concat_axis=2, tiled=True)
    scale = 1.0 / math.sqrt(lax.axis_size("dp") * n_mem * n_points)
    upward = jnp.einsum("mvp,hv->mph", back, w_out, preferred_element_type=jnp.float32)
    pullback = jax.vjp(jax.nn.gelu, pre)[1]
    dhidden = pullback(upward.reshape(mem_dev * pts_dev, hid_width))[0].astype(jnp.bfloat16)
    grad_out = jnp.einsum("mph,mvp->hv", hidden3, back, preferred_element_type=jnp.float32) * scale
    grad_bout = jnp.sum(back.astype(jnp.float32), axis=(0, 2)) * scale
    grad_bin = jnp.sum(dhidden.astype(jnp.float32), axis=0) * scale
    grad_out, grad_bin, grad_bout = lax.psum(
        (grad_out, grad_bin, grad_bout), ("member", "grid", "dp")
    )
    grad_in = lax.psum_scatter(
        jnp.einsum("rl,rh->lh", rows_x, dhidden, preferred_element_type=jnp.float32) * scale,
        ("member", "grid", "dp"),
        scatter_dimension=0,
        tiled=True,
    )
    return (loss, grad_in, grad_out, grad_bin, grad_bout)


def solution(mesh):
    in_specs = (
        P("dp", "member", "grid", None),
        P(),
        P(),
        P(),
        P(),
        P("dp", None, ("grid", "member")),
        P(("grid", "member")),
        P(),
        P("dp", None, None, ("grid", "member")),
        P("dp", None, ("grid", "member")),
    )
    out_specs = (P("dp"), P(("member", "grid", "dp"), None), P(), P(), P())
    return jax.shard_map(
        per_device, mesh=mesh, in_specs=in_specs, out_specs=out_specs, check_vma=False
    )
```

profile of v0, /device:TPU:1, one launch (start us, length us, event | category | flops | bytes accessed | tf_op | source)
XLA Modules:
  0.0 332.8 jit_solution(16528571863491468570)
XLA Ops:
  7.2 0.0 copy-start
  7.2 0.0 all-reduce.5.cloned.1.call-start
  7.2 1.5 copy-done
  8.8 6.6 %multiply_convert_fusion = (bf16[1024,1024]{1,0:T(8,128)(2,1)S(1)}, f32[1024,1024]{1,0:T(8,128)}) fusion(f32[1024]{0:T(1024)} %param.12, bf16[1024,1024]{1,0:T(8,128)(2,1)S(1)} %bitcast.91, bf16[1024,1024]{1,0:T(8,128)(2,1)} %param.11), kind=kOutput, calls=%fused_computation.11 | convolution fusion | flops 2157969408 | bytes 10489856 | tf_op jit(solution)/shard_map/dot_general | solution.py:18
  15.4 1.3 copy-done.1
  16.7 0.8 fusion.9
  17.5 0.2 copy.24
  17.7 10.5 %all_to_all.27 = bf16[4,100,256]{1,0,2:T(4,128)(2,1)S(1)} all-to-all(bf16[4,100,256]{1,0,2:T(4,128)(2,1)S(1)} %copy.24), channel_id=1, replica_groups=mesh['member'=4,'grid'=16,'dp'=4] {'member'}, dimensions={2} | all-to-all | bytes 409600 | tf_op jit(solution)/shard_map/all_to_all | solution.py:25
  28.2 0.1 convert_bitcast_fusion
  28.4 1.2 fusion.11
  29.7 0.7 broadcast_multiply_fusion
  30.4 0.2 fusion.49
  30.5 7.9 %all_to_all.28 = bf16[16,100,64]{1,2,0:T(8,128)(2,1)S(1)} all-to-all(bf16[16,100,64]{1,2,0:T(8,128)(2,1)S(1)} %fusion.49), channel_id=1, replica_groups=mesh['member'=4,'grid'=16,'dp'=4] {'member'}, dimensions={0} | all-to-all | bytes 409600 | tf_op jit(solution)/shard_map/all_to_all | solution.py:45
  38.5 1.3 fusion.7
  39.7 3.4 %convert_reduce_fusion = (f32[1024]{0:T(1024)S(1)}, bf16[1024,1024]{1,0:T(8,128)(2,1)S(1)}) fusion(f32[1024,1024]{1,0:T(8,128)S(1)} %copy-done.11, f32[1024]{0:T(1024)S(1)} %copy-done.10, bf16[1024,100]{1,0:T(8,128)(2,1)S(1)} %bitcast.99, bf16[1024,100]{0,1:T(8,128)(2,1)S(1)} %copy-done.4), kind=kOutput, calls=%fused_computation.9 | convolution fusion | flops 233831424 | bytes 6709248 | tf_op jit(solution)/shard_map/mvp,hv->mph/dot_general | solution.py:47
  43.1 4.4 %multiply_bitcast_fusion = f32[1024,1024]{0,1:T(8,128)} fusion(bf16[1024,1024]{1,0:T(8,128)(2,1)S(1)} %get-tuple-element.64, bf16[1024,1024]{1,0:T(8,128)(2,1)S(1)} %bitcast.92), kind=kOutput, calls=%fused_computation.10 | convolution fusion | flops 2148532224 | bytes 8388608 | tf_op jit(solution)/shard_map/rl,rh->lh/dot_general | solution.py:57
  47.5 0.0 all-reduce.5.cloned.1.call-update
  47.5 141.9 %psum.28 = f32[]{:T(128)} all-reduce(f32[]{:T(128)} %get-tuple-element.60), channel_id=1, replica_groups=mesh['member'=4,'grid'=16,'dp'=4] {'member','grid'}, use_global_device_ids=true, to_apply=%region_18.0 | all-reduce | flops 1 | bytes 8 | tf_op jit(solution)/shard_map/psum | solution.py:38
  190.1 0.2 convert_reduce_fusion.1
  190.2 76.5 %all-reduce.1 = (f32[1024]{0:T(1024)}, f32[100]{0:T(128)}) all-reduce(f32[1024]{0:T(1024)S(1)} %broadcast_multiply_fusion.1, f32[100]{0:T(128)S(1)} %broadcast_multiply_fusion.2), channel_id=1, replica_groups=mesh['member'=4,'grid'=16,'dp'=4] {'member','grid','dp'}, use_global_device_ids=true, to_apply=%region_22.23 | all-reduce | flops 1124 | bytes 8992 | tf_op jit(solution)/shard_map/psum | solution.py:53
  266.8 54.2 %all-reduce.5.cloned.1.call-done = (f32[1024,1024]{0,1:T(8,128)}, f32[1024,100]{0,1:T(8,128)}) async-done(((f32[1024,1024]{0,1:T(8,128)}, f32[1024,100]{0,1:T(8,128)}), (f32[1024,1024]{0,1:T(8,128)}, f32[1024,100]{0,1:T(8,128)})) %all-reduce.5.cloned.1.call-update) | async-done | bytes 4603920
  320.9 1.2 constant_dynamic-slice_fusion
  322.2 0.8 copy.30
  323.0 1.8 copy.40
  (26 shorter events, 0.2 us)
Async XLA Ops:
  7.2 1.6 copy-start
  7.2 313.8 %all-reduce.5.cloned.1.call-start = ((), (), s32[]{:S(2)}) async-start(), calls=%async_computation.2 | async-start | bytes 9240576
  8.8 7.9 %copy-start.4 = (bf16[1024,100]{0,1:T(8,128)(2,1)S(1)}, bf16[1024,100]{0,1:T(8,128)(2,1)}, u32[]{:S(2)}) copy-start(bf16[1024,100]{0,1:T(8,128)(2,1)} %param.13) | copy-start | bytes 614404
  8.8 7.9 %copy-start.9 = (f32[100]{0:T(128)S(1)}, f32[100]{0:T(128)}, u32[]{:S(2)}) copy-start(f32[100]{0:T(128)} %param.14) | copy-start | bytes 1204
  15.4 1.3 copy-start.1
  15.4 13.0 %copy-start.5 = (f32[1,100,64]{1,2,0:T(8,128)S(1)}, f32[1,100,64]{1,2,0:T(8,128)}, u32[]{:S(2)}) copy-start(f32[1,100,64]{1,2,0:T(8,128)} %param.15) | copy-start | bytes 76804
  15.4 14.3 %copy-start.7 = (f32[100]{0:T(128)S(1)}, f32[100]{0:T(128)}, u32[]{:S(2)}) copy-start(f32[100]{0:T(128)} %param.17) | copy-start | bytes 1204
  15.4 14.3 %copy-start.8 = (f32[64]{0:T(128)S(1)}, f32[64]{0:T(128)}, u32[]{:S(2)}) copy-start(f32[64]{0:T(128)} %param.16) | copy-start | bytes 772
  16.7 13.6 %copy-start.3 = (s32[1,16,100,64]{2,3,1,0:T(8,128)S(1)}, s32[1,16,100,64]{2,3,1,0:T(8,128)}, u32[]{:S(2)}) copy-start(s32[1,16,100,64]{2,3,1,0:T(8,128)} %param.18) | copy-start | bytes 1228804
  16.7 13.6 %copy-start.6 = (s32[1,100,64]{1,2,0:T(8,128)S(1)}, s32[1,100,64]{1,2,0:T(8,128)}, u32[]{:S(2)}) copy-start(s32[1,100,64]{1,2,0:T(8,128)} %param.19) | copy-start | bytes 76804
  17.7 20.7 %copy-start.2 = (bf16[1024,1024]{1,0:T(8,128)(2,1)S(1)}, bf16[1024,1024]{1,0:T(8,128)(2,1)}, u32[]{:S(2)}) copy-start(bf16[1024,1024]{1,0:T(8,128)(2,1)} %copy-done.1) | copy-start | bytes 6291460
  28.4 11.3 %copy-start.10 = (f32[1024]{0:T(1024)S(1)}, f32[1024]{0:T(1024)}, u32[]{:S(2)}) copy-start(f32[1024]{0:T(1024)} %param.12) | copy-start | bytes 12292
  28.4 11.3 %copy-start.11 = (f32[1024,1024]{1,0:T(8,128)S(1)}, f32[1024,1024]{1,0:T(8,128)}, u32[]{:S(2)}) copy-start(f32[1024,1024]{1,0:T(8,128)} %get-tuple-element.62) | copy-start | bytes 12582916
Sparse Core Ops, SparseCore 0:
  47.7 273.2 all-reduce.4
where the time goes:
time: 334 us; the launch traced here: 333 us
  blocking collectives  237 us (71%)
  waiting for transfers between devices  54.2 us (16%)
  matrix products  16.4 us (5%)
  between operations  16 us (5%)
  local copies, waits for them, and re-layouts  7.03 us (2%)
    psum x1, blocking collectives, per_device(): total = lax.psum(local_loss, ('member', 'grid'))  142 us
    psum x1, blocking collectives, per_device(): lax.psum((grad_out, grad_bin, grad_bout), ('member', 'grid', 'dp'))  76.5 us
    unnamed x2, waiting for transfers between devices  54.2 us
    all_to_all x1, blocking collectives, per_device(): lax.all_to_all(values, 'member', split_axis=2, concat_axis=0, tiled=True)  10.5 us
    all_to_all x1, blocking collectives, per_device(): lax.all_to_all(cotangent, 'member', split_axis=0, concat_axis=2, tiled=True)  7.92 us
    unnamed x27, local copies, waits for them, and re-layouts  6.73 us
  transfers between devices with their start and end apart: 1, of which 1 were waited for; matrix products, arithmetic and copies ran while one was open for 0% of the time, Pallas kernels for 0%

commit v1 on v0

v1 whole, which is shorter than its diff:
```python
import math

import jax
import jax.numpy as jnp
from jax import lax
from jax.sharding import Mesh
from jax.sharding import PartitionSpec as P

ALPHA = 0.95
NAMES = ("y", "zlo", "x", "core", "zhi")
PLANE = ("y", "zlo", "x")
GRID = ("zlo", "x", "core")


def shift(axis, step):
    size = lax.axis_size(axis)
    return [(i, (i + step) % size) for i in range(size)]


def exchange(blocks, axis):
    size = blocks.shape[0]
    me = lax.axis_index(axis)
    out = blocks
    for step in range(1, size):
        part = lax.dynamic_index_in_dim(blocks, (me + step) % size, 0, keepdims=False)
        got = lax.ppermute(part, axis, shift(axis, step))
        out = lax.dynamic_update_index_in_dim(out, got, (me - step) % size, 0)
    return out


def low_part(value):
    return value - lax.reduce_precision(value, 8, 7)


def pack(extra):
    return jnp.concatenate(
        [extra, low_part(extra[:, 100:]), jnp.zeros((extra.shape[0], 22), jnp.float32)], axis=1
    ).astype(jnp.bfloat16)


def unpack(packed):
    wide = packed.astype(jnp.float32)
    low = jnp.pad(wide[..., 103:106], [(0, 0)] * (wide.ndim - 1) + [(100, 0)])
    return wide[..., :103] + low


def per_device(latents, w_in, b_in, w_out, b_out, targets, area, var_weight, member_rank, obs_rank):
    mem_dev = latents.shape[1]
    pts_dev = latents.shape[2]
    width = latents.shape[3]
    hid = w_in.shape[1]
    n_vars = w_out.shape[1]
    n_y = lax.axis_size("y")
    n_mem = mem_dev * n_y
    sub = pts_dev // n_y
    n_points = pts_dev * lax.axis_size(GRID)
    core = lax.axis_index("core")
    zhi = lax.axis_index("zhi")
    epsil = (1.0 - ALPHA) / n_mem
    scale = 1.0 / math.sqrt(lax.axis_size("zhi") * n_mem * n_points)

    weight = area[None, :] * var_weight[:, None]
    ranks = member_rank[0]
    sign = jnp.where(ranks >= obs_rank[0][None], 1.0, -1.0).astype(jnp.float32)
    centred = (2 * ranks - n_mem + 1).astype(jnp.float32)
    cot = (weight[None] * (sign - (1.0 - epsil) / (n_mem - 1) * centred)).astype(jnp.bfloat16)
    part_bout = jnp.sum(cot.astype(jnp.float32), axis=(0, 2))
    back = exchange(cot.reshape(n_y, mem_dev, n_vars, sub), "y")
    back = back.transpose(1, 2, 0, 3).reshape(mem_dev, n_vars, pts_dev)

    rows_x = latents.reshape(mem_dev * pts_dev, width)
    pre = jnp.dot(rows_x, w_in, preferred_element_type=jnp.float32) + b_in
    hidden = jax.nn.gelu(pre).astype(jnp.bfloat16)
    hidden3 = hidden.reshape(mem_dev, pts_dev, hid)
    values = (
        jnp.einsum("mph,hv->mvp", hidden3, w_out, preferred_element_type=jnp.float32)
        + b_out[None, :, None]
    ).astype(jnp.bfloat16)
    sent = values.reshape(mem_dev, n_vars, n_y, sub).transpose(2, 0, 1, 3)
    ens = exchange(sent, "y").reshape(n_mem, n_vars, sub).astype(jnp.float32)
    skill = jnp.sum(jnp.abs(ens - targets[0][None]), axis=0)
    spread = jnp.zeros_like(skill)
    for first in range(n_mem):
        spread = spread + jnp.sum(jnp.abs(ens[first : first + 1] - ens), axis=0)
    part_loss = jnp.sum(
        weight * (skill / n_mem - (1.0 - epsil) / (2.0 * n_mem * (n_mem - 1)) * spread)
    )

    upward = jnp.einsum("mvp,hv->mph", back, w_out, preferred_element_type=jnp.float32)
    pullback = jax.vjp(jax.nn.gelu, pre)[1]
    dhidden = pullback(upward.reshape(mem_dev * pts_dev, hid))[0].astype(jnp.bfloat16)
    part_out = jnp.einsum("mph,mvp->hv", hidden3, back, preferred_element_type=jnp.float32)
    part_bin = jnp.sum(dhidden.astype(jnp.float32), axis=0)
    part_in = jnp.einsum("rl,rh->lh", rows_x, dhidden, preferred_element_type=jnp.float32)

    extra = jnp.concatenate(
        [
            part_out,
            part_bin[:, None],
            jnp.pad(part_bout, (0, hid - n_vars))[:, None],
            jnp.where(jnp.arange(hid) == zhi, part_loss, 0.0)[:, None],
        ],
        axis=1,
    )

    n_plane = lax.axis_size(PLANE)
    block = width // (2 * n_plane)
    in4 = part_in.reshape(n_plane, 2, block, hid)
    ex4 = extra.reshape(n_plane, 2, block, 103)
    other = [(0, 1), (1, 0)]
    pick = lambda arr, which: lax.dynamic_index_in_dim(arr, which, 1, keepdims=False)
    got_in = lax.ppermute(pick(in4, 1 - core).astype(jnp.bfloat16), "core", other)
    got_ex = lax.ppermute(pick(ex4, 1 - core), "core", other)
    half_in = pick(in4, core) + got_in.astype(jnp.float32)
    half_ex = pick(ex4, core) + got_ex

    packed = pack(half_ex.reshape(n_plane * block, 103)).reshape(n_plane, block, 128)
    payload = jnp.concatenate([half_in.astype(jnp.bfloat16), packed], axis=2)
    landed = lax.all_to_all(payload, PLANE, 0, 0, tiled=True)
    sum_in = jnp.sum(landed[..., :hid].astype(jnp.float32), axis=0)
    sum_ex = jnp.sum(unpack(landed[..., hid:]), axis=0)

    n_zhi = lax.axis_size("zhi")
    rows4 = sum_in.reshape(n_zhi, block // n_zhi, hid)
    sum_ex = jnp.pad(sum_ex, ((0, 0), (0, 25)))
    total_in = lax.dynamic_index_in_dim(rows4, zhi, 0, keepdims=False)
    from_zhi = jnp.broadcast_to(sum_ex[None], (n_zhi, block, 128))
    for step in range(1, n_zhi):
        part = lax.dynamic_index_in_dim(rows4, (zhi + step) % n_zhi, 0, keepdims=False)
        both = jnp.concatenate([part.reshape(-1, 128), sum_ex], axis=0)
        got = lax.ppermute(both, "zhi", shift("zhi", step))
        total_in = total_in + got[: -block].reshape(block // n_zhi, hid)
        source = (zhi - step) % n_zhi
        from_zhi = lax.dynamic_update_index_in_dim(from_zhi, got[-block:], source, 0)
    total_ex = jnp.sum(from_zhi, axis=0)

    copies = jnp.broadcast_to(total_ex[None], (n_plane, block, 128))
    mine = lax.all_to_all(copies, PLANE, 0, 0, tiled=True)
    theirs = lax.ppermute(mine, "core", other)
    first = jnp.where(core == 0, mine, theirs)
    second = jnp.where(core == 0, theirs, mine)
    full = jnp.stack([first, second], axis=1).reshape(hid, 128)
    grad_out = full[:, :n_vars] * scale
    grad_bin = full[:, n_vars] * scale
    grad_bout = full[:n_vars, n_vars + 1] * scale
    loss = lax.dynamic_slice(full[:, n_vars + 2], (zhi,), (1,)) / (n_points * n_vars)
    return (loss, total_in * scale, grad_out, grad_bin, grad_bout)


def solution(mesh):
    split = Mesh(mesh.devices.reshape(4, 2, 4, 2, 4), NAMES)
    points = GRID + ("y",)
    in_specs = (
        P("zhi", "y", GRID, None),
        P(),
        P(),
        P(),
        P(),
        P("zhi", None, points),
        P(points),
        P(),
        P("zhi", None, None, points),
        P("zhi", None, points),
    )
    out_specs = (P("zhi"), P(NAMES, None), P(), P(), P())
    return jax.shard_map(
        per_device, mesh=split, in_specs=in_specs, out_specs=out_specs, check_vma=False
    )
```

time: 334 us -> 120 us (0.36)
  blocking collectives: 237 us -> 13.7 us
  starting transfers between devices: 0.04 us -> 34 us
  waiting for transfers between devices: 54.2 us -> 26.5 us
  between operations: 16 us -> 1.13 us
  local copies, waits for them, and re-layouts: 7.03 us -> 16.9 us
  other arithmetic: 2.27 us -> 11.3 us
    psum x2 -> x0, blocking collectives: 218 us -> none  [the longest x1 142 us: per_device(): total = lax.psum(local_loss, ('member', 'grid'))]
    unnamed x2 -> x0, waiting for transfers between devices: 54.2 us -> none
    ppermute x0 -> x12, starting transfers between devices: none -> 26.1 us  [the longest x3 9.67 us: per_device(): got = lax.ppermute(both, 'zhi', shift('zhi', step))]
    all_to_all x0 -> x1, waiting for transfers between devices: none -> 17.4 us  [per_device(): landed = lax.all_to_all(payload, PLANE, 0, 0, tiled=True)]
    ppermute x0 -> x12, waiting for transfers between devices: none -> 9.09 us  [the longest x6 5.65 us: exchange(): got = lax.ppermute(part, axis, shift(axis, step))]
    all_to_all x0 -> x1, starting transfers between devices: none -> 7.87 us  [per_device(): landed = lax.all_to_all(payload, PLANE, 0, 0, tiled=True)]
    all_to_all x2 -> x1, blocking collectives: 18.4 us -> 13.7 us  [per_device(): mine = lax.all_to_all(copies, PLANE, 0, 0, tiled=True)]
    concatenate x0 -> x3, local copies, waits for them, and re-layouts: none -> 4.32 us  [the longest x2 2.32 us: per_device(): jnp.concatenate([part_out, part_bin[:, None], jnp.pad(part_bout, (0, hid...]
  transfers between devices with their start and end apart: 1 -> 13, of which waited for: 1 -> 7; matrix products, arithmetic and copies ran while one was open for 0% -> 10% of each run, Pallas kernels for 0% -> 0%
where the time goes in v1:
time: 120 us; the launch traced here: 119 us
  starting transfers between devices  34 us (28%)
  waiting for transfers between devices  26.5 us (22%)
  local copies, waits for them, and re-layouts  16.9 us (14%)
  matrix products  15.6 us (13%)
  blocking collectives  13.7 us (11%)
  other arithmetic  11.3 us (9%)
    all_to_all x1, waiting for transfers between devices, per_device(): landed = lax.all_to_all(payload, PLANE, 0, 0, tiled=True)  17.4 us
    all_to_all x1, blocking collectives, per_device(): mine = lax.all_to_all(copies, PLANE, 0, 0, tiled=True)  13.7 us
    ppermute x3, starting transfers between devices, per_device(): got = lax.ppermute(both, 'zhi', shift('zhi', step))  9.67 us
    ppermute x6, starting transfers between devices, exchange(): got = lax.ppermute(part, axis, shift(axis, step))  8.02 us
    all_to_all x1, starting transfers between devices, per_device(): landed = lax.all_to_all(payload, PLANE, 0, 0, tiled=True)  7.87 us
    dot_general x1, matrix products, per_device(): pre = jnp.dot(rows_x, w_in, preferred_element_type=jnp.float32) + b_in  6.61 us
    unnamed x21, local copies, waits for them, and re-layouts  5.81 us
    ppermute x6, waiting for transfers between devices, exchange(): got = lax.ppermute(part, axis, shift(axis, step))  5.65 us
  transfers between devices with their start and end apart: 13, of which 7 were waited for; matrix products, arithmetic and copies ran while one was open for 10% of the time, Pallas kernels for 0%

profile of v1, /device:TPU:1, one launch (start us, length us, event | category | flops | bytes accessed | tf_op | source)
XLA Modules:
  0.0 119.1 jit_solution(2586653843144242624)
XLA Ops:
  0.7 1.5 %copy-done = bf16[1,4,256,1024]{3,2,1,0:T(8,128)(2,1)S(1)} copy-done((bf16[1,4,256,1024]{3,2,1,0:T(8,128)(2,1)S(1)}, bf16[1,4,256,1024]{3,2,1,0:T(8,128)(2,1)}, u32[]{:S(2)}) %copy-start) | copy-done | bytes 2097176
  2.2 6.6 %multiply_convert_fusion = (bf16[1024,1024]{1,0:T(8,128)(2,1)S(1)}, f32[1024,1024]{1,0:T(8,128)}) fusion(f32[1024]{0:T(1024)} %param.12, bf16[1024,1024]{1,0:T(8,128)(2,1)S(1)} %bitcast.164, bf16[1024,1024]{1,0:T(8,128)(2,1)} %param.11), kind=kOutput, calls=%fused_computation.10 | convolution fusion | flops 2157969408 | bytes 10489856 | tf_op jit(solution)/shard_map/dot_general | solution.py:72
  11.2 2.2 %collective-permute-start.4 = (bf16[4,100,64]{1,2,0:T(8,128)(2,1)S(1)}, bf16[4,100,64]{1,2,0:T(8,128)(2,1)S(1)}, u32[]{:S(2)}, u32[]{:S(2)}) collective-permute-start(bf16[4,100,64]{1,2,0:T(8,128)(2,1)S(1)} %get-tuple-element.56), channel_id=1, source_target_pairs={{0,64},{64,128},{128,192},{192,0},{1,65},{65,129},{129,193},{193,1... | collective-permute-start | bytes 153608 | tf_op jit(solution)/shard_map/ppermute | solution.py:26
  13.4 2.6 %collective-permute-start.5 = (bf16[4,100,64]{1,2,0:T(8,128)(2,1)S(1)}, bf16[4,100,64]{1,2,0:T(8,128)(2,1)S(1)}, u32[]{:S(2)}, u32[]{:S(2)}) collective-permute-start(bf16[4,100,64]{1,2,0:T(8,128)(2,1)S(1)} %get-tuple-element.55), channel_id=1, source_target_pairs={{0,128},{64,192},{128,0},{192,64},{1,129},{65,193},{129,1},{193,65... | collective-permute-start | bytes 153608 | tf_op jit(solution)/shard_map/ppermute | solution.py:26
  17.1 4.0 %copy.37 = bf16[4,256,1024]{1,2,0:T(8,128)(2,1)} copy(bf16[4,256,1024]{2,1,0:T(8,128)(2,1)} %bitcast.170) | data formatting | bytes 4194304 | tf_op jit(solution)/shard_map/reshape | solution.py:74
  22.5 1.4 %multiply_reduce_fusion = (f32[]{:T(128)}, f32[100,64]{0,1:T(8,128)S(1)}) fusion(f32[100,64]{0,1:T(8,128)S(1)} %get-tuple-element.31, f32[100,64]{0,1:T(8,128)S(1)} %get-tuple-element.30, f32[100,64]{0,1:T(8,128)S(1)} %get-tuple-element.29, f32[100,64]{0,1:T(8,128)S(1)} %get-tuple-element.28, f32[100,64]{0,1:T(8,128)S(1)} %get-tuple-element.27, ...), kind=kLoop, calls=%fused_computation.133 | loop fusion | flops 134399 | bytes 461460 | tf_op jit(solution)/shard_map/reduce_sum | solution.py:85
  24.8 3.7 %collective-permute-done = bf16[4,100,64]{1,2,0:T(8,128)(2,1)S(1)} collective-permute-done((bf16[4,100,64]{1,2,0:T(8,128)(2,1)S(1)}, bf16[4,100,64]{1,2,0:T(8,128)(2,1)S(1)}, u32[]{:S(2)}, u32[]{:S(2)}) %collective-permute-start) | collective-permute-done | bytes 51232 | tf_op jit(solution)/shard_map/ppermute | solution.py:26
  30.6 1.6 %collective-permute-start.2 = (bf16[4,100,64]{1,2,0:T(8,128)(2,1)S(1)}, bf16[4,100,64]{1,2,0:T(8,128)(2,1)S(1)}, u32[]{:S(2)}, u32[]{:S(2)}) collective-permute-start(bf16[4,100,64]{1,2,0:T(8,128)(2,1)S(1)} %get-tuple-element.57), channel_id=1, source_target_pairs={{0,192},{64,0},{128,64},{192,128},{1,193},{65,1},{129,65},{193,129... | collective-permute-start | bytes 153608 | tf_op jit(solution)/shard_map/ppermute | solution.py:26
  34.1 5.0 %convert_reduce_fusion = (f32[1024]{0:T(1024)S(1)}, bf16[1024,1024]{1,0:T(8,128)(2,1)S(1)}) fusion(f32[1024,1024]{1,0:T(8,128)} %get-tuple-element.69, f32[1024]{0:T(1024)S(1)} %copy-done.9, bf16[1024,100]{1,0:T(8,128)(2,1)S(1)} %bitcast.180, bf16[1024,100]{0,1:T(8,128)(2,1)S(1)} %copy-done.5), kind=kOutput, calls=%fused_computation.9 | convolution fusion | flops 233831424 | bytes 6709248 | tf_op jit(solution)/shard_map/mvp,hv->mph/dot_general | solution.py:89
  39.0 2.5 %fusion.67 = f32[1024,1024]{0,1:T(8,128)S(1)} fusion(bf16[1024,1024]{1,0:T(8,128)(2,1)S(1)} %get-tuple-element.71, bf16[1024,1024]{1,0:T(8,128)(2,1)S(1)} %bitcast.165), kind=kOutput, calls=%fused_computation.151 | convolution fusion | flops 2147483648 | bytes 8388608 | tf_op jit(solution)/shard_map/rl,rh->lh/dot_general | solution.py:94
  41.6 1.9 %copy-done.2 = f32[1024,1024]{0,1:T(8,128)} copy-done((f32[1024,1024]{0,1:T(8,128)}, f32[1024,1024]{0,1:T(8,128)S(1)}, u32[]{:S(2)}) %copy-start.2) | copy-done | bytes 4194328
  44.6 4.3 %collective-permute-start.3 = (bf16[32,16,1024]{2,1,0:T(8,128)(2,1)}, bf16[32,16,1024]{2,1,0:T(8,128)(2,1)}, u32[]{:S(2)}, u32[]{:S(2)}) collective-permute-start(bf16[32,16,1024]{2,1,0:T(8,128)(2,1)} %fusion.12), channel_id=1, source_target_pairs={{0,4},{4,0},{1,5},{5,1},{2,6},{6,2},{3,7},{7,3},{8,12},{12,8},{9,1... | collective-permute-start | bytes 3145736 | tf_op jit(solution)/shard_map/ppermute | solution.py:112
  51.6 1.8 %pad_maximum_fusion = f32[32,2,16,103]{3,2,1,0:T(8,128)S(1)} fusion(f32[32,2,16,1]{3,2,1,0:T(8,128)S(1)} %fusion.54, f32[32,2,16,1]{3,2,1,0:T(8,128)} %concatenate.35, f32[32,2,16,1]{3,2,1,0:T(8,128)} %concatenate.34, f32[32,2,16,100]{3,2,1,0:T(8,128)} %bitcast.175), kind=kLoop, calls=%fused_computation.75 | loop fusion | flops 316416 | bytes 843776 | tf_op jit(solution)/shard_map/concatenate | solution.py:96
  53.6 1.5 %collective-permute-done.7 = f32[32,16,103]{2,1,0:T(8,128)S(1)} collective-permute-done((f32[32,16,103]{2,1,0:T(8,128)S(1)}, f32[32,16,103]{2,1,0:T(8,128)S(1)}, u32[]{:S(2)}, u32[]{:S(2)}) %collective-permute-start.7) | collective-permute-done | bytes 210976 | tf_op jit(solution)/shard_map/ppermute | solution.py:113
  55.3 2.3 %fusion.9 = bf16[32,16,1024]{2,1,0:T(8,128)(2,1)S(1)} fusion(bf16[32,16,1024]{2,1,0:T(8,128)(2,1)} %collective-permute-done.3, f32[32,2,16,1024]{3,2,1,0:T(8,128)} %bitcast.174, s32[]{:T(128)S(6)} %select_n.170), kind=kLoop, calls=%fused_computation.31 | loop fusion | flops 1572864 | bytes 4194308 | tf_op jit(solution)/shard_map/convert_element_type | solution.py:118
  57.7 2.0 %concatenate.30 = bf16[32,16,1152]{2,1,0:T(8,128)(2,1)} concatenate(bf16[32,16,1024]{2,1,0:T(8,128)(2,1)S(1)} %fusion.9, bf16[32,16,103]{2,1,0:T(8,128)(2,1)S(1)} %get-tuple-element.32, bf16[32,16,3]{2,1,0:T(8,128)(2,1)S(1)} %bitcast.182, bf16[32,16,22]{2,1,0:T(8,128)(2,1)S(1)} %broadcast_in_dim.84), dimensions={2} | concatenate | bytes 2359296 | tf_op jit(solution)/shard_map/concatenate | solution.py:118
  59.7 7.9 %all-to-all-start = ((bf16[32,16,1152]{2,1,0:T(8,128)(2,1)}), bf16[32,16,1152]{2,1,0:T(8,128)(2,1)S(1)}, u32[]{:S(2)}, u32[]{:S(2)}) async-start(bf16[32,16,1152]{2,1,0:T(8,128)(2,1)} %concatenate.30), calls=%async_computation | async-start | bytes 2359296 | tf_op jit(solution)/shard_map/all_to_all | solution.py:119
  67.6 17.4 %all-to-all-done = bf16[32,16,1152]{2,1,0:T(8,128)(2,1)S(1)} async-done(((bf16[32,16,1152]{2,1,0:T(8,128)(2,1)}), bf16[32,16,1152]{2,1,0:T(8,128)(2,1)S(1)}, u32[]{:S(2)}, u32[]{:S(2)}) %all-to-all-start) | async-done | bytes 1179680 | tf_op jit(solution)/shard_map/all_to_all | solution.py:119
  85.6 3.1 %collective-permute-start.8 = (f32[48,128]{1,0:T(8,128)S(1)}, f32[48,128]{1,0:T(8,128)S(1)}, u32[]{:S(2)}, u32[]{:S(2)}) collective-permute-start(f32[48,128]{1,0:T(8,128)S(1)} %get-tuple-element.65), channel_id=1, source_target_pairs={{0,1},{1,2},{2,3},{3,0},{4,5},{5,6},{6,7},{7,4},{8,9},{9,10},{10,1... | collective-permute-start | bytes 73736 | tf_op jit(solution)/shard_map/ppermute | solution.py:131
  88.6 4.2 %collective-permute-start.9 = (f32[48,128]{1,0:T(8,128)S(1)}, f32[48,128]{1,0:T(8,128)S(1)}, u32[]{:S(2)}, u32[]{:S(2)}) collective-permute-start(f32[48,128]{1,0:T(8,128)S(1)} %get-tuple-element.64), channel_id=1, source_target_pairs={{0,2},{1,3},{2,0},{3,1},{4,6},{5,7},{6,4},{7,5},{8,10},{9,11},{10,... | collective-permute-start | bytes 73736 | tf_op jit(solution)/shard_map/ppermute | solution.py:131
  92.8 2.4 %collective-permute-start.10 = (f32[48,128]{1,0:T(8,128)S(1)}, f32[48,128]{1,0:T(8,128)S(1)}, u32[]{:S(2)}, u32[]{:S(2)}) collective-permute-start(f32[48,128]{1,0:T(8,128)S(1)} %get-tuple-element.63), channel_id=1, source_target_pairs={{0,3},{1,0},{2,1},{3,2},{4,7},{5,4},{6,5},{7,6},{8,11},{9,8},{10,9... | collective-permute-start | bytes 73736 | tf_op jit(solution)/shard_map/ppermute | solution.py:131
  95.3 1.4 %collective-permute-done.10 = f32[48,128]{1,0:T(8,128)S(1)} collective-permute-done((f32[48,128]{1,0:T(8,128)S(1)}, f32[48,128]{1,0:T(8,128)S(1)}, u32[]{:S(2)}, u32[]{:S(2)}) %collective-permute-start.10) | collective-permute-done | bytes 24608 | tf_op jit(solution)/shard_map/ppermute | solution.py:131
  96.7 13.7 %all_to_all.10 = f32[32,16,128]{2,1,0:T(8,128)S(1)} all-to-all(f32[32,16,128]{2,1,0:T(8,128)S(1)} %broadcast_in_dim.89), channel_id=1, replica_groups=mesh['y'=4,'zlo'=2,'x'=4,'core'=2,'zhi'=4] {'y','zlo','x'}, dimensions={0} | all-to-all | bytes 524288 | tf_op jit(solution)/shard_map/all_to_all | solution.py:138
  110.5 4.1 %collective-permute-start.11 = (f32[32,16,128]{2,1,0:T(8,128)S(1)}, f32[32,16,128]{2,1,0:T(8,128)S(1)}, u32[]{:S(2)}, u32[]{:S(2)}) collective-permute-start(f32[32,16,128]{2,1,0:T(8,128)S(1)} %all_to_all.10), channel_id=1, source_target_pairs={{0,4},{4,0},{1,5},{5,1},{2,6},{6,2},{3,7},{7,3},{8,12},{12,8},{9,1... | collective-permute-start | bytes 786440 | tf_op jit(solution)/shard_map/ppermute | solution.py:139
  (88 shorter events, 18.9 us)
Async XLA Ops:
  0.6 1.6 %copy-start = (bf16[1,4,256,1024]{3,2,1,0:T(8,128)(2,1)S(1)}, bf16[1,4,256,1024]{3,2,1,0:T(8,128)(2,1)}, u32[]{:S(2)}) copy-start(bf16[1,4,256,1024]{3,2,1,0:T(8,128)(2,1)} %param.10) | copy-start | bytes 6291460
  2.2 8.0 %copy-start.5 = (bf16[1024,100]{0,1:T(8,128)(2,1)S(1)}, bf16[1024,100]{0,1:T(8,128)(2,1)}, u32[]{:S(2)}) copy-start(bf16[1024,100]{0,1:T(8,128)(2,1)} %param.13) | copy-start | bytes 614404
  2.2 8.0 %copy-start.8 = (f32[100]{0:T(128)S(1)}, f32[100]{0:T(128)}, u32[]{:S(2)}) copy-start(f32[100]{0:T(128)} %param.14) | copy-start | bytes 1204
  8.8 1.3 %copy-start.1 = (bf16[1024,1024]{1,0:T(8,128)(2,1)}, bf16[1024,1024]{1,0:T(8,128)(2,1)S(1)}, u32[]{:S(2)}) copy-start(bf16[1024,1024]{1,0:T(8,128)(2,1)S(1)} %get-tuple-element.68) | copy-start | bytes 6291460
  11.0 10.3 %copy-start.7 = (f32[1,100,64]{1,2,0:T(8,128)S(1)}, f32[1,100,64]{1,2,0:T(8,128)}, u32[]{:S(2)}) copy-start(f32[1,100,64]{1,2,0:T(8,128)} %param.15) | copy-start | bytes 76804
  11.2 9.9 %collective-permute-start.4 = (bf16[4,100,64]{1,2,0:T(8,128)(2,1)S(1)}, bf16[4,100,64]{1,2,0:T(8,128)(2,1)S(1)}, u32[]{:S(2)}, u32[]{:S(2)}) collective-permute-start(bf16[4,100,64]{1,2,0:T(8,128)(2,1)S(1)} %get-tuple-element.56), channel_id=1, source_target_pairs={{0,64},{64,128},{128,192},{192,0},{1,65},{65,129},{129,193},{193,1... | collective-permute-start | bytes 153608 | tf_op jit(solution)/shard_map/ppermute | solution.py:26
  13.4 7.7 %collective-permute-start.5 = (bf16[4,100,64]{1,2,0:T(8,128)(2,1)S(1)}, bf16[4,100,64]{1,2,0:T(8,128)(2,1)S(1)}, u32[]{:S(2)}, u32[]{:S(2)}) collective-permute-start(bf16[4,100,64]{1,2,0:T(8,128)(2,1)S(1)} %get-tuple-element.55), channel_id=1, source_target_pairs={{0,128},{64,192},{128,0},{192,64},{1,129},{65,193},{129,1},{193,65... | collective-permute-start | bytes 153608 | tf_op jit(solution)/shard_map/ppermute | solution.py:26
  16.1 5.1 %collective-permute-start.6 = (bf16[4,100,64]{1,2,0:T(8,128)(2,1)S(1)}, bf16[4,100,64]{1,2,0:T(8,128)(2,1)S(1)}, u32[]{:S(2)}, u32[]{:S(2)}) collective-permute-start(bf16[4,100,64]{1,2,0:T(8,128)(2,1)S(1)} %get-tuple-element.54), channel_id=1, source_target_pairs={{0,192},{64,0},{128,64},{192,128},{1,193},{65,1},{129,65},{193,129... | collective-permute-start | bytes 153608 | tf_op jit(solution)/shard_map/ppermute | solution.py:26
  17.1 6.8 %copy-start.4 = (s32[1,16,100,64]{2,3,1,0:T(8,128)S(1)}, s32[1,16,100,64]{2,3,1,0:T(8,128)}, u32[]{:S(2)}) copy-start(s32[1,16,100,64]{2,3,1,0:T(8,128)} %param.18) | copy-start | bytes 1228804
  17.1 6.8 %copy-start.6 = (s32[1,100,64]{1,2,0:T(8,128)S(1)}, s32[1,100,64]{1,2,0:T(8,128)}, u32[]{:S(2)}) copy-start(s32[1,100,64]{1,2,0:T(8,128)} %param.19) | copy-start | bytes 76804
  21.1 12.9 %copy-start.9 = (f32[1024]{0:T(1024)S(1)}, f32[1024]{0:T(1024)}, u32[]{:S(2)}) copy-start(f32[1024]{0:T(1024)} %param.12) | copy-start | bytes 12292
  24.1 4.4 %collective-permute-start = (bf16[4,100,64]{1,2,0:T(8,128)(2,1)S(1)}, bf16[4,100,64]{1,2,0:T(8,128)(2,1)S(1)}, u32[]{:S(2)}, u32[]{:S(2)}) collective-permute-start(bf16[4,100,64]{1,2,0:T(8,128)(2,1)S(1)} %dynamic-slice_bitcast_fusion.6), channel_id=1, source_target_pairs={{0,64},{64,128},{128,192},{192,0},{1,65},{65,129},{129,193},{193,1... | collective-permute-start | bytes 153608 | tf_op jit(solution)/shard_map/ppermute | solution.py:26
  28.5 4.7 %collective-permute-start.1 = (bf16[4,100,64]{1,2,0:T(8,128)(2,1)S(1)}, bf16[4,100,64]{1,2,0:T(8,128)(2,1)S(1)}, u32[]{:S(2)}, u32[]{:S(2)}) collective-permute-start(bf16[4,100,64]{1,2,0:T(8,128)(2,1)S(1)} %get-tuple-element.58), channel_id=1, source_target_pairs={{0,128},{64,192},{128,0},{192,64},{1,129},{65,193},{129,1},{193,65... | collective-permute-start | bytes 153608 | tf_op jit(solution)/shard_map/ppermute | solution.py:26
  30.6 3.5 %collective-permute-start.2 = (bf16[4,100,64]{1,2,0:T(8,128)(2,1)S(1)}, bf16[4,100,64]{1,2,0:T(8,128)(2,1)S(1)}, u32[]{:S(2)}, u32[]{:S(2)}) collective-permute-start(bf16[4,100,64]{1,2,0:T(8,128)(2,1)S(1)} %get-tuple-element.57), channel_id=1, source_target_pairs={{0,192},{64,0},{128,64},{192,128},{1,193},{65,1},{129,65},{193,129... | collective-permute-start | bytes 153608 | tf_op jit(solution)/shard_map/ppermute | solution.py:26
  39.0 9.9 %copy-start.3 = (bf16[4,256,1024]{1,2,0:T(8,128)(2,1)S(1)}, bf16[4,256,1024]{1,2,0:T(8,128)(2,1)}, u32[]{:S(2)}) copy-start(bf16[4,256,1024]{1,2,0:T(8,128)(2,1)} %copy.37) | copy-start | bytes 6291460
  41.5 1.9 %copy-start.2 = (f32[1024,1024]{0,1:T(8,128)}, f32[1024,1024]{0,1:T(8,128)S(1)}, u32[]{:S(2)}) copy-start(f32[1024,1024]{0,1:T(8,128)S(1)} %fusion.67) | copy-start | bytes 12582916
  44.6 10.7 %collective-permute-start.3 = (bf16[32,16,1024]{2,1,0:T(8,128)(2,1)}, bf16[32,16,1024]{2,1,0:T(8,128)(2,1)}, u32[]{:S(2)}, u32[]{:S(2)}) collective-permute-start(bf16[32,16,1024]{2,1,0:T(8,128)(2,1)} %fusion.12), channel_id=1, source_target_pairs={{0,4},{4,0},{1,5},{5,1},{2,6},{6,2},{3,7},{7,3},{8,12},{12,8},{9,1... | collective-permute-start | bytes 3145736 | tf_op jit(solution)/shard_map/ppermute | solution.py:112
  53.5 1.6 %collective-permute-start.7 = (f32[32,16,103]{2,1,0:T(8,128)S(1)}, f32[32,16,103]{2,1,0:T(8,128)S(1)}, u32[]{:S(2)}, u32[]{:S(2)}) collective-permute-start(f32[32,16,103]{2,1,0:T(8,128)S(1)} %dynamic-slice_bitcast_fusion), channel_id=1, source_target_pairs={{0,4},{4,0},{1,5},{5,1},{2,6},{6,2},{3,7},{7,3},{8,12},{12,8},{9,1... | collective-permute-start | bytes 632840 | tf_op jit(solution)/shard_map/ppermute | solution.py:113
  59.7 25.3 %all-to-all-start = ((bf16[32,16,1152]{2,1,0:T(8,128)(2,1)}), bf16[32,16,1152]{2,1,0:T(8,128)(2,1)S(1)}, u32[]{:S(2)}, u32[]{:S(2)}) async-start(bf16[32,16,1152]{2,1,0:T(8,128)(2,1)} %concatenate.30), calls=%async_computation | async-start | bytes 2359296 | tf_op jit(solution)/shard_map/all_to_all | solution.py:119
  85.6 9.7 %collective-permute-start.8 = (f32[48,128]{1,0:T(8,128)S(1)}, f32[48,128]{1,0:T(8,128)S(1)}, u32[]{:S(2)}, u32[]{:S(2)}) collective-permute-start(f32[48,128]{1,0:T(8,128)S(1)} %get-tuple-element.65), channel_id=1, source_target_pairs={{0,1},{1,2},{2,3},{3,0},{4,5},{5,6},{6,7},{7,4},{8,9},{9,10},{10,1... | collective-permute-start | bytes 73736 | tf_op jit(solution)/shard_map/ppermute | solution.py:131
  88.6 6.6 %collective-permute-start.9 = (f32[48,128]{1,0:T(8,128)S(1)}, f32[48,128]{1,0:T(8,128)S(1)}, u32[]{:S(2)}, u32[]{:S(2)}) collective-permute-start(f32[48,128]{1,0:T(8,128)S(1)} %get-tuple-element.64), channel_id=1, source_target_pairs={{0,2},{1,3},{2,0},{3,1},{4,6},{5,7},{6,4},{7,5},{8,10},{9,11},{10,... | collective-permute-start | bytes 73736 | tf_op jit(solution)/shard_map/ppermute | solution.py:131
  92.8 3.9 %collective-permute-start.10 = (f32[48,128]{1,0:T(8,128)S(1)}, f32[48,128]{1,0:T(8,128)S(1)}, u32[]{:S(2)}, u32[]{:S(2)}) collective-permute-start(f32[48,128]{1,0:T(8,128)S(1)} %get-tuple-element.63), channel_id=1, source_target_pairs={{0,3},{1,0},{2,1},{3,2},{4,7},{5,4},{6,5},{7,6},{8,11},{9,8},{10,9... | collective-permute-start | bytes 73736 | tf_op jit(solution)/shard_map/ppermute | solution.py:131
  110.5 5.2 %collective-permute-start.11 = (f32[32,16,128]{2,1,0:T(8,128)S(1)}, f32[32,16,128]{2,1,0:T(8,128)S(1)}, u32[]{:S(2)}, u32[]{:S(2)}) collective-permute-start(f32[32,16,128]{2,1,0:T(8,128)S(1)} %all_to_all.10), channel_id=1, source_target_pairs={{0,4},{4,0},{1,5},{5,1},{2,6},{6,2},{3,7},{7,3},{8,12},{12,8},{9,1... | collective-permute-start | bytes 786440 | tf_op jit(solution)/shard_map/ppermute | solution.py:139

commit v2 on v0

v2 whole, which is shorter than its diff:
```python
import math

import jax
import jax.numpy as jnp
from jax import lax
from jax.experimental import pallas as pl
from jax.experimental.pallas import tpu as pltpu
from jax.sharding import Mesh
from jax.sharding import PartitionSpec as P

ALPHA = 0.95
NAMES = ("y", "zlo", "x", "core", "zhi")
PLANE = ("y", "zlo", "x")
GRID = ("zlo", "x", "core")
F32 = jnp.float32
BF16 = jnp.bfloat16
GELU_C = math.sqrt(2.0 / math.pi)
GELU_A = 0.044715
LARGE = pltpu.CompilerParams(vmem_limit_bytes=60 * 1024 * 1024)
SMALL = pltpu.CompilerParams(vmem_limit_bytes=24 * 1024 * 1024)
SMEM = pl.BlockSpec(memory_space=pltpu.SMEM)

PER_BLOCK = 13
ROW_BIN, ROW_BOUT, ROW_LOSS = 121, 122, 15


def shift(axis, step):
    size = lax.axis_size(axis)
    return [(i, (i + step) % size) for i in range(size)]


def const_spec(shape):
    return pl.BlockSpec(shape, lambda *_: (0,) * len(shape))


def fold(block):
    row = lax.broadcasted_iota(jnp.int32, block.shape, 0)
    up = pltpu.roll(block, 12, 0)
    low = (row == 13) | (row == 14)
    return jnp.where((row == 9) | (row == 10), block + up, jnp.where(low, 0.0, block))


def unfold(block):
    row = lax.broadcasted_iota(jnp.int32, block.shape, 0)
    low = block - block.astype(BF16).astype(F32)
    return jnp.where((row == 13) | (row == 14), pltpu.roll(low, 4, 0), block)


def cotangent_kernel(
    ids, rank_ref, obs_ref, area_ref, vw_ref, weight_ref, bout_ref, send0, send1, send2, send3, every
):
    n_mem, sub, n_vars = rank_ref.shape
    mem_dev = n_mem // 4
    epsil = (1.0 - ALPHA) / n_mem
    row = lax.broadcasted_iota(jnp.int32, (sub, sub), 0)
    lane = lax.broadcasted_iota(jnp.int32, (sub, sub), 1)
    area = jnp.sum(jnp.where(row == lane, area_ref[...], 0.0), axis=1, keepdims=True)
    weight = area * vw_ref[...]
    weight_ref[...] = weight
    obs = obs_ref[...]
    total = jnp.zeros_like(weight)
    for member in range(n_mem):
        rank = rank_ref[member]
        sign = jnp.where(rank >= obs, 1.0, -1.0)
        centred = (2 * rank - n_mem + 1).astype(F32)
        cot = (weight * (sign - (1.0 - epsil) / (n_mem - 1) * centred)).astype(BF16)
        every[member // mem_dev, member % mem_dev] = cot
        total = total + cot.astype(F32)
    bout_ref[...] = jnp.sum(total, axis=0, keepdims=True)
    y = ids[0]
    for k, out in enumerate((send0, send1, send2, send3)):
        out[...] = every[lax.rem(y + k, 4)]


def forward_kernel(
    ids, x_ref, w_in_ref, b_in_ref, w_out_ref, b_out_ref,
    hidden_ref, slope_ref, send0, send1, send2, send3, every,
):
    step = pl.program_id(0)
    n_vars, hid = w_out_ref.shape
    sub = x_ref.shape[0] // 4
    x = x_ref[...]
    values = b_out_ref[...]
    for start in range(0, hid, 512):
        cols = slice(start, start + 512)
        pre = jnp.dot(x, w_in_ref[:, cols], preferred_element_type=F32) + b_in_ref[:, cols]
        square = pre * pre
        t = jnp.tanh(pre * (GELU_C + (GELU_C * GELU_A) * square))
        half = 0.5 + 0.5 * t
        hidden = (pre * half).astype(BF16)
        hidden_ref[:, cols] = hidden
        slope_ref[:, cols] = half + pre * (0.5 - 0.5 * (t * t)) * (
            GELU_C + (3.0 * GELU_A * GELU_C) * square
        )
        values = values + lax.dot_general(
            hidden, w_out_ref[:, cols], (((1,), (1,)), ((), ())), preferred_element_type=F32
        )
    values = values.astype(BF16).reshape(4, sub, n_vars)
    for dest in range(4):
        every[dest, step] = values[dest]

    @pl.when(step == 3)
    def _():
        y = ids[0]
        for k, out in enumerate((send0, send1, send2, send3)):
            out[...] = every[lax.rem(y + k, 4)]


def loss_kernel(got0, got1, got2, got3, target_ref, weight_ref, loss_ref):
    gots = (got0, got1, got2, got3)
    mem_dev = got0.shape[0]
    n_mem = 4 * mem_dev
    epsil = (1.0 - ALPHA) / n_mem
    ens = [got[m].astype(F32) for got in gots for m in range(mem_dev)]
    truth = target_ref[...]
    skill = jnp.zeros_like(truth)
    spread = jnp.zeros_like(truth)
    for j in range(n_mem):
        skill = skill + jnp.abs(ens[j] - truth)
        for k in range(j):
            spread = spread + jnp.abs(ens[j] - ens[k])
    cell = weight_ref[...] * (skill / n_mem - (1.0 - epsil) / (n_mem * (n_mem - 1)) * spread)
    loss_ref[...] = jnp.zeros((8, 128), F32) + jnp.sum(cell)


def backward_kernel(
    ids, got0, got1, got2, got3, x_ref, hidden_ref, slope_ref, w_out_ref, bout_ref,
    keep_ref, send_ref, keep_small, send_small, back, back_wide, small,
):
    step = pl.program_id(0)
    last = pl.num_programs(0) - 1
    mem_dev, sub, n_vars = got0.shape
    core = ids[2]
    cols = hidden_ref.shape[1]

    @pl.when(step == 0)
    def _():
        y = ids[0]
        for k, got in enumerate((got0, got1, got2, got3)):
            source = lax.rem(y + 4 - k, 4)
            for m in range(mem_dev):
                start = pl.multiple_of(m * 4 * sub + source * sub, sub)
                back[pl.ds(start, sub), :] = got[m]
        var = lax.broadcasted_iota(jnp.int32, (n_vars, 128), 0)
        lane = lax.broadcasted_iota(jnp.int32, (n_vars, 128), 1)
        place = jnp.where(lane == var + 3 * (var // PER_BLOCK), 1.0, 0.0).astype(BF16)
        back_wide[...] = jnp.dot(back[...], place, preferred_element_type=F32).astype(BF16)

    col = pl.multiple_of(step * cols, cols)
    upward = jnp.dot(back[...], w_out_ref[...], preferred_element_type=F32)
    dhidden = (upward * slope_ref[...]).astype(BF16)
    small[:, pl.ds(col, cols)] = lax.dot_general(
        back_wide[...], hidden_ref[...], (((0,), (0,)), ((), ())), preferred_element_type=F32
    )
    small[ROW_BIN : ROW_BIN + 1, pl.ds(col, cols)] = jnp.sum(
        dhidden.astype(F32), axis=0, keepdims=True
    )
    grad = lax.dot_general(
        x_ref[...], dhidden, (((0,), (0,)), ((), ())), preferred_element_type=F32
    )
    grad = grad.reshape(32, 2, 16, cols)
    first, second = grad[:, 0], grad[:, 1]
    keep_ref[...] = jnp.where(core == 0, first, second)
    send_ref[...] = jnp.where(core == 0, second, first).astype(BF16)

    @pl.when(step == last)
    def _():
        small[ROW_BOUT : ROW_BOUT + 1, 0:n_vars] = bout_ref[...]
        for part in range(4):
            start = pl.multiple_of((2 * part + core) * 16, 16)
            rows = small[pl.ds(start, 16), :]
            for j in range(8):
                keep_small[part * 8 + j] = rows[:, j * 128 : (j + 1) * 128]
            start = pl.multiple_of((2 * part + 1 - core) * 16, 16)
            rows = unfold(small[pl.ds(start, 16), :]).astype(BF16)
            for j in range(8):
                send_small[part * 8 + j] = rows[:, j * 128 : (j + 1) * 128]


def payload_kernel(keep_ref, got_ref, keep_small, got_small, out_ref):
    hid = keep_ref.shape[2]
    out_ref[:, :, 0:hid] = (keep_ref[...] + got_ref[...].astype(F32)).astype(BF16)
    for j in range(keep_small.shape[0]):
        block = unfold(keep_small[j] + fold(got_small[j].astype(F32)))
        out_ref[j, :, hid:] = block.astype(BF16)


def plane_kernel(ids, landed_ref, own_ref, small_ref, part1, part2, part3):
    hid = own_ref.shape[1]
    total = jnp.sum(landed_ref[...].astype(F32), axis=0)
    small = fold(total[:, hid:])
    small_ref[...] = small
    zhi = ids[1]
    quarters = [total[4 * z : 4 * z + 4, 0:hid] for z in range(4)]

    def quarter(which):
        out = quarters[3]
        for z in range(3):
            out = jnp.where(which == z, quarters[z], out)
        return out

    own_ref[...] = quarter(zhi)
    for k, out in ((1, part1), (2, part2), (3, part3)):
        rows = quarter(lax.rem(zhi + k, 4))
        for j in range(4):
            out[4 * j : 4 * j + 4, 0:256] = rows[:, j * 256 : (j + 1) * 256]
        out[:, 256:384] = small


def total_kernel(scale, ids, own_ref, small_ref, got1, got2, got3, loss_ref, grad_ref, copies_ref):
    zhi = ids[1]
    for j in range(4):
        acc = own_ref[:, j * 256 : (j + 1) * 256]
        for got in (got1, got2, got3):
            acc = acc + got[4 * j : 4 * j + 4, 0:256]
        grad_ref[:, j * 256 : (j + 1) * 256] = acc * scale
    parts = [small_ref[...]] + [got[:, 256:384] for got in (got1, got2, got3)]
    acc = None
    for source in range(4):
        term = parts[0]
        for k in range(1, 4):
            term = jnp.where(lax.rem(zhi + 4 - k, 4) == source, parts[k], term)
        acc = term if acc is None else acc + term
    row = lax.broadcasted_iota(jnp.int32, acc.shape, 0)
    acc = jnp.where(row == ROW_LOSS, loss_ref[0:1, :], acc)
    copies_ref[...] = jnp.broadcast_to(acc[None], copies_ref.shape)


def final_kernel(scale, loss_scale, ids, mine, theirs, out_ref, bin_ref, bout_ref, loss_ref, full):
    core = ids[2]
    n_vars = out_ref.shape[0]
    for which, blocks in ((core, mine), (1 - core, theirs)):
        for part in range(4):
            start = pl.multiple_of((2 * part + which) * 16, 16)
            for j in range(8):
                full[pl.ds(start, 16), j * 128 : (j + 1) * 128] = blocks[part * 8 + j]
    for q in range(8):
        count = min(PER_BLOCK, n_vars - PER_BLOCK * q)
        out_ref[PER_BLOCK * q : PER_BLOCK * q + count, :] = full[16 * q : 16 * q + count, :] * scale
    bin_ref[...] = full[ROW_BIN : ROW_BIN + 1, :] * scale
    bout_ref[...] = full[ROW_BOUT : ROW_BOUT + 1, 0:n_vars] * scale
    total = jnp.zeros((1, 128), F32)
    for q in range(8):
        for j in range(8):
            total = total + full[16 * q + ROW_LOSS : 16 * q + ROW_LOSS + 1, 128 * j : 128 * (j + 1)]
    loss_ref[...] = total[:, 0:1] * loss_scale


def per_device(latents, w_in, b_in, w_out, b_out, targets, area, var_weight, member_rank, obs_rank):
    mem_dev = latents.shape[1]
    pts_dev = latents.shape[2]
    width = latents.shape[3]
    hid = w_in.shape[1]
    n_vars = w_out.shape[1]
    n_y = lax.axis_size("y")
    n_mem = mem_dev * n_y
    sub = pts_dev // n_y
    rows = mem_dev * pts_dev
    n_points = pts_dev * lax.axis_size(GRID)
    scale = 1.0 / math.sqrt(lax.axis_size("zhi") * n_mem * n_points)
    ids = jnp.stack(
        [lax.axis_index("y"), lax.axis_index("zhi"), lax.axis_index("core")]
    ).astype(jnp.int32)
    shape = jax.ShapeDtypeStruct

    x = latents.reshape(rows, width)
    w_out_t = w_out.T
    ranks = member_rank[0].transpose(0, 2, 1)
    obs = obs_rank[0].T
    truth = targets[0].T
    sent = shape((mem_dev, sub, n_vars), BF16)
    whole = pl.BlockSpec(memory_space=pltpu.VMEM)

    weight, bout, cot0, cot1, cot2, cot3 = pl.pallas_call(
        cotangent_kernel,
        in_specs=[SMEM] + [whole] * 4,
        out_shape=[shape((sub, n_vars), F32), shape((1, n_vars), F32)] + [sent] * 4,
        scratch_shapes=[pltpu.VMEM((n_y, mem_dev, sub, n_vars), BF16)],
        compiler_params=SMALL,
        name="cotangent",
    )(ids, ranks, obs, area[None, :], var_weight[None, :])
    ids_later, cot1, cot2, cot3 = lax.optimization_barrier((ids, cot1, cot2, cot3))
    cot1 = lax.ppermute(cot1, "y", shift("y", 1))
    cot2 = lax.ppermute(cot2, "y", shift("y", 2))
    cot3 = lax.ppermute(cot3, "y", shift("y", 3))

    hidden, slope, val0, val1, val2, val3 = pl.pallas_call(
        forward_kernel,
        grid=(mem_dev,),
        in_specs=[
            SMEM,
            pl.BlockSpec((pts_dev, width), lambda i: (i, 0)),
            const_spec((width, hid)),
            const_spec((1, hid)),
            const_spec((n_vars, hid)),
            const_spec((1, n_vars)),
        ],
        out_specs=[
            pl.BlockSpec((pts_dev, hid), lambda i: (i, 0)),
            pl.BlockSpec((pts_dev, hid), lambda i: (i, 0)),
        ]
        + [const_spec(sent.shape)] * 4,
        out_shape=[shape((rows, hid), BF16), shape((rows, hid), F32)] + [sent] * 4,
        scratch_shapes=[pltpu.VMEM((n_y, mem_dev, sub, n_vars), BF16)],
        compiler_params=LARGE,
        name="forward",
    )(ids_later, x, w_in, b_in[None, :], w_out_t, b_out[None, :])

    cols = 512
    n_plane = lax.axis_size(PLANE)
    block = width // (2 * n_plane)
    keep, send, keep_small, send_small = pl.pallas_call(
        backward_kernel,
        grid=(hid // cols,),
        in_specs=[SMEM]
        + [const_spec(sent.shape)] * 4
        + [
            const_spec((rows, width)),
            pl.BlockSpec((rows, cols), lambda i: (0, i)),
            pl.BlockSpec((rows, cols), lambda i: (0, i)),
            pl.BlockSpec((n_vars, cols), lambda i: (0, i)),
            const_spec((1, n_vars)),
        ],
        out_specs=[
            pl.BlockSpec((n_plane, block, cols), lambda i: (0, 0, i)),
            pl.BlockSpec((n_plane, block, cols), lambda i: (0, 0, i)),
            const_spec((n_plane, block, 128)),
            const_spec((n_plane, block, 128)),
        ],
        out_shape=[
            shape((n_plane, block, hid), F32),
            shape((n_plane, block, hid), BF16),
            shape((n_plane, block, 128), F32),
            shape((n_plane, block, 128), BF16),
        ],
        scratch_shapes=[
            pltpu.VMEM((rows, n_vars), BF16),
            pltpu.VMEM((rows, 128), BF16),
            pltpu.VMEM((128, hid), F32),
        ],
        compiler_params=LARGE,
        name="backward",
    )(ids, cot0, cot1, cot2, cot3, x, hidden, slope, w_out_t, bout)

    swap = [(0, 1), (1, 0)]
    got = lax.ppermute(send, "core", swap)
    got_small = lax.ppermute(send_small, "core", swap)
    payload = pl.pallas_call(
        payload_kernel,
        out_shape=shape((n_plane, block, hid + 128), BF16),
        compiler_params=SMALL,
        name="payload",
    )(keep, got, keep_small, got_small)
    payload, val1, val2, val3 = lax.optimization_barrier((payload, val1, val2, val3))
    landed = lax.all_to_all(payload, PLANE, 0, 0, tiled=True)
    val1 = lax.ppermute(val1, "y", shift("y", 1))
    val2 = lax.ppermute(val2, "y", shift("y", 2))
    val3 = lax.ppermute(val3, "y", shift("y", 3))
    part_loss = pl.pallas_call(
        loss_kernel, out_shape=shape((8, 128), F32), compiler_params=SMALL, name="loss"
    )(val0, val1, val2, val3, truth, weight)

    part = shape((block, 384), F32)
    own, small, part1, part2, part3 = pl.pallas_call(
        plane_kernel,
        in_specs=[SMEM, whole],
        out_shape=[shape((block // 4, hid), F32), shape((block, 128), F32), part, part, part],
        compiler_params=SMALL,
        name="plane_sum",
    )(ids, landed)
    part1 = lax.ppermute(part1, "zhi", shift("zhi", 1))
    part2 = lax.ppermute(part2, "zhi", shift("zhi", 2))
    part3 = lax.ppermute(part3, "zhi", shift("zhi", 3))
    grad_in, copies = pl.pallas_call(
        lambda *refs: total_kernel(scale, *refs),
        in_specs=[SMEM] + [whole] * 6,
        out_shape=[shape((block // 4, hid), F32), shape((n_plane, block, 128), F32)],
        compiler_params=SMALL,
        name="total",
    )(ids, own, small, part1, part2, part3, part_loss)

    mine = lax.all_to_all(copies, PLANE, 0, 0, tiled=True)
    theirs = lax.ppermute(mine, "core", swap)
    grad_out, grad_bin, grad_bout, loss = pl.pallas_call(
        lambda *refs: final_kernel(scale, 1.0 / (n_points * n_vars), *refs),
        in_specs=[SMEM] + [whole] * 2,
        out_shape=[
            shape((n_vars, hid), F32),
            shape((1, hid), F32),
            shape((1, n_vars), F32),
            shape((1, 1), F32),
        ],
        scratch_shapes=[pltpu.VMEM((128, hid), F32)],
        compiler_params=SMALL,
        name="unpack",
    )(ids, mine, theirs)
    return (loss.reshape(1), grad_in, grad_out.T, grad_bin.reshape(hid), grad_bout.reshape(n_vars))


def solution(mesh):
    split = Mesh(mesh.devices.reshape(4, 2, 4, 2, 4), NAMES)
    points = GRID + ("y",)
    in_specs = (
        P("zhi", "y", GRID, None),
        P(),
        P(),
        P(),
        P(),
        P("zhi", None, points),
        P(points),
        P(),
        P("zhi", None, None, points),
        P("zhi", None, points),
    )
    out_specs = (P("zhi"), P(NAMES, None), P(), P(), P())
    return jax.shard_map(
        per_device, mesh=split, in_specs=in_specs, out_specs=out_specs, check_vma=False
    )
```

time: 334 us -> 94.8 us (0.28)
  blocking collectives: 237 us -> 13.8 us
  waiting for transfers between devices: 54.2 us -> 16.9 us
  starting transfers between devices: 0.04 us -> 32.1 us
  Pallas kernels: 0 us -> 23.2 us
  matrix products: 16.4 us -> 0 us
  between operations: 16 us -> 0.81 us
    psum x2 -> x0, blocking collectives: 218 us -> none  [the longest x1 142 us: per_device(): total = lax.psum(local_loss, ('member', 'grid'))]
    unnamed x2 -> x0, waiting for transfers between devices: 54.2 us -> none
    ppermute x0 -> x12, starting transfers between devices: none -> 26.1 us  [the longest x1 4.22 us: per_device(): part2 = lax.ppermute(part2, 'zhi', shift('zhi', 2))]
    pallas_call x0 -> x8, Pallas kernels: none -> 23.2 us  [the longest x1 8.89 us: per_device(): pl.pallas_call(forward_kernel, grid=(mem_dev,), in_specs=[SMEM, pl.BlockS...]
    dot_general x5 -> x0, matrix products: 16.4 us -> none  [the longest x1 6.61 us: per_device(): pre = jnp.dot(rows_x, w_in, preferred_element_type=jnp.float32) + b_in]
    all_to_all x0 -> x1, waiting for transfers between devices: none -> 12.3 us  [per_device(): landed = lax.all_to_all(payload, PLANE, 0, 0, tiled=True)]
    all_to_all x0 -> x1, starting transfers between devices: none -> 6.02 us  [per_device(): landed = lax.all_to_all(payload, PLANE, 0, 0, tiled=True)]
    all_to_all x2 -> x1, blocking collectives: 18.4 us -> 13.8 us  [per_device(): mine = lax.all_to_all(copies, PLANE, 0, 0, tiled=True)]
  transfers between devices with their start and end apart: 1 -> 13, of which waited for: 1 -> 4; matrix products, arithmetic and copies ran while one was open for 0% -> 0% of each run, Pallas kernels for 0% -> 11%
where the time goes in v2:
time: 94.8 us; the launch traced here: 94.3 us
  starting transfers between devices  32.1 us (34%)
  Pallas kernels  23.2 us (24%)
  waiting for transfers between devices  16.9 us (18%)
  blocking collectives  13.8 us (15%)
  local copies, waits for them, and re-layouts  7.45 us (8%)
    all_to_all x1, blocking collectives, per_device(): mine = lax.all_to_all(copies, PLANE, 0, 0, tiled=True)  13.8 us
    all_to_all x1, waiting for transfers between devices, per_device(): landed = lax.all_to_all(payload, PLANE, 0, 0, tiled=True)  12.3 us
    pallas_call x1, Pallas kernels, per_device(): pl.pallas_call(forward_kernel, grid=(mem_dev,), in_specs=[SMEM, pl.BlockS...  8.89 us
    pallas_call x1, Pallas kernels, per_device(): pl.pallas_call(backward_kernel, grid=(hid // cols,), in_specs=[SMEM] + [c...  8.24 us
    unnamed x36, local copies, waits for them, and re-layouts  7.45 us
    all_to_all x1, starting transfers between devices, per_device(): landed = lax.all_to_all(payload, PLANE, 0, 0, tiled=True)  6.02 us
    ppermute x1, starting transfers between devices, per_device(): part2 = lax.ppermute(part2, 'zhi', shift('zhi', 2))  4.22 us
    ppermute x1, starting transfers between devices, per_device(): theirs = lax.ppermute(mine, 'core', swap)  4.06 us
  transfers between devices with their start and end apart: 13, of which 4 were waited for; matrix products, arithmetic and copies ran while one was open for 0% of the time, Pallas kernels for 11%

profile of v2, /device:TPU:1, one launch (start us, length us, event | category | flops | bytes accessed | tf_op | source)
XLA Modules:
  0.0 94.3 jit_solution(7951853440706437729)
XLA Ops:
  0.7 1.0 %copy-done.1 = s32[1,16,100,64]{2,3,1,0:T(8,128)S(1)} copy-done((s32[1,16,100,64]{2,3,1,0:T(8,128)S(1)}, s32[1,16,100,64]{2,3,1,0:T(8,128)}, u32[]{:S(2)}) %copy-start.1) | copy-done | bytes 409624
  5.8 2.1 %collective-permute-start = (bf16[4,64,100]{2,1,0:T(8,128)(2,1)S(1)}, bf16[4,64,100]{2,1,0:T(8,128)(2,1)S(1)}, u32[]{:S(2)}, u32[]{:S(2)}) collective-permute-start(bf16[4,64,100]{2,1,0:T(8,128)(2,1)S(1)} %get-tuple-element.44), channel_id=1, source_target_pairs={{0,64},{64,128},{128,192},{192,0},{1,65},{65,129},{129,193},{193,1... | collective-permute-start | bytes 153608 | tf_op jit(solution)/shard_map/ppermute | solution.py:283
  7.9 2.6 %collective-permute-start.1 = (bf16[4,64,100]{2,1,0:T(8,128)(2,1)S(1)}, bf16[4,64,100]{2,1,0:T(8,128)(2,1)S(1)}, u32[]{:S(2)}, u32[]{:S(2)}) collective-permute-start(bf16[4,64,100]{2,1,0:T(8,128)(2,1)S(1)} %get-tuple-element.45), channel_id=1, source_target_pairs={{0,128},{64,192},{128,0},{192,64},{1,129},{65,193},{129,1},{193,65... | collective-permute-start | bytes 153608 | tf_op jit(solution)/shard_map/ppermute | solution.py:284
  10.5 1.1 %collective-permute-start.2 = (bf16[4,64,100]{2,1,0:T(8,128)(2,1)S(1)}, bf16[4,64,100]{2,1,0:T(8,128)(2,1)S(1)}, u32[]{:S(2)}, u32[]{:S(2)}) collective-permute-start(bf16[4,64,100]{2,1,0:T(8,128)(2,1)S(1)} %get-tuple-element.46), channel_id=1, source_target_pairs={{0,192},{64,0},{128,64},{192,128},{1,193},{65,1},{129,65},{193,129... | collective-permute-start | bytes 153608 | tf_op jit(solution)/shard_map/ppermute | solution.py:285
  11.6 8.9 %forward.1 = (bf16[1024,1024]{1,0:T(8,128)(2,1)}, f32[1024,1024]{1,0:T(8,128)}, bf16[4,64,100]{2,1,0:T(8,128)(2,1)}, bf16[4,64,100]{2,1,0:T(8,128)(2,1)}, bf16[4...) custom-call(s32[3]{0:T(128)} %copy-done.7, bf16[1024,1024]{1,0:T(8,128)(2,1)} %bitcast.27, ...), custom_call_target="tpu_custom_call" | custom-call | tf_op jit(solution)/shard_map/forward/pallas_call | solution.py:287
  21.2 8.2 %backward.1 = (f32[32,16,1024]{2,1,0:T(8,128)}, bf16[32,16,1024]{2,1,0:T(8,128)(2,1)}, f32[32,16,128]{2,1,0:T(8,128)}, bf16[32,16,128]{2,1,0:T(8,128)(2,1)}) custom-call(s32[3]{0:T(128)} %copy-done.7, bf16[4,64,100]{2,1,0:T(8,128)(2,1)} %copy-done.3, bf16[4,64,100]{2,1,0:T(8,128)(2,1)} %copy-done.12, bf16[4,64,100]{2,1,0:T(8,128)(2,1)} %copy-done.13, ...), custom_call_target="tpu_custom_call" | custom-call | tf_op jit(solution)/shard_map/backward/pallas_call | solution.py:312
  29.4 1.6 %collective-permute-start.3 = (bf16[32,16,1024]{2,1,0:T(8,128)(2,1)}, bf16[32,16,1024]{2,1,0:T(8,128)(2,1)S(1)}, u32[]{:S(2)}, u32[]{:S(2)}) collective-permute-start(bf16[32,16,1024]{2,1,0:T(8,128)(2,1)} %get-tuple-element.52), channel_id=1, source_target_pairs={{0,4},{4,0},{1,5},{5,1},{2,6},{6,2},{3,7},{7,3},{8,12},{12,8},{9,1... | collective-permute-start | bytes 3145736 | tf_op jit(solution)/shard_map/ppermute | solution.py:346
  31.1 2.6 %collective-permute-done.4.got_small = bf16[32,16,128]{2,1,0:T(8,128)(2,1)S(1)} collective-permute-done((bf16[32,16,128]{2,1,0:T(8,128)(2,1)}, bf16[32,16,128]{2,1,0:T(8,128)(2,1)S(1)}, u32[]{:S(2)}, u32[]{:S(2)}) %collective-permute-start.4) | collective-permute-done | bytes 131104 | tf_op jit(solution)/shard_map/ppermute | solution.py:347
  33.7 1.6 %copy-done = f32[32,16,1024]{2,1,0:T(8,128)S(1)} copy-done((f32[32,16,1024]{2,1,0:T(8,128)S(1)}, f32[32,16,1024]{2,1,0:T(8,128)}, u32[]{:S(2)}) %copy-start) | copy-done | bytes 2097176
  35.3 0.9 %copy-done.2 = f32[32,16,128]{2,1,0:T(8,128)S(1)} copy-done((f32[32,16,128]{2,1,0:T(8,128)S(1)}, f32[32,16,128]{2,1,0:T(8,128)}, u32[]{:S(2)}) %copy-start.2) | copy-done | bytes 262168
  36.3 1.3 %payload.1 = bf16[32,16,1152]{2,1,0:T(8,128)(2,1)} custom-call(f32[32,16,1024]{2,1,0:T(8,128)S(1)} %copy-done, bf16[32,16,1024]{2,1,0:T(8,128)(2,1)S(1)} %collective-permute-done.3.got_ref, f32[32,16,128]{2,1,0:T(8,128)S(1)} %copy-done.2, bf16[32,16,128]{2,1,0:T(8,128)(2,1)S(1)} %collective-permute-done.4.got_small), custom_call_target="tpu_custom_call" | custom-call | tf_op jit(solution)/shard_map/payload/pallas_call | solution.py:348
  37.6 6.0 %all-to-all-start = ((bf16[32,16,1152]{2,1,0:T(8,128)(2,1)}), bf16[32,16,1152]{2,1,0:T(8,128)(2,1)S(1)}, u32[]{:S(2)}, u32[]{:S(2)}) async-start(bf16[32,16,1152]{2,1,0:T(8,128)(2,1)} %payload.1), calls=%async_computation | async-start | bytes 2359296 | tf_op jit(solution)/shard_map/all_to_all | solution.py:355
  43.6 1.3 %collective-permute-start.8 = (bf16[4,64,100]{2,1,0:T(8,128)(2,1)S(1)}, bf16[4,64,100]{2,1,0:T(8,128)(2,1)S(1)}, u32[]{:S(2)}, u32[]{:S(2)}) collective-permute-start(bf16[4,64,100]{2,1,0:T(8,128)(2,1)S(1)} %copy-done.17), channel_id=1, source_target_pairs={{0,64},{64,128},{128,192},{192,0},{1,65},{65,129},{129,193},{193,1... | collective-permute-start | bytes 153608 | tf_op jit(solution)/shard_map/ppermute | solution.py:356
  45.0 2.4 %collective-permute-start.9 = (bf16[4,64,100]{2,1,0:T(8,128)(2,1)S(1)}, bf16[4,64,100]{2,1,0:T(8,128)(2,1)S(1)}, u32[]{:S(2)}, u32[]{:S(2)}) collective-permute-start(bf16[4,64,100]{2,1,0:T(8,128)(2,1)S(1)} %copy-done.16), channel_id=1, source_target_pairs={{0,128},{64,192},{128,0},{192,64},{1,129},{65,193},{129,1},{193,65... | collective-permute-start | bytes 153608 | tf_op jit(solution)/shard_map/ppermute | solution.py:357
  47.4 1.1 %collective-permute-start.10 = (bf16[4,64,100]{2,1,0:T(8,128)(2,1)S(1)}, bf16[4,64,100]{2,1,0:T(8,128)(2,1)S(1)}, u32[]{:S(2)}, u32[]{:S(2)}) collective-permute-start(bf16[4,64,100]{2,1,0:T(8,128)(2,1)S(1)} %copy-done.15), channel_id=1, source_target_pairs={{0,192},{64,0},{128,64},{192,128},{1,193},{65,1},{129,65},{193,129... | collective-permute-start | bytes 153608 | tf_op jit(solution)/shard_map/ppermute | solution.py:358
  48.5 12.3 %all-to-all-done.landed_ref = bf16[32,16,1152]{2,1,0:T(8,128)(2,1)S(1)} async-done(((bf16[32,16,1152]{2,1,0:T(8,128)(2,1)}), bf16[32,16,1152]{2,1,0:T(8,128)(2,1)S(1)}, u32[]{:S(2)}, u32[]{:S(2)}) %all-to-all-start) | async-done | bytes 1179680 | tf_op jit(solution)/shard_map/all_to_all | solution.py:355
  61.6 3.1 %collective-permute-start.5 = (f32[16,384]{1,0:T(8,128)S(1)}, f32[16,384]{1,0:T(8,128)S(1)}, u32[]{:S(2)}, u32[]{:S(2)}) collective-permute-start(f32[16,384]{1,0:T(8,128)S(1)} %get-tuple-element.61), channel_id=1, source_target_pairs={{0,1},{1,2},{2,3},{3,0},{4,5},{5,6},{6,7},{7,4},{8,9},{9,10},{10,1... | collective-permute-start | bytes 73736 | tf_op jit(solution)/shard_map/ppermute | solution.py:371
  64.6 4.2 %collective-permute-start.6 = (f32[16,384]{1,0:T(8,128)S(1)}, f32[16,384]{1,0:T(8,128)S(1)}, u32[]{:S(2)}, u32[]{:S(2)}) collective-permute-start(f32[16,384]{1,0:T(8,128)S(1)} %get-tuple-element.62), channel_id=1, source_target_pairs={{0,2},{1,3},{2,0},{3,1},{4,6},{5,7},{6,4},{7,5},{8,10},{9,11},{10,... | collective-permute-start | bytes 73736 | tf_op jit(solution)/shard_map/ppermute | solution.py:372
  68.9 2.4 %collective-permute-start.7 = (f32[16,384]{1,0:T(8,128)S(1)}, f32[16,384]{1,0:T(8,128)S(1)}, u32[]{:S(2)}, u32[]{:S(2)}) collective-permute-start(f32[16,384]{1,0:T(8,128)S(1)} %get-tuple-element.63), channel_id=1, source_target_pairs={{0,3},{1,0},{2,1},{3,2},{4,7},{5,4},{6,5},{7,6},{8,11},{9,8},{10,9... | collective-permute-start | bytes 73736 | tf_op jit(solution)/shard_map/ppermute | solution.py:373
  72.7 1.2 %total.1 = (f32[4,1024]{1,0:T(4,128)}, f32[32,16,128]{2,1,0:T(8,128)S(1)}) custom-call(s32[3]{0:T(128)S(1)} %copy-done.8, f32[4,1024]{1,0:T(4,128)S(1)} %get-tuple-element.59.refs_1_, f32[16,128]{1,0:T(8,128)S(1)} %get-tuple-element.60.refs_2_, f32[16,384]{1,0:T(8,128)S(1)} %collective-permute-done.5.refs_3_, f32[16,384]{1,0:T(8,128)S(1)} %collective-permute-done.6.refs_4_, ...), custom_call_target="tpu_custom_call" | custom-call | tf_op jit(solution)/shard_map/total/pallas_call | solution.py:374
  73.9 13.8 %all_to_all.10.refs_1_ = f32[32,16,128]{2,1,0:T(8,128)S(1)} all-to-all(f32[32,16,128]{2,1,0:T(8,128)S(1)} %get-tuple-element.69), channel_id=1, replica_groups=mesh['y'=4,'zlo'=2,'x'=4,'core'=2,'zhi'=4] {'y','zlo','x'}, dimensions={0} | all-to-all | bytes 524288 | tf_op jit(solution)/shard_map/all_to_all | solution.py:382
  87.7 4.1 %collective-permute-start.11 = (f32[32,16,128]{2,1,0:T(8,128)S(1)}, f32[32,16,128]{2,1,0:T(8,128)S(1)}, u32[]{:S(2)}, u32[]{:S(2)}) collective-permute-start(f32[32,16,128]{2,1,0:T(8,128)S(1)} %all_to_all.10.refs_1_), channel_id=1, source_target_pairs={{0,4},{4,0},{1,5},{5,1},{2,6},{6,2},{3,7},{7,3},{8,12},{12,8},{9,1... | collective-permute-start | bytes 786440 | tf_op jit(solution)/shard_map/ppermute | solution.py:383
  91.7 1.2 %collective-permute-done.11.refs_2_ = f32[32,16,128]{2,1,0:T(8,128)S(1)} collective-permute-done((f32[32,16,128]{2,1,0:T(8,128)S(1)}, f32[32,16,128]{2,1,0:T(8,128)S(1)}, u32[]{:S(2)}, u32[]{:S(2)}) %collective-permute-start.11) | collective-permute-done | bytes 262176 | tf_op jit(solution)/shard_map/ppermute | solution.py:383
  92.9 1.4 %unpack.1 = (f32[100,1024]{1,0:T(8,128)}, f32[1,1024]{1,0:T(1,128)}, f32[1,100]{1,0:T(1,128)}, f32[1,1]{1,0:T(1,128)}) custom-call(s32[3]{0:T(128)S(1)} %copy-done.8, f32[32,16,128]{2,1,0:T(8,128)S(1)} %all_to_all.10.refs_1_, f32[32,16,128]{2,1,0:T(8,128)S(1)} %collective-permute-done.11.refs_2_), custom_call_target="tpu_custom_call" | custom-call | tf_op jit(solution)/shard_map/unpack/pallas_call | solution.py:384
  (48 shorter events, 7.1 us)
Async XLA Ops:
  0.7 10.9 %copy-start.7 = (s32[3]{0:T(128)}, s32[3]{0:T(128)S(1)}, u32[]{:S(2)}) copy-start(s32[3]{0:T(128)S(1)} %pad_add_fusion.ids.refs_0_) | copy-start | bytes 40
  0.7 1.0 %copy-start.1 = (s32[1,16,100,64]{2,3,1,0:T(8,128)S(1)}, s32[1,16,100,64]{2,3,1,0:T(8,128)}, u32[]{:S(2)}) copy-start(s32[1,16,100,64]{2,3,1,0:T(8,128)} %param.18) | copy-start | bytes 1228804
  1.8 0.8 copy-start.5
  5.8 14.7 %collective-permute-start = (bf16[4,64,100]{2,1,0:T(8,128)(2,1)S(1)}, bf16[4,64,100]{2,1,0:T(8,128)(2,1)S(1)}, u32[]{:S(2)}, u32[]{:S(2)}) collective-permute-start(bf16[4,64,100]{2,1,0:T(8,128)(2,1)S(1)} %get-tuple-element.44), channel_id=1, source_target_pairs={{0,64},{64,128},{128,192},{192,0},{1,65},{65,129},{129,193},{193,1... | collective-permute-start | bytes 153608 | tf_op jit(solution)/shard_map/ppermute | solution.py:283
  7.9 12.6 %collective-permute-start.1 = (bf16[4,64,100]{2,1,0:T(8,128)(2,1)S(1)}, bf16[4,64,100]{2,1,0:T(8,128)(2,1)S(1)}, u32[]{:S(2)}, u32[]{:S(2)}) collective-permute-start(bf16[4,64,100]{2,1,0:T(8,128)(2,1)S(1)} %get-tuple-element.45), channel_id=1, source_target_pairs={{0,128},{64,192},{128,0},{192,64},{1,129},{65,193},{129,1},{193,65... | collective-permute-start | bytes 153608 | tf_op jit(solution)/shard_map/ppermute | solution.py:284
  10.5 10.0 %collective-permute-start.2 = (bf16[4,64,100]{2,1,0:T(8,128)(2,1)S(1)}, bf16[4,64,100]{2,1,0:T(8,128)(2,1)S(1)}, u32[]{:S(2)}, u32[]{:S(2)}) collective-permute-start(bf16[4,64,100]{2,1,0:T(8,128)(2,1)S(1)} %get-tuple-element.46), channel_id=1, source_target_pairs={{0,192},{64,0},{128,64},{192,128},{1,193},{65,1},{129,65},{193,129... | collective-permute-start | bytes 153608 | tf_op jit(solution)/shard_map/ppermute | solution.py:285
  29.4 4.3 %collective-permute-start.3 = (bf16[32,16,1024]{2,1,0:T(8,128)(2,1)}, bf16[32,16,1024]{2,1,0:T(8,128)(2,1)S(1)}, u32[]{:S(2)}, u32[]{:S(2)}) collective-permute-start(bf16[32,16,1024]{2,1,0:T(8,128)(2,1)} %get-tuple-element.52), channel_id=1, source_target_pairs={{0,4},{4,0},{1,5},{5,1},{2,6},{6,2},{3,7},{7,3},{8,12},{12,8},{9,1... | collective-permute-start | bytes 3145736 | tf_op jit(solution)/shard_map/ppermute | solution.py:346
  31.0 2.7 %collective-permute-start.4 = (bf16[32,16,128]{2,1,0:T(8,128)(2,1)}, bf16[32,16,128]{2,1,0:T(8,128)(2,1)S(1)}, u32[]{:S(2)}, u32[]{:S(2)}) collective-permute-start(bf16[32,16,128]{2,1,0:T(8,128)(2,1)} %get-tuple-element.54), channel_id=1, source_target_pairs={{0,4},{4,0},{1,5},{5,1},{2,6},{6,2},{3,7},{7,3},{8,12},{12,8},{9,1... | collective-permute-start | bytes 393224 | tf_op jit(solution)/shard_map/ppermute | solution.py:347
  33.7 1.6 %copy-start = (f32[32,16,1024]{2,1,0:T(8,128)S(1)}, f32[32,16,1024]{2,1,0:T(8,128)}, u32[]{:S(2)}) copy-start(f32[32,16,1024]{2,1,0:T(8,128)} %get-tuple-element.51.keep_ref) | copy-start | bytes 6291460
  35.3 0.9 %copy-start.2 = (f32[32,16,128]{2,1,0:T(8,128)S(1)}, f32[32,16,128]{2,1,0:T(8,128)}, u32[]{:S(2)}) copy-start(f32[32,16,128]{2,1,0:T(8,128)} %get-tuple-element.53.keep_small) | copy-start | bytes 786436
  37.6 6.1 %copy-start.17 = (bf16[4,64,100]{2,1,0:T(8,128)(2,1)S(1)}, bf16[4,64,100]{2,1,0:T(8,128)(2,1)}, u32[]{:S(2)}) copy-start(bf16[4,64,100]{2,1,0:T(8,128)(2,1)} %get-tuple-element.65) | copy-start | bytes 153604
  37.6 7.4 %copy-start.16 = (bf16[4,64,100]{2,1,0:T(8,128)(2,1)S(1)}, bf16[4,64,100]{2,1,0:T(8,128)(2,1)}, u32[]{:S(2)}) copy-start(bf16[4,64,100]{2,1,0:T(8,128)(2,1)} %get-tuple-element.66) | copy-start | bytes 153604
  37.6 9.8 %copy-start.15 = (bf16[4,64,100]{2,1,0:T(8,128)(2,1)S(1)}, bf16[4,64,100]{2,1,0:T(8,128)(2,1)}, u32[]{:S(2)}) copy-start(bf16[4,64,100]{2,1,0:T(8,128)(2,1)} %get-tuple-element.67) | copy-start | bytes 153604
  37.6 23.2 %copy-start.8 = (s32[3]{0:T(128)S(1)}, s32[3]{0:T(128)}, u32[]{:S(2)}) copy-start(s32[3]{0:T(128)} %copy-done.7) | copy-start | bytes 40
  37.6 33.7 %copy-start.4 = (bf16[4,64,100]{2,1,0:T(8,128)(2,1)S(1)}, bf16[4,64,100]{2,1,0:T(8,128)(2,1)}, u32[]{:S(2)}) copy-start(bf16[4,64,100]{2,1,0:T(8,128)(2,1)} %get-tuple-element.64.got0) | copy-start | bytes 153604
  37.6 33.7 %copy-start.6 = (f32[1,100,64]{1,2,0:T(8,128)S(1)}, f32[1,100,64]{1,2,0:T(8,128)}, u32[]{:S(2)}) copy-start(f32[1,100,64]{1,2,0:T(8,128)} %param.15) | copy-start | bytes 76804
  37.6 23.2 %all-to-all-start = ((bf16[32,16,1152]{2,1,0:T(8,128)(2,1)}), bf16[32,16,1152]{2,1,0:T(8,128)(2,1)S(1)}, u32[]{:S(2)}, u32[]{:S(2)}) async-start(bf16[32,16,1152]{2,1,0:T(8,128)(2,1)} %payload.1), calls=%async_computation | async-start | bytes 2359296 | tf_op jit(solution)/shard_map/all_to_all | solution.py:355
  43.6 25.2 %collective-permute-start.8 = (bf16[4,64,100]{2,1,0:T(8,128)(2,1)S(1)}, bf16[4,64,100]{2,1,0:T(8,128)(2,1)S(1)}, u32[]{:S(2)}, u32[]{:S(2)}) collective-permute-start(bf16[4,64,100]{2,1,0:T(8,128)(2,1)S(1)} %copy-done.17), channel_id=1, source_target_pairs={{0,64},{64,128},{128,192},{192,0},{1,65},{65,129},{129,193},{193,1... | collective-permute-start | bytes 153608 | tf_op jit(solution)/shard_map/ppermute | solution.py:356
  45.0 26.3 %collective-permute-start.9 = (bf16[4,64,100]{2,1,0:T(8,128)(2,1)S(1)}, bf16[4,64,100]{2,1,0:T(8,128)(2,1)S(1)}, u32[]{:S(2)}, u32[]{:S(2)}) collective-permute-start(bf16[4,64,100]{2,1,0:T(8,128)(2,1)S(1)} %copy-done.16), channel_id=1, source_target_pairs={{0,128},{64,192},{128,0},{192,64},{1,129},{65,193},{129,1},{193,65... | collective-permute-start | bytes 153608 | tf_op jit(solution)/shard_map/ppermute | solution.py:357
  47.4 23.8 %collective-permute-start.10 = (bf16[4,64,100]{2,1,0:T(8,128)(2,1)S(1)}, bf16[4,64,100]{2,1,0:T(8,128)(2,1)S(1)}, u32[]{:S(2)}, u32[]{:S(2)}) collective-permute-start(bf16[4,64,100]{2,1,0:T(8,128)(2,1)S(1)} %copy-done.15), channel_id=1, source_target_pairs={{0,192},{64,0},{128,64},{192,128},{1,193},{65,1},{129,65},{193,129... | collective-permute-start | bytes 153608 | tf_op jit(solution)/shard_map/ppermute | solution.py:358
  61.6 10.3 %collective-permute-start.5 = (f32[16,384]{1,0:T(8,128)S(1)}, f32[16,384]{1,0:T(8,128)S(1)}, u32[]{:S(2)}, u32[]{:S(2)}) collective-permute-start(f32[16,384]{1,0:T(8,128)S(1)} %get-tuple-element.61), channel_id=1, source_target_pairs={{0,1},{1,2},{2,3},{3,0},{4,5},{5,6},{6,7},{7,4},{8,9},{9,10},{10,1... | collective-permute-start | bytes 73736 | tf_op jit(solution)/shard_map/ppermute | solution.py:371
  64.6 7.2 %collective-permute-start.6 = (f32[16,384]{1,0:T(8,128)S(1)}, f32[16,384]{1,0:T(8,128)S(1)}, u32[]{:S(2)}, u32[]{:S(2)}) collective-permute-start(f32[16,384]{1,0:T(8,128)S(1)} %get-tuple-element.62), channel_id=1, source_target_pairs={{0,2},{1,3},{2,0},{3,1},{4,6},{5,7},{6,4},{7,5},{8,10},{9,11},{10,... | collective-permute-start | bytes 73736 | tf_op jit(solution)/shard_map/ppermute | solution.py:372
  68.9 3.9 %collective-permute-start.7 = (f32[16,384]{1,0:T(8,128)S(1)}, f32[16,384]{1,0:T(8,128)S(1)}, u32[]{:S(2)}, u32[]{:S(2)}) collective-permute-start(f32[16,384]{1,0:T(8,128)S(1)} %get-tuple-element.63), channel_id=1, source_target_pairs={{0,3},{1,0},{2,1},{3,2},{4,7},{5,4},{6,5},{7,6},{8,11},{9,8},{10,9... | collective-permute-start | bytes 73736 | tf_op jit(solution)/shard_map/ppermute | solution.py:373
  87.7 5.2 %collective-permute-start.11 = (f32[32,16,128]{2,1,0:T(8,128)S(1)}, f32[32,16,128]{2,1,0:T(8,128)S(1)}, u32[]{:S(2)}, u32[]{:S(2)}) collective-permute-start(f32[32,16,128]{2,1,0:T(8,128)S(1)} %all_to_all.10.refs_1_), channel_id=1, source_target_pairs={{0,4},{4,0},{1,5},{5,1},{2,6},{6,2},{3,7},{7,3},{8,12},{12,8},{9,1... | collective-permute-start | bytes 786440 | tf_op jit(solution)/shard_map/ppermute | solution.py:383
  (7 other events, 4.3 us)

commit v3 on v2

v3 whole, which is shorter than its diff:
```python
import math

import jax
import jax.numpy as jnp
from jax import lax
from jax.experimental import pallas as pl
from jax.experimental.pallas import tpu as pltpu
from jax.sharding import Mesh
from jax.sharding import PartitionSpec as P

ALPHA = 0.95
NAMES = ("y", "zlo", "x", "core", "zhi")
PLANE = ("y", "zlo", "x")
GRID = ("zlo", "x", "core")
F32 = jnp.float32
BF16 = jnp.bfloat16
GELU_C = math.sqrt(2.0 / math.pi)
GELU_A = 0.044715
PARAMS = pltpu.CompilerParams(vmem_limit_bytes=24 * 1024 * 1024)
SMEM = pl.BlockSpec(memory_space=pltpu.SMEM)

PER_BLOCK = 13
ROW_BIN, ROW_BOUT, ROW_LOSS = 121, 122, 15


def shift(axis, step):
    size = lax.axis_size(axis)
    return [(i, (i + step) % size) for i in range(size)]


def const_spec(shape):
    return pl.BlockSpec(shape, lambda *_: (0,) * len(shape))


def fold(block):
    row = lax.broadcasted_iota(jnp.int32, block.shape, 0)
    up = pltpu.roll(block, 12, 0)
    low = (row == 13) | (row == 14)
    return jnp.where((row == 9) | (row == 10), block + up, jnp.where(low, 0.0, block))


def unfold(block):
    row = lax.broadcasted_iota(jnp.int32, block.shape, 0)
    low = block - block.astype(BF16).astype(F32)
    return jnp.where((row == 13) | (row == 14), pltpu.roll(low, 4, 0), block)


def cotangent_kernel(
    ids, rank_hbm, obs_hbm, area_hbm, vw_hbm, x_hbm, w_in_hbm, b_in_hbm, w_out_hbm, b_out_hbm,
    weight_ref, bout_ref, send0, send1, send2, send3, x_ref, w_in_ref, b_in_ref, w_out_ref, b_out_ref,
    every, rank_ref, obs_ref, area_ref, vw_ref, sems,
):
    pairs = [(rank_hbm, rank_ref), (obs_hbm, obs_ref), (area_hbm, area_ref), (vw_hbm, vw_ref)]
    needed = len(pairs)
    pairs += [(w_out_hbm, w_out_ref), (b_in_hbm, b_in_ref), (b_out_hbm, b_out_ref)]
    for source, target in ((x_hbm, x_ref), (w_in_hbm, w_in_ref)):
        piece = source.shape[0] // 4
        for i in range(4):
            rows = pl.ds(i * piece, piece)
            pairs.append((source.at[rows, :], target.at[rows, :]))
    fetches = [
        pltpu.make_async_copy(source, target, sems.at[i]) for i, (source, target) in enumerate(pairs)
    ]
    for fetch in fetches:
        fetch.start()
    for fetch in fetches[:needed]:
        fetch.wait()
    n_mem, sub, n_vars = rank_ref.shape
    mem_dev = n_mem // 4
    epsil = (1.0 - ALPHA) / n_mem
    row = lax.broadcasted_iota(jnp.int32, (sub, sub), 0)
    lane = lax.broadcasted_iota(jnp.int32, (sub, sub), 1)
    area = jnp.sum(jnp.where(row == lane, area_ref[...], 0.0), axis=1, keepdims=True)
    weight = area * vw_ref[...]
    weight_ref[...] = weight
    obs = obs_ref[...]
    total = jnp.zeros_like(weight)
    for member in range(n_mem):
        rank = rank_ref[member]
        sign = jnp.where(rank >= obs, 1.0, -1.0)
        centred = (2 * rank - n_mem + 1).astype(F32)
        cot = (weight * (sign - (1.0 - epsil) / (n_mem - 1) * centred)).astype(BF16)
        every[member // mem_dev, member % mem_dev] = cot
        total = total + cot.astype(F32)
    bout_ref[...] = jnp.sum(total, axis=0, keepdims=True)
    y = ids[0]
    for k, out in enumerate((send0, send1, send2, send3)):
        out[...] = every[lax.rem(y + k, 4)]
    for fetch in fetches[needed:]:
        fetch.wait()


def forward_kernel(
    ids, x_ref, w_in_ref, b_in_ref, w_out_ref, b_out_ref,
    hidden_ref, slope_ref, send0, send1, send2, send3, values,
):
    step = pl.program_id(0)
    mem_dev, sub, _ = send0.shape
    pre = jnp.dot(x_ref[...], w_in_ref[...], preferred_element_type=F32) + b_in_ref[...]
    square = pre * pre
    t = jnp.tanh(pre * (GELU_C + (GELU_C * GELU_A) * square))
    half = 0.5 + 0.5 * t
    hidden = (pre * half).astype(BF16)
    hidden_ref[...] = hidden
    slope_ref[...] = half + pre * (0.5 - 0.5 * (t * t)) * (
        GELU_C + (3.0 * GELU_A * GELU_C) * square
    )
    part = lax.dot_general(
        hidden, w_out_ref[...], (((1,), (1,)), ((), ())), preferred_element_type=F32
    )

    @pl.when(step == 0)
    def _():
        values[...] = part + b_out_ref[...]

    @pl.when(step > 0)
    def _():
        values[...] += part

    @pl.when(step == pl.num_programs(0) - 1)
    def _():
        y = ids[0]
        for k, out in enumerate((send0, send1, send2, send3)):
            dest = lax.rem(y + k, 4)
            for m in range(mem_dev):
                start = pl.multiple_of(m * 4 * sub + dest * sub, sub)
                out[m] = values[pl.ds(start, sub), :].astype(BF16)


def loss_kernel(got0, got1, got2, got3, target_ref, weight_ref, loss_ref):
    gots = (got0, got1, got2, got3)
    mem_dev = got0.shape[0]
    n_mem = 4 * mem_dev
    epsil = (1.0 - ALPHA) / n_mem
    ens = [got[m].astype(F32) for got in gots for m in range(mem_dev)]
    truth = target_ref[...]
    skill = jnp.zeros_like(truth)
    spread = jnp.zeros_like(truth)
    for j in range(n_mem):
        skill = skill + jnp.abs(ens[j] - truth)
        for k in range(j):
            spread = spread + jnp.abs(ens[j] - ens[k])
    cell = weight_ref[...] * (skill / n_mem - (1.0 - epsil) / (n_mem * (n_mem - 1)) * spread)
    loss_ref[...] = jnp.zeros((8, 128), F32) + jnp.sum(cell)


def backward_kernel(
    ids, got0, got1, got2, got3, x_ref, hidden_ref, slope_ref, w_out_ref, bout_ref,
    keep_ref, send_ref, back, back_wide, small,
):
    mem_dev, sub, n_vars = got0.shape
    core = ids[2]
    hid = hidden_ref.shape[1]
    y = ids[0]
    for k, got in enumerate((got0, got1, got2, got3)):
        source = lax.rem(y + 4 - k, 4)
        for m in range(mem_dev):
            start = pl.multiple_of(m * 4 * sub + source * sub, sub)
            back[pl.ds(start, sub), :] = got[m]
    var = lax.broadcasted_iota(jnp.int32, (n_vars, 128), 0)
    lane = lax.broadcasted_iota(jnp.int32, (n_vars, 128), 1)
    place = jnp.where(lane == var + 3 * (var // PER_BLOCK), 1.0, 0.0).astype(BF16)
    back_wide[...] = jnp.dot(back[...], place, preferred_element_type=F32).astype(BF16)

    for start in range(0, hid, 256):
        cols = slice(start, start + 256)
        upward = jnp.dot(back[...], w_out_ref[:, cols], preferred_element_type=F32)
        dhidden = (upward * slope_ref[:, cols]).astype(BF16)
        small[:, cols] = lax.dot_general(
            back_wide[...], hidden_ref[:, cols], (((0,), (0,)), ((), ())), preferred_element_type=F32
        )
        small[ROW_BIN : ROW_BIN + 1, cols] = jnp.sum(dhidden.astype(F32), axis=0, keepdims=True)
        grad = lax.dot_general(
            x_ref[...], dhidden, (((0,), (0,)), ((), ())), preferred_element_type=F32
        )
        grad = grad.reshape(32, 2, 16, 256)
        first, second = grad[:, 0], grad[:, 1]
        keep_ref[:, :, cols] = jnp.where(core == 0, first, second)
        send_ref[:, :, cols] = jnp.where(core == 0, second, first).astype(BF16)

    small[ROW_BOUT : ROW_BOUT + 1, 0:n_vars] = bout_ref[...]
    for part in range(4):
        start = pl.multiple_of((2 * part + core) * 16, 16)
        rows = small[pl.ds(start, 16), :]
        for j in range(8):
            keep_ref[part * 8 + j, :, hid:] = rows[:, j * 128 : (j + 1) * 128]
        start = pl.multiple_of((2 * part + 1 - core) * 16, 16)
        rows = unfold(small[pl.ds(start, 16), :]).astype(BF16)
        for j in range(8):
            send_ref[part * 8 + j, :, hid:] = rows[:, j * 128 : (j + 1) * 128]


def payload_kernel(keep_ref, got_ref, out_hbm, out_ref, sems):
    n_plane, _, width = keep_ref.shape
    hid = width - 128
    piece = n_plane // 4
    stores = []
    for i in range(4):
        part = slice(i * piece, (i + 1) * piece)
        total = keep_ref[part, :, 0:hid] + got_ref[part, :, 0:hid].astype(F32)
        out_ref[part, :, 0:hid] = total.astype(BF16)
        for j in range(i * piece, (i + 1) * piece):
            block = unfold(keep_ref[j, :, hid:] + fold(got_ref[j, :, hid:].astype(F32)))
            out_ref[j, :, hid:] = block.astype(BF16)
        part = pl.ds(i * piece, piece)
        store = pltpu.make_async_copy(out_ref.at[part], out_hbm.at[part], sems.at[i])
        store.start()
        stores.append(store)
    for store in stores:
        store.wait()


def plane_kernel(ids, landed_ref, own_ref, small_ref, part1, part2, part3):
    hid = own_ref.shape[1]
    total = jnp.sum(landed_ref[...].astype(F32), axis=0)
    small = fold(total[:, hid:])
    small_ref[...] = small
    zhi = ids[1]
    quarters = [total[4 * z : 4 * z + 4, 0:hid] for z in range(4)]

    def quarter(which):
        out = quarters[3]
        for z in range(3):
            out = jnp.where(which == z, quarters[z], out)
        return out

    own_ref[...] = quarter(zhi)
    for k, out in ((1, part1), (2, part2), (3, part3)):
        rows = quarter(lax.rem(zhi + k, 4))
        for j in range(4):
            out[4 * j : 4 * j + 4, 0:256] = rows[:, j * 256 : (j + 1) * 256]
        out[:, 256:384] = small


def total_kernel(scale, ids, own_ref, small_ref, got1, got2, got3, loss_ref, grad_ref, copies_ref):
    zhi = ids[1]
    for j in range(4):
        acc = own_ref[:, j * 256 : (j + 1) * 256]
        for got in (got1, got2, got3):
            acc = acc + got[4 * j : 4 * j + 4, 0:256]
        grad_ref[:, j * 256 : (j + 1) * 256] = acc * scale
    parts = [small_ref[...]] + [got[:, 256:384] for got in (got1, got2, got3)]
    acc = None
    for source in range(4):
        term = parts[0]
        for k in range(1, 4):
            term = jnp.where(lax.rem(zhi + 4 - k, 4) == source, parts[k], term)
        acc = term if acc is None else acc + term
    row = lax.broadcasted_iota(jnp.int32, acc.shape, 0)
    acc = jnp.where(row == ROW_LOSS, loss_ref[0:1, :], acc)
    copies_ref[...] = jnp.broadcast_to(acc[None], copies_ref.shape)


def final_kernel(scale, loss_scale, ids, mine, theirs, out_ref, bin_ref, bout_ref, loss_ref, full):
    core = ids[2]
    n_vars = out_ref.shape[0]
    for which, blocks in ((core, mine), (1 - core, theirs)):
        for part in range(4):
            start = pl.multiple_of((2 * part + which) * 16, 16)
            for j in range(8):
                full[pl.ds(start, 16), j * 128 : (j + 1) * 128] = blocks[part * 8 + j]
    for q in range(8):
        count = min(PER_BLOCK, n_vars - PER_BLOCK * q)
        out_ref[PER_BLOCK * q : PER_BLOCK * q + count, :] = full[16 * q : 16 * q + count, :] * scale
    bin_ref[...] = full[ROW_BIN : ROW_BIN + 1, :] * scale
    bout_ref[...] = full[ROW_BOUT : ROW_BOUT + 1, 0:n_vars] * scale
    total = jnp.zeros((1, 128), F32)
    for q in range(8):
        for j in range(8):
            total = total + full[16 * q + ROW_LOSS : 16 * q + ROW_LOSS + 1, 128 * j : 128 * (j + 1)]
    loss_ref[...] = total[:, 0:1] * loss_scale


def per_device(latents, w_in, b_in, w_out, b_out, targets, area, var_weight, member_rank, obs_rank):
    mem_dev = latents.shape[1]
    pts_dev = latents.shape[2]
    width = latents.shape[3]
    hid = w_in.shape[1]
    n_vars = w_out.shape[1]
    n_y = lax.axis_size("y")
    n_mem = mem_dev * n_y
    sub = pts_dev // n_y
    rows = mem_dev * pts_dev
    n_points = pts_dev * lax.axis_size(GRID)
    scale = 1.0 / math.sqrt(lax.axis_size("zhi") * n_mem * n_points)
    ids = jnp.stack(
        [lax.axis_index("y"), lax.axis_index("zhi"), lax.axis_index("core")]
    ).astype(jnp.int32)
    shape = jax.ShapeDtypeStruct

    x = latents.reshape(rows, width)
    w_out_t = w_out.T
    ranks = member_rank[0].transpose(0, 2, 1)
    obs = obs_rank[0].T
    truth = targets[0].T
    sent = shape((mem_dev, sub, n_vars), BF16)
    whole = pl.BlockSpec(memory_space=pltpu.VMEM)

    hbm = pl.BlockSpec(memory_space=pltpu.HBM)
    operands = [
        pltpu.with_memory_space_constraint(arr, pltpu.HBM)
        for arr in (
            ranks, obs, area[None, :], var_weight[None, :],
            x, w_in, b_in[None, :], w_out_t, b_out[None, :],
        )
    ]
    weight, bout, cot0, cot1, cot2, cot3, x, w_in, b_in, w_out_t, b_out = pl.pallas_call(
        cotangent_kernel,
        in_specs=[SMEM] + [hbm] * 9,
        out_specs=[whole] * 11,
        out_shape=[shape((sub, n_vars), F32), shape((1, n_vars), F32)]
        + [sent] * 4
        + [
            shape((rows, width), BF16),
            shape((width, hid), BF16),
            shape((1, hid), F32),
            shape((n_vars, hid), BF16),
            shape((1, n_vars), F32),
        ],
        scratch_shapes=[
            pltpu.VMEM((n_y, mem_dev, sub, n_vars), BF16),
            pltpu.VMEM((n_mem, sub, n_vars), jnp.int32),
            pltpu.VMEM((sub, n_vars), jnp.int32),
            pltpu.VMEM((1, sub), F32),
            pltpu.VMEM((1, n_vars), F32),
            pltpu.SemaphoreType.DMA((15,)),
        ],
        compiler_params=PARAMS,
        name="cotangent",
    )(ids, *operands)
    ids_later, cot1, cot2, cot3 = lax.optimization_barrier((ids, cot1, cot2, cot3))
    cot2 = lax.ppermute(cot2, "y", shift("y", 2))
    cot1 = lax.ppermute(cot1, "y", shift("y", 1))
    cot3 = lax.ppermute(cot3, "y", shift("y", 3))

    cols = 512
    by_cols = lambda height: pl.BlockSpec((height, cols), lambda i: (0, i))
    hidden, slope, val0, val1, val2, val3 = pl.pallas_call(
        forward_kernel,
        grid=(hid // cols,),
        in_specs=[
            SMEM,
            const_spec((rows, width)),
            by_cols(width),
            by_cols(1),
            by_cols(n_vars),
            const_spec((1, n_vars)),
        ],
        out_specs=[by_cols(rows), by_cols(rows)] + [const_spec(sent.shape)] * 4,
        out_shape=[shape((rows, hid), BF16), shape((rows, hid), F32)] + [sent] * 4,
        scratch_shapes=[pltpu.VMEM((rows, n_vars), F32)],
        compiler_params=PARAMS,
        name="forward",
    )(ids_later, x, w_in, b_in, w_out_t, b_out)

    n_plane = lax.axis_size(PLANE)
    block = width // (2 * n_plane)
    keep, send = pl.pallas_call(
        backward_kernel,
        in_specs=[SMEM] + [whole] * 9,
        out_specs=[whole] * 2,
        out_shape=[
            shape((n_plane, block, hid + 128), F32),
            shape((n_plane, block, hid + 128), BF16),
        ],
        scratch_shapes=[
            pltpu.VMEM((rows, n_vars), BF16),
            pltpu.VMEM((rows, 128), BF16),
            pltpu.VMEM((128, hid), F32),
        ],
        compiler_params=PARAMS,
        name="backward",
    )(ids, cot0, cot1, cot2, cot3, x, hidden, slope, w_out_t, bout)

    swap = [(0, 1), (1, 0)]
    got = lax.ppermute(send, "core", swap)
    payload_shape = (n_plane, block, hid + 128)
    payload = pl.pallas_call(
        payload_kernel,
        in_specs=[whole] * 2,
        out_specs=hbm,
        out_shape=shape(payload_shape, BF16),
        scratch_shapes=[pltpu.VMEM(payload_shape, BF16), pltpu.SemaphoreType.DMA((4,))],
        compiler_params=PARAMS,
        name="payload",
    )(keep, got)
    payload, val1, val2, val3 = lax.optimization_barrier((payload, val1, val2, val3))
    landed = lax.all_to_all(payload, PLANE, 0, 0, tiled=True)
    val2 = lax.ppermute(val2, "y", shift("y", 2))
    val1 = lax.ppermute(val1, "y", shift("y", 1))
    val3 = lax.ppermute(val3, "y", shift("y", 3))
    part_loss = pl.pallas_call(
        loss_kernel,
        in_specs=[whole] * 6,
        out_specs=whole,
        out_shape=shape((8, 128), F32),
        compiler_params=PARAMS,
        name="loss",
    )(val0, val1, val2, val3, truth, weight)

    part = shape((block, 384), F32)
    own, small, part1, part2, part3 = pl.pallas_call(
        plane_kernel,
        in_specs=[SMEM, whole],
        out_specs=[whole] * 5,
        out_shape=[shape((block // 4, hid), F32), shape((block, 128), F32), part, part, part],
        compiler_params=PARAMS,
        name="plane_sum",
    )(ids, landed)
    part2 = lax.ppermute(part2, "zhi", shift("zhi", 2))
    part1 = lax.ppermute(part1, "zhi", shift("zhi", 1))
    part3 = lax.ppermute(part3, "zhi", shift("zhi", 3))
    grad_in, copies = pl.pallas_call(
        lambda *refs: total_kernel(scale, *refs),
        in_specs=[SMEM] + [whole] * 6,
        out_specs=[whole] * 2,
        out_shape=[shape((block // 4, hid), F32), shape((n_plane, block, 128), F32)],
        compiler_params=PARAMS,
        name="total",
    )(ids, own, small, part1, part2, part3, part_loss)

    mine = lax.all_to_all(copies, PLANE, 0, 0, tiled=True)
    theirs = lax.ppermute(mine, "core", swap)
    grad_out, grad_bin, grad_bout, loss = pl.pallas_call(
        lambda *refs: final_kernel(scale, 1.0 / (n_points * n_vars), *refs),
        in_specs=[SMEM] + [whole] * 2,
        out_specs=[whole] * 4,
        out_shape=[
            shape((n_vars, hid), F32),
            shape((1, hid), F32),
            shape((1, n_vars), F32),
            shape((1, 1), F32),
        ],
        scratch_shapes=[pltpu.VMEM((128, hid), F32)],
        compiler_params=PARAMS,
        name="unpack",
    )(ids, mine, theirs)
    return (loss.reshape(1), grad_in, grad_out.T, grad_bin.reshape(hid), grad_bout.reshape(n_vars))


def solution(mesh):
    split = Mesh(mesh.devices.reshape(4, 2, 4, 2, 4), NAMES)
    points = GRID + ("y",)
    in_specs = (
        P("zhi", "y", GRID, None),
        P(),
        P(),
        P(),
        P(),
        P("zhi", None, points),
        P(points),
        P(),
        P("zhi", None, None, points),
        P("zhi", None, points),
    )
    out_specs = (P("zhi"), P(NAMES, None), P(), P(), P())
    return jax.shard_map(
        per_device, mesh=split, in_specs=in_specs, out_specs=out_specs, check_vma=False
    )
```

time: 94.8 us -> 81.9 us (0.86)
  local copies, waits for them, and re-layouts: 7.45 us -> 0.01 us
  Pallas kernels: 23.2 us -> 18.1 us
    unnamed x36 -> x2, local copies, waits for them, and re-layouts: 7.45 us -> 0.01 us
    pallas_call x6, Pallas kernels: 20.6 us -> 15.5 us  [the longest x1 5.64 us: per_device(): pl.pallas_call(forward_kernel, grid=(hid // cols,), in_specs=[SMEM, const...]
    ppermute x1 -> x0, waiting for transfers between devices: 2.58 us -> none  [per_device(): got_small = lax.ppermute(send_small, 'core', swap)]
    ppermute x1, waiting for transfers between devices: 0.01 us -> 2.47 us  [per_device(): got = lax.ppermute(send, 'core', swap)]
  transfers between devices with their start and end apart: 13 -> 12, of which waited for: 4 -> 4; matrix products, arithmetic and copies ran while one was open for 0% -> 0% of each run, Pallas kernels for 11% -> 9%
where the time goes in v3:
time: 81.9 us; the launch traced here: 81.6 us
  starting transfers between devices  32.2 us (39%)
  Pallas kernels  18.1 us (22%)
  waiting for transfers between devices  16.8 us (21%)
  blocking collectives  13.8 us (17%)
    all_to_all x1, blocking collectives, per_device(): mine = lax.all_to_all(copies, PLANE, 0, 0, tiled=True)  13.8 us
    all_to_all x1, waiting for transfers between devices, per_device(): landed = lax.all_to_all(payload, PLANE, 0, 0, tiled=True)  12.3 us
    all_to_all x1, starting transfers between devices, per_device(): landed = lax.all_to_all(payload, PLANE, 0, 0, tiled=True)  5.89 us
    pallas_call x1, Pallas kernels, per_device(): pl.pallas_call(forward_kernel, grid=(hid // cols,), in_specs=[SMEM, const...  5.64 us
    ppermute x1, starting transfers between devices, per_device(): part2 = lax.ppermute(part2, 'zhi', shift('zhi', 2))  4.21 us
    pallas_call x1, Pallas kernels, per_device(): pl.pallas_call(backward_kernel, in_specs=[SMEM] + [whole] * 9, out_specs=...  4.21 us
    ppermute x1, starting transfers between devices, per_device(): theirs = lax.ppermute(mine, 'core', swap)  4.06 us
    ppermute x1, starting transfers between devices, per_device(): part1 = lax.ppermute(part1, 'zhi', shift('zhi', 1))  3.25 us
  transfers between devices with their start and end apart: 12, of which 4 were waited for; matrix products, arithmetic and copies ran while one was open for 0% of the time, Pallas kernels for 9%

profile of v3, /device:TPU:1, one launch (start us, length us, event | category | flops | bytes accessed | tf_op | source)
XLA Modules:
  0.0 81.6 jit_solution(8421181363834652819)
XLA Ops:
  0.7 3.1 %cotangent.1 = (f32[64,100]{1,0:T(8,128)S(1)}, f32[1,100]{1,0:T(1,128)S(1)}, bf16[4,64,100]{2,1,0:T(8,128)(2,1)S(1)}, bf16[4,64,100]{2,1,0:T(8,128)(2,1)S(1)}, b...) custom-call(s32[3]{0:T(128)S(1)} %pad_add_fusion.ids.refs_0_, ...), custom_call_target="tpu_custom_call" | custom-call | tf_op jit(solution)/shard_map/cotangent/pallas_call | solution.py:307
  3.8 2.2 %collective-permute-start = (bf16[4,64,100]{2,1,0:T(8,128)(2,1)S(1)}, bf16[4,64,100]{2,1,0:T(8,128)(2,1)S(1)}, u32[]{:S(2)}, u32[]{:S(2)}) collective-permute-start(bf16[4,64,100]{2,1,0:T(8,128)(2,1)S(1)} %get-tuple-element.47), channel_id=1, source_target_pairs={{0,64},{64,128},{128,192},{192,0},{1,65},{65,129},{129,193},{193,1... | collective-permute-start | bytes 153608 | tf_op jit(solution)/shard_map/ppermute | solution.py:333
  6.0 2.6 %collective-permute-start.1 = (bf16[4,64,100]{2,1,0:T(8,128)(2,1)S(1)}, bf16[4,64,100]{2,1,0:T(8,128)(2,1)S(1)}, u32[]{:S(2)}, u32[]{:S(2)}) collective-permute-start(bf16[4,64,100]{2,1,0:T(8,128)(2,1)S(1)} %get-tuple-element.48), channel_id=1, source_target_pairs={{0,128},{64,192},{128,0},{192,64},{1,129},{65,193},{129,1},{193,65... | collective-permute-start | bytes 153608 | tf_op jit(solution)/shard_map/ppermute | solution.py:332
  8.7 1.1 %collective-permute-start.2 = (bf16[4,64,100]{2,1,0:T(8,128)(2,1)S(1)}, bf16[4,64,100]{2,1,0:T(8,128)(2,1)S(1)}, u32[]{:S(2)}, u32[]{:S(2)}) collective-permute-start(bf16[4,64,100]{2,1,0:T(8,128)(2,1)S(1)} %get-tuple-element.49), channel_id=1, source_target_pairs={{0,192},{64,0},{128,64},{192,128},{1,193},{65,1},{129,65},{193,129... | collective-permute-start | bytes 153608 | tf_op jit(solution)/shard_map/ppermute | solution.py:334
  9.7 5.6 %forward.1 = (bf16[1024,1024]{1,0:T(8,128)(2,1)S(1)}, f32[1024,1024]{1,0:T(8,128)S(1)}, bf16[4,64,100]{2,1,0:T(8,128)(2,1)S(1)}, bf16[4,64,100]{2,1,0:T(8,128)(2...) custom-call(s32[3]{0:T(128)S(1)} %pad_add_fusion.ids.refs_0_, ...), custom_call_target="tpu_custom_call" | custom-call | tf_op jit(solution)/shard_map/forward/pallas_call | solution.py:338
  15.4 4.2 %backward.1 = (f32[32,16,1152]{2,1,0:T(8,128)S(1)}, bf16[32,16,1152]{2,1,0:T(8,128)(2,1)S(1)}) custom-call(s32[3]{0:T(128)S(1)} %pad_add_fusion.ids.refs_0_, bf16[4,64,100]{2,1,0:T(8,128)(2,1)S(1)} %get-tuple-element.43.got0, bf16[4,64,100]{2,1,0:T(8,128)(2,1)S(1)} %collective-permute-done.got1, bf16[4,64,100]{2,1,0:T(8,128)(2,1)S(1)} %collective-permute-done.1.got2, ...), custom_call_target="tpu_custom_call" | custom-call | tf_op jit(solution)/shard_map/backward/pallas_call | solution.py:358
  19.6 1.6 %collective-permute-start.3 = (bf16[32,16,1152]{2,1,0:T(8,128)(2,1)S(1)}, bf16[32,16,1152]{2,1,0:T(8,128)(2,1)S(1)}, u32[]{:S(2)}, u32[]{:S(2)}) collective-permute-start(bf16[32,16,1152]{2,1,0:T(8,128)(2,1)S(1)} %get-tuple-element.60), channel_id=1, source_target_pairs={{0,4},{4,0},{1,5},{5,1},{2,6},{6,2},{3,7},{7,3},{8,12},{12,8},{9,1... | collective-permute-start | bytes 3538952 | tf_op jit(solution)/shard_map/ppermute | solution.py:376
  21.2 2.5 %collective-permute-done.3.got_ref = bf16[32,16,1152]{2,1,0:T(8,128)(2,1)S(1)} collective-permute-done((bf16[32,16,1152]{2,1,0:T(8,128)(2,1)S(1)}, bf16[32,16,1152]{2,1,0:T(8,128)(2,1)S(1)}, u32[]{:S(2)}, u32[]{:S(2)}) %collective-permute-start.3) | collective-permute-done | bytes 1179680 | tf_op jit(solution)/shard_map/ppermute | solution.py:376
  23.7 1.2 %payload.1 = bf16[32,16,1152]{2,1,0:T(8,128)(2,1)} custom-call(f32[32,16,1152]{2,1,0:T(8,128)S(1)} %get-tuple-element.59.keep_ref, bf16[32,16,1152]{2,1,0:T(8,128)(2,1)S(1)} %collective-permute-done.3.got_ref), custom_call_target="tpu_custom_call" | custom-call | tf_op jit(solution)/shard_map/payload/pallas_call | solution.py:378
  24.9 5.9 %all-to-all-start = ((bf16[32,16,1152]{2,1,0:T(8,128)(2,1)}), bf16[32,16,1152]{2,1,0:T(8,128)(2,1)S(1)}, u32[]{:S(2)}, u32[]{:S(2)}) async-start(bf16[32,16,1152]{2,1,0:T(8,128)(2,1)} %payload.1), calls=%async_computation | async-start | bytes 2359296 | tf_op jit(solution)/shard_map/all_to_all | solution.py:388
  30.8 1.3 %collective-permute-start.7 = (bf16[4,64,100]{2,1,0:T(8,128)(2,1)S(1)}, bf16[4,64,100]{2,1,0:T(8,128)(2,1)S(1)}, u32[]{:S(2)}, u32[]{:S(2)}) collective-permute-start(bf16[4,64,100]{2,1,0:T(8,128)(2,1)S(1)} %get-tuple-element.71), channel_id=1, source_target_pairs={{0,64},{64,128},{128,192},{192,0},{1,65},{65,129},{129,193},{193,1... | collective-permute-start | bytes 153608 | tf_op jit(solution)/shard_map/ppermute | solution.py:390
  32.1 2.4 %collective-permute-start.8 = (bf16[4,64,100]{2,1,0:T(8,128)(2,1)S(1)}, bf16[4,64,100]{2,1,0:T(8,128)(2,1)S(1)}, u32[]{:S(2)}, u32[]{:S(2)}) collective-permute-start(bf16[4,64,100]{2,1,0:T(8,128)(2,1)S(1)} %get-tuple-element.72), channel_id=1, source_target_pairs={{0,128},{64,192},{128,0},{192,64},{1,129},{65,193},{129,1},{193,65... | collective-permute-start | bytes 153608 | tf_op jit(solution)/shard_map/ppermute | solution.py:389
  34.6 1.1 %collective-permute-start.9 = (bf16[4,64,100]{2,1,0:T(8,128)(2,1)S(1)}, bf16[4,64,100]{2,1,0:T(8,128)(2,1)S(1)}, u32[]{:S(2)}, u32[]{:S(2)}) collective-permute-start(bf16[4,64,100]{2,1,0:T(8,128)(2,1)S(1)} %get-tuple-element.73), channel_id=1, source_target_pairs={{0,192},{64,0},{128,64},{192,128},{1,193},{65,1},{129,65},{193,129... | collective-permute-start | bytes 153608 | tf_op jit(solution)/shard_map/ppermute | solution.py:391
  35.7 12.3 %all-to-all-done.landed_ref = bf16[32,16,1152]{2,1,0:T(8,128)(2,1)S(1)} async-done(((bf16[32,16,1152]{2,1,0:T(8,128)(2,1)}), bf16[32,16,1152]{2,1,0:T(8,128)(2,1)S(1)}, u32[]{:S(2)}, u32[]{:S(2)}) %all-to-all-start) | async-done | bytes 1179680 | tf_op jit(solution)/shard_map/all_to_all | solution.py:388
  48.0 0.8 plane_sum.1
  48.7 3.2 %collective-permute-start.4 = (f32[16,384]{1,0:T(8,128)S(1)}, f32[16,384]{1,0:T(8,128)S(1)}, u32[]{:S(2)}, u32[]{:S(2)}) collective-permute-start(f32[16,384]{1,0:T(8,128)S(1)} %get-tuple-element.67), channel_id=1, source_target_pairs={{0,1},{1,2},{2,3},{3,0},{4,5},{5,6},{6,7},{7,4},{8,9},{9,10},{10,1... | collective-permute-start | bytes 73736 | tf_op jit(solution)/shard_map/ppermute | solution.py:411
  52.0 4.2 %collective-permute-start.5 = (f32[16,384]{1,0:T(8,128)S(1)}, f32[16,384]{1,0:T(8,128)S(1)}, u32[]{:S(2)}, u32[]{:S(2)}) collective-permute-start(f32[16,384]{1,0:T(8,128)S(1)} %get-tuple-element.68), channel_id=1, source_target_pairs={{0,2},{1,3},{2,0},{3,1},{4,6},{5,7},{6,4},{7,5},{8,10},{9,11},{10,... | collective-permute-start | bytes 73736 | tf_op jit(solution)/shard_map/ppermute | solution.py:410
  56.2 2.4 %collective-permute-start.6 = (f32[16,384]{1,0:T(8,128)S(1)}, f32[16,384]{1,0:T(8,128)S(1)}, u32[]{:S(2)}, u32[]{:S(2)}) collective-permute-start(f32[16,384]{1,0:T(8,128)S(1)} %get-tuple-element.69), channel_id=1, source_target_pairs={{0,3},{1,0},{2,1},{3,2},{4,7},{5,4},{6,5},{7,6},{8,11},{9,8},{10,9... | collective-permute-start | bytes 73736 | tf_op jit(solution)/shard_map/ppermute | solution.py:412
  59.2 0.9 %collective-permute-done.6.refs_5_ = f32[16,384]{1,0:T(8,128)S(1)} collective-permute-done((f32[16,384]{1,0:T(8,128)S(1)}, f32[16,384]{1,0:T(8,128)S(1)}, u32[]{:S(2)}, u32[]{:S(2)}) %collective-permute-start.6) | collective-permute-done | bytes 24608 | tf_op jit(solution)/shard_map/ppermute | solution.py:412
  60.1 1.2 %total.1 = (f32[4,1024]{1,0:T(4,128)}, f32[32,16,128]{2,1,0:T(8,128)S(1)}) custom-call(s32[3]{0:T(128)S(1)} %pad_add_fusion.ids.refs_0_, f32[4,1024]{1,0:T(4,128)S(1)} %get-tuple-element.65.refs_1_, f32[16,128]{1,0:T(8,128)S(1)} %get-tuple-element.66.refs_2_, f32[16,384]{1,0:T(8,128)S(1)} %collective-permute-done.4.refs_3_, ...), custom_call_target="tpu_custom_call" | custom-call | tf_op jit(solution)/shard_map/total/pallas_call | solution.py:413
  61.2 13.8 %all_to_all.10.refs_1_ = f32[32,16,128]{2,1,0:T(8,128)S(1)} all-to-all(f32[32,16,128]{2,1,0:T(8,128)S(1)} %get-tuple-element.75), channel_id=1, replica_groups=mesh['y'=4,'zlo'=2,'x'=4,'core'=2,'zhi'=4] {'y','zlo','x'}, dimensions={0} | all-to-all | bytes 524288 | tf_op jit(solution)/shard_map/all_to_all | solution.py:422
  75.0 4.1 %collective-permute-start.10 = (f32[32,16,128]{2,1,0:T(8,128)S(1)}, f32[32,16,128]{2,1,0:T(8,128)S(1)}, u32[]{:S(2)}, u32[]{:S(2)}) collective-permute-start(f32[32,16,128]{2,1,0:T(8,128)S(1)} %all_to_all.10.refs_1_), channel_id=1, source_target_pairs={{0,4},{4,0},{1,5},{5,1},{2,6},{6,2},{3,7},{7,3},{8,12},{12,8},{9,1... | collective-permute-start | bytes 786440 | tf_op jit(solution)/shard_map/ppermute | solution.py:423
  79.1 1.2 %collective-permute-done.10.refs_2_ = f32[32,16,128]{2,1,0:T(8,128)S(1)} collective-permute-done((f32[32,16,128]{2,1,0:T(8,128)S(1)}, f32[32,16,128]{2,1,0:T(8,128)S(1)}, u32[]{:S(2)}, u32[]{:S(2)}) %collective-permute-start.10) | collective-permute-done | bytes 262176 | tf_op jit(solution)/shard_map/ppermute | solution.py:423
  80.2 1.4 %unpack.1 = (f32[100,1024]{1,0:T(8,128)}, f32[1,1024]{1,0:T(1,128)}, f32[1,100]{1,0:T(1,128)}, f32[1,1]{1,0:T(1,128)}) custom-call(s32[3]{0:T(128)S(1)} %pad_add_fusion.ids.refs_0_, f32[32,16,128]{2,1,0:T(8,128)S(1)} %all_to_all.10.refs_1_, f32[32,16,128]{2,1,0:T(8,128)S(1)} %collective-permute-done.10.refs_2_), custom_call_target="tpu_custom_call" | custom-call | tf_op jit(solution)/shard_map/unpack/pallas_call | solution.py:424
  (12 shorter events, 0.7 us)
Async XLA Ops:
  3.8 11.5 %collective-permute-start = (bf16[4,64,100]{2,1,0:T(8,128)(2,1)S(1)}, bf16[4,64,100]{2,1,0:T(8,128)(2,1)S(1)}, u32[]{:S(2)}, u32[]{:S(2)}) collective-permute-start(bf16[4,64,100]{2,1,0:T(8,128)(2,1)S(1)} %get-tuple-element.47), channel_id=1, source_target_pairs={{0,64},{64,128},{128,192},{192,0},{1,65},{65,129},{129,193},{193,1... | collective-permute-start | bytes 153608 | tf_op jit(solution)/shard_map/ppermute | solution.py:333
  6.0 9.4 %collective-permute-start.1 = (bf16[4,64,100]{2,1,0:T(8,128)(2,1)S(1)}, bf16[4,64,100]{2,1,0:T(8,128)(2,1)S(1)}, u32[]{:S(2)}, u32[]{:S(2)}) collective-permute-start(bf16[4,64,100]{2,1,0:T(8,128)(2,1)S(1)} %get-tuple-element.48), channel_id=1, source_target_pairs={{0,128},{64,192},{128,0},{192,64},{1,129},{65,193},{129,1},{193,65... | collective-permute-start | bytes 153608 | tf_op jit(solution)/shard_map/ppermute | solution.py:332
  8.7 6.7 %collective-permute-start.2 = (bf16[4,64,100]{2,1,0:T(8,128)(2,1)S(1)}, bf16[4,64,100]{2,1,0:T(8,128)(2,1)S(1)}, u32[]{:S(2)}, u32[]{:S(2)}) collective-permute-start(bf16[4,64,100]{2,1,0:T(8,128)(2,1)S(1)} %get-tuple-element.49), channel_id=1, source_target_pairs={{0,192},{64,0},{128,64},{192,128},{1,193},{65,1},{129,65},{193,129... | collective-permute-start | bytes 153608 | tf_op jit(solution)/shard_map/ppermute | solution.py:334
  19.6 4.1 %collective-permute-start.3 = (bf16[32,16,1152]{2,1,0:T(8,128)(2,1)S(1)}, bf16[32,16,1152]{2,1,0:T(8,128)(2,1)S(1)}, u32[]{:S(2)}, u32[]{:S(2)}) collective-permute-start(bf16[32,16,1152]{2,1,0:T(8,128)(2,1)S(1)} %get-tuple-element.60), channel_id=1, source_target_pairs={{0,4},{4,0},{1,5},{5,1},{2,6},{6,2},{3,7},{7,3},{8,12},{12,8},{9,1... | collective-permute-start | bytes 3538952 | tf_op jit(solution)/shard_map/ppermute | solution.py:376
  24.9 33.7 %copy-start = (f32[1,100,64]{1,2,0:T(8,128)S(1)}, f32[1,100,64]{1,2,0:T(8,128)}, u32[]{:S(2)}) copy-start(f32[1,100,64]{1,2,0:T(8,128)} %param.15) | copy-start | bytes 76804
  24.9 23.1 %all-to-all-start = ((bf16[32,16,1152]{2,1,0:T(8,128)(2,1)}), bf16[32,16,1152]{2,1,0:T(8,128)(2,1)S(1)}, u32[]{:S(2)}, u32[]{:S(2)}) async-start(bf16[32,16,1152]{2,1,0:T(8,128)(2,1)} %payload.1), calls=%async_computation | async-start | bytes 2359296 | tf_op jit(solution)/shard_map/all_to_all | solution.py:388
  30.8 25.4 %collective-permute-start.7 = (bf16[4,64,100]{2,1,0:T(8,128)(2,1)S(1)}, bf16[4,64,100]{2,1,0:T(8,128)(2,1)S(1)}, u32[]{:S(2)}, u32[]{:S(2)}) collective-permute-start(bf16[4,64,100]{2,1,0:T(8,128)(2,1)S(1)} %get-tuple-element.71), channel_id=1, source_target_pairs={{0,64},{64,128},{128,192},{192,0},{1,65},{65,129},{129,193},{193,1... | collective-permute-start | bytes 153608 | tf_op jit(solution)/shard_map/ppermute | solution.py:390
  32.1 26.5 %collective-permute-start.8 = (bf16[4,64,100]{2,1,0:T(8,128)(2,1)S(1)}, bf16[4,64,100]{2,1,0:T(8,128)(2,1)S(1)}, u32[]{:S(2)}, u32[]{:S(2)}) collective-permute-start(bf16[4,64,100]{2,1,0:T(8,128)(2,1)S(1)} %get-tuple-element.72), channel_id=1, source_target_pairs={{0,128},{64,192},{128,0},{192,64},{1,129},{65,193},{129,1},{193,65... | collective-permute-start | bytes 153608 | tf_op jit(solution)/shard_map/ppermute | solution.py:389
  34.6 24.0 %collective-permute-start.9 = (bf16[4,64,100]{2,1,0:T(8,128)(2,1)S(1)}, bf16[4,64,100]{2,1,0:T(8,128)(2,1)S(1)}, u32[]{:S(2)}, u32[]{:S(2)}) collective-permute-start(bf16[4,64,100]{2,1,0:T(8,128)(2,1)S(1)} %get-tuple-element.73), channel_id=1, source_target_pairs={{0,192},{64,0},{128,64},{192,128},{1,193},{65,1},{129,65},{193,129... | collective-permute-start | bytes 153608 | tf_op jit(solution)/shard_map/ppermute | solution.py:391
  48.7 10.5 %collective-permute-start.4 = (f32[16,384]{1,0:T(8,128)S(1)}, f32[16,384]{1,0:T(8,128)S(1)}, u32[]{:S(2)}, u32[]{:S(2)}) collective-permute-start(f32[16,384]{1,0:T(8,128)S(1)} %get-tuple-element.67), channel_id=1, source_target_pairs={{0,1},{1,2},{2,3},{3,0},{4,5},{5,6},{6,7},{7,4},{8,9},{9,10},{10,1... | collective-permute-start | bytes 73736 | tf_op jit(solution)/shard_map/ppermute | solution.py:411
  52.0 7.2 %collective-permute-start.5 = (f32[16,384]{1,0:T(8,128)S(1)}, f32[16,384]{1,0:T(8,128)S(1)}, u32[]{:S(2)}, u32[]{:S(2)}) collective-permute-start(f32[16,384]{1,0:T(8,128)S(1)} %get-tuple-element.68), channel_id=1, source_target_pairs={{0,2},{1,3},{2,0},{3,1},{4,6},{5,7},{6,4},{7,5},{8,10},{9,11},{10,... | collective-permute-start | bytes 73736 | tf_op jit(solution)/shard_map/ppermute | solution.py:410
  56.2 3.9 %collective-permute-start.6 = (f32[16,384]{1,0:T(8,128)S(1)}, f32[16,384]{1,0:T(8,128)S(1)}, u32[]{:S(2)}, u32[]{:S(2)}) collective-permute-start(f32[16,384]{1,0:T(8,128)S(1)} %get-tuple-element.69), channel_id=1, source_target_pairs={{0,3},{1,0},{2,1},{3,2},{4,7},{5,4},{6,5},{7,6},{8,11},{9,8},{10,9... | collective-permute-start | bytes 73736 | tf_op jit(solution)/shard_map/ppermute | solution.py:412
  75.0 5.2 %collective-permute-start.10 = (f32[32,16,128]{2,1,0:T(8,128)S(1)}, f32[32,16,128]{2,1,0:T(8,128)S(1)}, u32[]{:S(2)}, u32[]{:S(2)}) collective-permute-start(f32[32,16,128]{2,1,0:T(8,128)S(1)} %all_to_all.10.refs_1_), channel_id=1, source_target_pairs={{0,4},{4,0},{1,5},{5,1},{2,6},{6,2},{3,7},{7,3},{8,12},{12,8},{9,1... | collective-permute-start | bytes 786440 | tf_op jit(solution)/shard_map/ppermute | solution.py:423

commit v4 on v3

--- a/solution.py
+++ b/solution.py
@@ -28,6 +28,10 @@
     return [(i, (i + step) % size) for i in range(size)]
 
 
+def pairs_of(axis, step):
+    return [(i, i ^ step) for i in range(lax.axis_size(axis))]
+
+
 def const_spec(shape):
     return pl.BlockSpec(shape, lambda *_: (0,) * len(shape))
 
@@ -47,7 +51,7 @@
 
 def cotangent_kernel(
     ids, rank_hbm, obs_hbm, area_hbm, vw_hbm, x_hbm, w_in_hbm, b_in_hbm, w_out_hbm, b_out_hbm,
-    weight_ref, bout_ref, send0, send1, send2, send3, x_ref, w_in_ref, b_in_ref, w_out_ref, b_out_ref,
+    weight_ref, bout_ref, send0, send2, send1, send3, x_ref, w_in_ref, b_in_ref, w_out_ref, b_out_ref,
     every, rank_ref, obs_ref, area_ref, vw_ref, sems,
 ):
     pairs = [(rank_hbm, rank_ref), (obs_hbm, obs_ref), (area_hbm, area_ref), (vw_hbm, vw_ref)]
@@ -85,14 +89,14 @@
     bout_ref[...] = jnp.sum(total, axis=0, keepdims=True)
     y = ids[0]
     for k, out in enumerate((send0, send1, send2, send3)):
-        out[...] = every[lax.rem(y + k, 4)]
+        out[...] = every[y ^ k]
     for fetch in fetches[needed:]:
         fetch.wait()
 
 
 def forward_kernel(
     ids, x_ref, w_in_ref, b_in_ref, w_out_ref, b_out_ref,
-    hidden_ref, slope_ref, send0, send1, send2, send3, values,
+    hidden_ref, slope_ref, send0, send2, send1, send3, values,
 ):
     step = pl.program_id(0)
     mem_dev, sub, _ = send0.shape
@@ -121,13 +125,13 @@
     def _():
         y = ids[0]
         for k, out in enumerate((send0, send1, send2, send3)):
-            dest = lax.rem(y + k, 4)
+            dest = y ^ k
             for m in range(mem_dev):
                 start = pl.multiple_of(m * 4 * sub + dest * sub, sub)
                 out[m] = values[pl.ds(start, sub), :].astype(BF16)
 
 
-def loss_kernel(got0, got1, got2, got3, target_ref, weight_ref, loss_ref):
+def loss_kernel(got0, got2, got1, got3, target_ref, weight_ref, loss_ref):
     gots = (got0, got1, got2, got3)
     mem_dev = got0.shape[0]
     n_mem = 4 * mem_dev
@@ -145,7 +149,7 @@
 
 
 def backward_kernel(
-    ids, got0, got1, got2, got3, x_ref, hidden_ref, slope_ref, w_out_ref, bout_ref,
+    ids, got0, got2, got1, got3, x_ref, hidden_ref, slope_ref, w_out_ref, bout_ref,
     keep_ref, send_ref, back, back_wide, small,
 ):
     mem_dev, sub, n_vars = got0.shape
@@ -153,7 +157,7 @@
     hid = hidden_ref.shape[1]
     y = ids[0]
     for k, got in enumerate((got0, got1, got2, got3)):
-        source = lax.rem(y + 4 - k, 4)
+        source = y ^ k
         for m in range(mem_dev):
             start = pl.multiple_of(m * 4 * sub + source * sub, sub)
             back[pl.ds(start, sub), :] = got[m]
@@ -210,7 +214,7 @@
         store.wait()
 
 
-def plane_kernel(ids, landed_ref, own_ref, small_ref, part1, part2, part3):
+def plane_kernel(ids, landed_ref, own_ref, small_ref, part2, part1, part3):
     hid = own_ref.shape[1]
     total = jnp.sum(landed_ref[...].astype(F32), axis=0)
     small = fold(total[:, hid:])
@@ -232,13 +236,13 @@
         out[:, 256:384] = small
 
 
-def total_kernel(scale, ids, own_ref, small_ref, got1, got2, got3, loss_ref, grad_ref, copies_ref):
+def total_kernel(ids, own_ref, small_ref, got2, got1, got3, loss_ref, grad_ref, copies_ref):
     zhi = ids[1]
     for j in range(4):
         acc = own_ref[:, j * 256 : (j + 1) * 256]
         for got in (got1, got2, got3):
             acc = acc + got[4 * j : 4 * j + 4, 0:256]
-        grad_ref[:, j * 256 : (j + 1) * 256] = acc * scale
+        grad_ref[:, j * 256 : (j + 1) * 256] = acc
     parts = [small_ref[...]] + [got[:, 256:384] for got in (got1, got2, got3)]
     acc = None
     for source in range(4):
@@ -251,9 +255,22 @@
     copies_ref[...] = jnp.broadcast_to(acc[None], copies_ref.shape)
 
 
-def final_kernel(scale, loss_scale, ids, mine, theirs, out_ref, bin_ref, bout_ref, loss_ref, full):
+def final_kernel(
+    scale, loss_scale, ids, grad_ref, mine, theirs,
+    in_hbm, out_hbm, bin_hbm, bout_hbm, loss_hbm,
+    full, in_ref, out_ref, bin_ref, bout_ref, loss_ref, sems,
+):
     core = ids[2]
     n_vars = out_ref.shape[0]
+    stores = []
+
+    def store(source, target):
+        copy = pltpu.make_async_copy(source, target, sems.at[len(stores)])
+        copy.start()
+        stores.append(copy)
+
+    in_ref[...] = grad_ref[...] * scale
+    store(in_ref, in_hbm)
     for which, blocks in ((core, mine), (1 - core, theirs)):
         for part in range(4):
             start = pl.multiple_of((2 * part + which) * 16, 16)
@@ -262,13 +279,21 @@
     for q in range(8):
         count = min(PER_BLOCK, n_vars - PER_BLOCK * q)
         out_ref[PER_BLOCK * q : PER_BLOCK * q + count, :] = full[16 * q : 16 * q + count, :] * scale
+        if q == 3:
+            store(out_ref.at[0:48, :], out_hbm.at[0:48, :])
+    store(out_ref.at[48:n_vars, :], out_hbm.at[48:n_vars, :])
     bin_ref[...] = full[ROW_BIN : ROW_BIN + 1, :] * scale
+    store(bin_ref, bin_hbm)
     bout_ref[...] = full[ROW_BOUT : ROW_BOUT + 1, 0:n_vars] * scale
+    store(bout_ref, bout_hbm)
     total = jnp.zeros((1, 128), F32)
     for q in range(8):
         for j in range(8):
             total = total + full[16 * q + ROW_LOSS : 16 * q + ROW_LOSS + 1, 128 * j : 128 * (j + 1)]
     loss_ref[...] = total[:, 0:1] * loss_scale
+    store(loss_ref, loss_hbm)
+    for copy in stores:
+        copy.wait()
 
 
 def per_device(latents, w_in, b_in, w_out, b_out, targets, area, var_weight, member_rank, obs_rank):
@@ -304,7 +329,7 @@
             x, w_in, b_in[None, :], w_out_t, b_out[None, :],
         )
     ]
-    weight, bout, cot0, cot1, cot2, cot3, x, w_in, b_in, w_out_t, b_out = pl.pallas_call(
+    weight, bout, cot0, cot2, cot1, cot3, x, w_in, b_in, w_out_t, b_out = pl.pallas_call(
         cotangent_kernel,
         in_specs=[SMEM] + [hbm] * 9,
         out_specs=[whole] * 11,
@@ -328,14 +353,14 @@
         compiler_params=PARAMS,
         name="cotangent",
     )(ids, *operands)
-    ids_later, cot1, cot2, cot3 = lax.optimization_barrier((ids, cot1, cot2, cot3))
-    cot2 = lax.ppermute(cot2, "y", shift("y", 2))
-    cot1 = lax.ppermute(cot1, "y", shift("y", 1))
-    cot3 = lax.ppermute(cot3, "y", shift("y", 3))
+    ids_later, cot2, cot1, cot3 = lax.optimization_barrier((ids, cot2, cot1, cot3))
+    cot2 = lax.ppermute(cot2, "y", pairs_of("y", 2))
+    cot1 = lax.ppermute(cot1, "y", pairs_of("y", 1))
+    cot3 = lax.ppermute(cot3, "y", pairs_of("y", 3))
 
     cols = 512
     by_cols = lambda height: pl.BlockSpec((height, cols), lambda i: (0, i))
-    hidden, slope, val0, val1, val2, val3 = pl.pallas_call(
+    hidden, slope, val0, val2, val1, val3 = pl.pallas_call(
         forward_kernel,
         grid=(hid // cols,),
         in_specs=[
@@ -370,7 +395,7 @@
         ],
         compiler_params=PARAMS,
         name="backward",
-    )(ids, cot0, cot1, cot2, cot3, x, hidden, slope, w_out_t, bout)
+    )(ids, cot0, cot2, cot1, cot3, x, hidden, slope, w_out_t, bout)
 
     swap = [(0, 1), (1, 0)]
     got = lax.ppermute(send, "core", swap)
@@ -384,11 +409,11 @@
         compiler_params=PARAMS,
         name="payload",
     )(keep, got)
-    payload, val1, val2, val3 = lax.optimization_barrier((payload, val1, val2, val3))
+    payload, val2, val1, val3 = lax.optimization_barrier((payload, val2, val1, val3))
     landed = lax.all_to_all(payload, PLANE, 0, 0, tiled=True)
-    val2 = lax.ppermute(val2, "y", shift("y", 2))
-    val1 = lax.ppermute(val1, "y", shift("y", 1))
-    val3 = lax.ppermute(val3, "y", shift("y", 3))
+    val2 = lax.ppermute(val2, "y", pairs_of("y", 2))
+    val1 = lax.ppermute(val1, "y", pairs_of("y", 1))
+    val3 = lax.ppermute(val3, "y", pairs_of("y", 3))
     part_loss = pl.pallas_call(
         loss_kernel,
         in_specs=[whole] * 6,
@@ -396,10 +421,10 @@
         out_shape=shape((8, 128), F32),
         compiler_params=PARAMS,
         name="loss",
-    )(val0, val1, val2, val3, truth, weight)
+    )(val0, val2, val1, val3, truth, weight)
 
     part = shape((block, 384), F32)
-    own, small, part1, part2, part3 = pl.pallas_call(
+    own, small, part2, part1, part3 = pl.pallas_call(
         plane_kernel,
         in_specs=[SMEM, whole],
         out_specs=[whole] * 5,
@@ -411,30 +436,34 @@
     part1 = lax.ppermute(part1, "zhi", shift("zhi", 1))
     part3 = lax.ppermute(part3, "zhi", shift("zhi", 3))
     grad_in, copies = pl.pallas_call(
-        lambda *refs: total_kernel(scale, *refs),
+        total_kernel,
         in_specs=[SMEM] + [whole] * 6,
         out_specs=[whole] * 2,
         out_shape=[shape((block // 4, hid), F32), shape((n_plane, block, 128), F32)],
         compiler_params=PARAMS,
         name="total",
-    )(ids, own, small, part1, part2, part3, part_loss)
+    )(ids, own, small, part2, part1, part3, part_loss)
 
     mine = lax.all_to_all(copies, PLANE, 0, 0, tiled=True)
     theirs = lax.ppermute(mine, "core", swap)
-    grad_out, grad_bin, grad_bout, loss = pl.pallas_call(
+    finals = [
+        shape((block // 4, hid), F32),
+        shape((n_vars, hid), F32),
+        shape((1, hid), F32),
+        shape((1, n_vars), F32),
+        shape((1, 1), F32),
+    ]
+    grad_in, grad_out, grad_bin, grad_bout, loss = pl.pallas_call(
         lambda *refs: final_kernel(scale, 1.0 / (n_points * n_vars), *refs),
-        in_specs=[SMEM] + [whole] * 2,
-        out_specs=[whole] * 4,
-        out_shape=[
-            shape((n_vars, hid), F32),
-            shape((1, hid), F32),
-            shape((1, n_vars), F32),
-            shape((1, 1), F32),
-        ],
-        scratch_shapes=[pltpu.VMEM((128, hid), F32)],
+        in_specs=[SMEM] + [whole] * 3,
+        out_specs=[hbm] * 5,
+        out_shape=finals,
+        scratch_shapes=[pltpu.VMEM((128, hid), F32)]
+        + [pltpu.VMEM(final.shape, F32) for final in finals]
+        + [pltpu.SemaphoreType.DMA((6,))],
         compiler_params=PARAMS,
         name="unpack",
-    )(ids, mine, theirs)
+    )(ids, grad_in, mine, theirs)
     return (loss.reshape(1), grad_in, grad_out.T, grad_bin.reshape(hid), grad_bout.reshape(n_vars))
 
 

time: 81.9 us -> 82.1 us (level)
  waiting for transfers between devices: 16.8 us -> 17.8 us
    ppermute x6, starting transfers between devices: 10.8 us -> 8.32 us  [the longest x1 3.83 us: per_device(): cot2 = lax.ppermute(cot2, 'y', pairs_of('y', 2))]
    ppermute x1, starting transfers between devices: 3.25 us -> 1.19 us  [per_device(): part1 = lax.ppermute(part1, 'zhi', shift('zhi', 1))]
    ppermute x1, starting transfers between devices: 4.21 us -> 6.1 us  [per_device(): part2 = lax.ppermute(part2, 'zhi', shift('zhi', 2))]
    ppermute x1, starting transfers between devices: 1.6 us -> 2.9 us  [per_device(): got = lax.ppermute(send, 'core', swap)]
    all_to_all x1, waiting for transfers between devices: 12.3 us -> 13.4 us  [per_device(): landed = lax.all_to_all(payload, PLANE, 0, 0, tiled=True)]
  transfers between devices with their start and end apart: 12 -> 12, of which waited for: 4 -> 5; matrix products, arithmetic and copies ran while one was open for 0% -> 0% of each run, Pallas kernels for 9% -> 9%
where the time goes in v4:
time: 82.1 us; the launch traced here: 81.8 us
  starting transfers between devices  32 us (39%)
  waiting for transfers between devices  17.8 us (22%)
  Pallas kernels  17.5 us (21%)
  blocking collectives  13.5 us (16%)
  between operations  0.91 us (1%)
    all_to_all x1, blocking collectives, per_device(): mine = lax.all_to_all(copies, PLANE, 0, 0, tiled=True)  13.5 us
    all_to_all x1, waiting for transfers between devices, per_device(): landed = lax.all_to_all(payload, PLANE, 0, 0, tiled=True)  13.4 us
    all_to_all x1, starting transfers between devices, per_device(): landed = lax.all_to_all(payload, PLANE, 0, 0, tiled=True)  6.67 us
    ppermute x1, starting transfers between devices, per_device(): part2 = lax.ppermute(part2, 'zhi', shift('zhi', 2))  6.1 us
    pallas_call x1, Pallas kernels, per_device(): pl.pallas_call(forward_kernel, grid=(hid // cols,), in_specs=[SMEM, const...  5.64 us
    ppermute x1, starting transfers between devices, per_device(): theirs = lax.ppermute(mine, 'core', swap)  4.4 us
    pallas_call x1, Pallas kernels, per_device(): pl.pallas_call(backward_kernel, in_specs=[SMEM] + [whole] * 9, out_specs=...  4.23 us
    ppermute x1, starting transfers between devices, per_device(): cot2 = lax.ppermute(cot2, 'y', pairs_of('y', 2))  3.83 us
  transfers between devices with their start and end apart: 12, of which 5 were waited for; matrix products, arithmetic and copies ran while one was open for 0% of the time, Pallas kernels for 9%

profile of v4, /device:TPU:1, one launch (start us, length us, event | category | flops | bytes accessed | tf_op | source)
XLA Modules:
  0.0 81.8 jit_solution(9702716092741341047)
XLA Ops:
  0.7 3.1 %cotangent.1 = (f32[64,100]{1,0:T(8,128)S(1)}, f32[1,100]{1,0:T(1,128)S(1)}, bf16[4,64,100]{2,1,0:T(8,128)(2,1)S(1)}, bf16[4,64,100]{2,1,0:T(8,128)(2,1)S(1)}, b...) custom-call(s32[3]{0:T(128)S(1)} %pad_add_fusion.ids.refs_0_, ...), custom_call_target="tpu_custom_call" | custom-call | tf_op jit(solution)/shard_map/cotangent/pallas_call | solution.py:332
  3.8 3.8 %collective-permute-start = (bf16[4,64,100]{2,1,0:T(8,128)(2,1)S(1)}, bf16[4,64,100]{2,1,0:T(8,128)(2,1)S(1)}, u32[]{:S(2)}, u32[]{:S(2)}) collective-permute-start(bf16[4,64,100]{2,1,0:T(8,128)(2,1)S(1)} %get-tuple-element.48), channel_id=1, source_target_pairs={{0,128},{64,192},{128,0},{192,64},{1,129},{65,193},{129,1},{193,65... | collective-permute-start | bytes 153608 | tf_op jit(solution)/shard_map/ppermute | solution.py:357
  7.7 0.4 collective-permute-start.1
  8.1 0.4 collective-permute-start.2
  8.5 5.6 %forward.1 = (bf16[1024,1024]{1,0:T(8,128)(2,1)S(1)}, f32[1024,1024]{1,0:T(8,128)S(1)}, bf16[4,64,100]{2,1,0:T(8,128)(2,1)S(1)}, bf16[4,64,100]{2,1,0:T(8,128)(2...) custom-call(s32[3]{0:T(128)S(1)} %pad_add_fusion.ids.refs_0_, ...), custom_call_target="tpu_custom_call" | custom-call | tf_op jit(solution)/shard_map/forward/pallas_call | solution.py:363
  14.1 4.2 %backward.1 = (f32[32,16,1152]{2,1,0:T(8,128)S(1)}, bf16[32,16,1152]{2,1,0:T(8,128)(2,1)S(1)}) custom-call(s32[3]{0:T(128)S(1)} %pad_add_fusion.ids.refs_0_, bf16[4,64,100]{2,1,0:T(8,128)(2,1)S(1)} %get-tuple-element.44.got0, bf16[4,64,100]{2,1,0:T(8,128)(2,1)S(1)} %collective-permute-done.got2, bf16[4,64,100]{2,1,0:T(8,128)(2,1)S(1)} %collective-permute-done.1.got1, ...), custom_call_target="tpu_custom_call" | custom-call | tf_op jit(solution)/shard_map/backward/pallas_call | solution.py:383
  18.4 2.9 %collective-permute-start.3 = (bf16[32,16,1152]{2,1,0:T(8,128)(2,1)S(1)}, bf16[32,16,1152]{2,1,0:T(8,128)(2,1)S(1)}, u32[]{:S(2)}, u32[]{:S(2)}) collective-permute-start(bf16[32,16,1152]{2,1,0:T(8,128)(2,1)S(1)} %get-tuple-element.61), channel_id=1, source_target_pairs={{0,4},{4,0},{1,5},{5,1},{2,6},{6,2},{3,7},{7,3},{8,12},{12,8},{9,1... | collective-permute-start | bytes 3538952 | tf_op jit(solution)/shard_map/ppermute | solution.py:401
  21.3 2.5 %collective-permute-done.3.got_ref = bf16[32,16,1152]{2,1,0:T(8,128)(2,1)S(1)} collective-permute-done((bf16[32,16,1152]{2,1,0:T(8,128)(2,1)S(1)}, bf16[32,16,1152]{2,1,0:T(8,128)(2,1)S(1)}, u32[]{:S(2)}, u32[]{:S(2)}) %collective-permute-start.3) | collective-permute-done | bytes 1179680 | tf_op jit(solution)/shard_map/ppermute | solution.py:401
  23.7 1.2 %payload.1 = bf16[32,16,1152]{2,1,0:T(8,128)(2,1)} custom-call(f32[32,16,1152]{2,1,0:T(8,128)S(1)} %get-tuple-element.60.keep_ref, bf16[32,16,1152]{2,1,0:T(8,128)(2,1)S(1)} %collective-permute-done.3.got_ref), custom_call_target="tpu_custom_call" | custom-call | tf_op jit(solution)/shard_map/payload/pallas_call | solution.py:403
  24.9 6.7 %all-to-all-start = ((bf16[32,16,1152]{2,1,0:T(8,128)(2,1)}), bf16[32,16,1152]{2,1,0:T(8,128)(2,1)S(1)}, u32[]{:S(2)}, u32[]{:S(2)}) async-start(bf16[32,16,1152]{2,1,0:T(8,128)(2,1)} %payload.1), calls=%async_computation | async-start | bytes 2359296 | tf_op jit(solution)/shard_map/all_to_all | solution.py:413
  31.6 2.8 %collective-permute-start.7 = (bf16[4,64,100]{2,1,0:T(8,128)(2,1)S(1)}, bf16[4,64,100]{2,1,0:T(8,128)(2,1)S(1)}, u32[]{:S(2)}, u32[]{:S(2)}) collective-permute-start(bf16[4,64,100]{2,1,0:T(8,128)(2,1)S(1)} %get-tuple-element.72), channel_id=1, source_target_pairs={{0,128},{64,192},{128,0},{192,64},{1,129},{65,193},{129,1},{193,65... | collective-permute-start | bytes 153608 | tf_op jit(solution)/shard_map/ppermute | solution.py:414
  34.8 0.6 collective-permute-start.9
  35.3 13.4 %all-to-all-done.landed_ref = bf16[32,16,1152]{2,1,0:T(8,128)(2,1)S(1)} async-done(((bf16[32,16,1152]{2,1,0:T(8,128)(2,1)}), bf16[32,16,1152]{2,1,0:T(8,128)(2,1)S(1)}, u32[]{:S(2)}, u32[]{:S(2)}) %all-to-all-start) | async-done | bytes 1179680 | tf_op jit(solution)/shard_map/all_to_all | solution.py:413
  48.8 0.8 plane_sum.1
  49.6 6.1 %collective-permute-start.4 = (f32[16,384]{1,0:T(8,128)S(1)}, f32[16,384]{1,0:T(8,128)S(1)}, u32[]{:S(2)}, u32[]{:S(2)}) collective-permute-start(f32[16,384]{1,0:T(8,128)S(1)} %get-tuple-element.68), channel_id=1, source_target_pairs={{0,2},{1,3},{2,0},{3,1},{4,6},{5,7},{6,4},{7,5},{8,10},{9,11},{10,... | collective-permute-start | bytes 73736 | tf_op jit(solution)/shard_map/ppermute | solution.py:435
  55.7 1.2 %collective-permute-start.5 = (f32[16,384]{1,0:T(8,128)S(1)}, f32[16,384]{1,0:T(8,128)S(1)}, u32[]{:S(2)}, u32[]{:S(2)}) collective-permute-start(f32[16,384]{1,0:T(8,128)S(1)} %get-tuple-element.69), channel_id=1, source_target_pairs={{0,1},{1,2},{2,3},{3,0},{4,5},{5,6},{6,7},{7,4},{8,9},{9,10},{10,1... | collective-permute-start | bytes 73736 | tf_op jit(solution)/shard_map/ppermute | solution.py:436
  56.8 2.4 %collective-permute-start.6 = (f32[16,384]{1,0:T(8,128)S(1)}, f32[16,384]{1,0:T(8,128)S(1)}, u32[]{:S(2)}, u32[]{:S(2)}) collective-permute-start(f32[16,384]{1,0:T(8,128)S(1)} %get-tuple-element.70), channel_id=1, source_target_pairs={{0,3},{1,0},{2,1},{3,2},{4,7},{5,4},{6,5},{7,6},{8,11},{9,8},{10,9... | collective-permute-start | bytes 73736 | tf_op jit(solution)/shard_map/ppermute | solution.py:437
  59.2 0.6 loss.1.loss_ref
  59.9 0.6 collective-permute-done.5.got1
  60.5 0.6 total.1
  61.1 13.5 %all_to_all.10.refs_2_ = f32[32,16,128]{2,1,0:T(8,128)S(1)} all-to-all(f32[32,16,128]{2,1,0:T(8,128)S(1)} %get-tuple-element.77), channel_id=1, replica_groups=mesh['y'=4,'zlo'=2,'x'=4,'core'=2,'zhi'=4] {'y','zlo','x'}, dimensions={0} | all-to-all | bytes 524288 | tf_op jit(solution)/shard_map/all_to_all | solution.py:447
  74.6 4.4 %collective-permute-start.10 = (f32[32,16,128]{2,1,0:T(8,128)S(1)}, f32[32,16,128]{2,1,0:T(8,128)S(1)}, u32[]{:S(2)}, u32[]{:S(2)}) collective-permute-start(f32[32,16,128]{2,1,0:T(8,128)S(1)} %all_to_all.10.refs_2_), channel_id=1, source_target_pairs={{0,4},{4,0},{1,5},{5,1},{2,6},{6,2},{3,7},{7,3},{8,12},{12,8},{9,1... | collective-permute-start | bytes 786440 | tf_op jit(solution)/shard_map/ppermute | solution.py:448
  79.1 1.2 %collective-permute-done.10.refs_3_ = f32[32,16,128]{2,1,0:T(8,128)S(1)} collective-permute-done((f32[32,16,128]{2,1,0:T(8,128)S(1)}, f32[32,16,128]{2,1,0:T(8,128)S(1)}, u32[]{:S(2)}, u32[]{:S(2)}) %collective-permute-start.10) | collective-permute-done | bytes 262176 | tf_op jit(solution)/shard_map/ppermute | solution.py:448
  80.2 1.4 %unpack.1 = (f32[4,1024]{1,0:T(4,128)}, f32[100,1024]{1,0:T(8,128)}, f32[1,1024]{1,0:T(1,128)}, f32[1,100]{1,0:T(1,128)}, f32[1,1]{1,0:T(1,128)}) custom-call(s32[3]{0:T(128)S(1)} %pad_add_fusion.ids.refs_0_, f32[4,1024]{1,0:T(4,128)S(1)} %get-tuple-element.76.refs_1_, f32[32,16,128]{2,1,0:T(8,128)S(1)} %all_to_all.10.refs_2_, ...), custom_call_target="tpu_custom_call" | custom-call | tf_op jit(solution)/shard_map/unpack/pallas_call | solution.py:456
  (12 shorter events, 0.5 us)
Async XLA Ops:
  3.8 10.3 %collective-permute-start = (bf16[4,64,100]{2,1,0:T(8,128)(2,1)S(1)}, bf16[4,64,100]{2,1,0:T(8,128)(2,1)S(1)}, u32[]{:S(2)}, u32[]{:S(2)}) collective-permute-start(bf16[4,64,100]{2,1,0:T(8,128)(2,1)S(1)} %get-tuple-element.48), channel_id=1, source_target_pairs={{0,128},{64,192},{128,0},{192,64},{1,129},{65,193},{129,1},{193,65... | collective-permute-start | bytes 153608 | tf_op jit(solution)/shard_map/ppermute | solution.py:357
  7.7 6.4 %collective-permute-start.1 = (bf16[4,64,100]{2,1,0:T(8,128)(2,1)S(1)}, bf16[4,64,100]{2,1,0:T(8,128)(2,1)S(1)}, u32[]{:S(2)}, u32[]{:S(2)}) collective-permute-start(bf16[4,64,100]{2,1,0:T(8,128)(2,1)S(1)} %get-tuple-element.49), channel_id=1, source_target_pairs={{0,64},{64,0},{128,192},{192,128},{1,65},{65,1},{129,193},{193,129... | collective-permute-start | bytes 153608 | tf_op jit(solution)/shard_map/ppermute | solution.py:358
  8.1 6.1 %collective-permute-start.2 = (bf16[4,64,100]{2,1,0:T(8,128)(2,1)S(1)}, bf16[4,64,100]{2,1,0:T(8,128)(2,1)S(1)}, u32[]{:S(2)}, u32[]{:S(2)}) collective-permute-start(bf16[4,64,100]{2,1,0:T(8,128)(2,1)S(1)} %get-tuple-element.50), channel_id=1, source_target_pairs={{0,192},{64,128},{128,64},{192,0},{1,193},{65,129},{129,65},{193,1... | collective-permute-start | bytes 153608 | tf_op jit(solution)/shard_map/ppermute | solution.py:359
  18.4 5.4 %collective-permute-start.3 = (bf16[32,16,1152]{2,1,0:T(8,128)(2,1)S(1)}, bf16[32,16,1152]{2,1,0:T(8,128)(2,1)S(1)}, u32[]{:S(2)}, u32[]{:S(2)}) collective-permute-start(bf16[32,16,1152]{2,1,0:T(8,128)(2,1)S(1)} %get-tuple-element.61), channel_id=1, source_target_pairs={{0,4},{4,0},{1,5},{5,1},{2,6},{6,2},{3,7},{7,3},{8,12},{12,8},{9,1... | collective-permute-start | bytes 3538952 | tf_op jit(solution)/shard_map/ppermute | solution.py:401
  24.9 34.3 %copy-start = (f32[1,100,64]{1,2,0:T(8,128)S(1)}, f32[1,100,64]{1,2,0:T(8,128)}, u32[]{:S(2)}) copy-start(f32[1,100,64]{1,2,0:T(8,128)} %param.15) | copy-start | bytes 76804
  24.9 23.8 %all-to-all-start = ((bf16[32,16,1152]{2,1,0:T(8,128)(2,1)}), bf16[32,16,1152]{2,1,0:T(8,128)(2,1)S(1)}, u32[]{:S(2)}, u32[]{:S(2)}) async-start(bf16[32,16,1152]{2,1,0:T(8,128)(2,1)} %payload.1), calls=%async_computation | async-start | bytes 2359296 | tf_op jit(solution)/shard_map/all_to_all | solution.py:413
  31.6 25.2 %collective-permute-start.7 = (bf16[4,64,100]{2,1,0:T(8,128)(2,1)S(1)}, bf16[4,64,100]{2,1,0:T(8,128)(2,1)S(1)}, u32[]{:S(2)}, u32[]{:S(2)}) collective-permute-start(bf16[4,64,100]{2,1,0:T(8,128)(2,1)S(1)} %get-tuple-element.72), channel_id=1, source_target_pairs={{0,128},{64,192},{128,0},{192,64},{1,129},{65,193},{129,1},{193,65... | collective-permute-start | bytes 153608 | tf_op jit(solution)/shard_map/ppermute | solution.py:414
  34.5 24.8 %collective-permute-start.8 = (bf16[4,64,100]{2,1,0:T(8,128)(2,1)S(1)}, bf16[4,64,100]{2,1,0:T(8,128)(2,1)S(1)}, u32[]{:S(2)}, u32[]{:S(2)}) collective-permute-start(bf16[4,64,100]{2,1,0:T(8,128)(2,1)S(1)} %get-tuple-element.73), channel_id=1, source_target_pairs={{0,64},{64,0},{128,192},{192,128},{1,65},{65,1},{129,193},{193,129... | collective-permute-start | bytes 153608 | tf_op jit(solution)/shard_map/ppermute | solution.py:415
  34.8 24.5 %collective-permute-start.9 = (bf16[4,64,100]{2,1,0:T(8,128)(2,1)S(1)}, bf16[4,64,100]{2,1,0:T(8,128)(2,1)S(1)}, u32[]{:S(2)}, u32[]{:S(2)}) collective-permute-start(bf16[4,64,100]{2,1,0:T(8,128)(2,1)S(1)} %get-tuple-element.74), channel_id=1, source_target_pairs={{0,192},{64,128},{128,64},{192,0},{1,193},{65,129},{129,65},{193,1... | collective-permute-start | bytes 153608 | tf_op jit(solution)/shard_map/ppermute | solution.py:416
  49.6 10.3 %collective-permute-start.4 = (f32[16,384]{1,0:T(8,128)S(1)}, f32[16,384]{1,0:T(8,128)S(1)}, u32[]{:S(2)}, u32[]{:S(2)}) collective-permute-start(f32[16,384]{1,0:T(8,128)S(1)} %get-tuple-element.68), channel_id=1, source_target_pairs={{0,2},{1,3},{2,0},{3,1},{4,6},{5,7},{6,4},{7,5},{8,10},{9,11},{10,... | collective-permute-start | bytes 73736 | tf_op jit(solution)/shard_map/ppermute | solution.py:435
  55.7 4.8 %collective-permute-start.5 = (f32[16,384]{1,0:T(8,128)S(1)}, f32[16,384]{1,0:T(8,128)S(1)}, u32[]{:S(2)}, u32[]{:S(2)}) collective-permute-start(f32[16,384]{1,0:T(8,128)S(1)} %get-tuple-element.69), channel_id=1, source_target_pairs={{0,1},{1,2},{2,3},{3,0},{4,5},{5,6},{6,7},{7,4},{8,9},{9,10},{10,1... | collective-permute-start | bytes 73736 | tf_op jit(solution)/shard_map/ppermute | solution.py:436
  56.8 3.7 %collective-permute-start.6 = (f32[16,384]{1,0:T(8,128)S(1)}, f32[16,384]{1,0:T(8,128)S(1)}, u32[]{:S(2)}, u32[]{:S(2)}) collective-permute-start(f32[16,384]{1,0:T(8,128)S(1)} %get-tuple-element.70), channel_id=1, source_target_pairs={{0,3},{1,0},{2,1},{3,2},{4,7},{5,4},{6,5},{7,6},{8,11},{9,8},{10,9... | collective-permute-start | bytes 73736 | tf_op jit(solution)/shard_map/ppermute | solution.py:437
  74.6 5.6 %collective-permute-start.10 = (f32[32,16,128]{2,1,0:T(8,128)S(1)}, f32[32,16,128]{2,1,0:T(8,128)S(1)}, u32[]{:S(2)}, u32[]{:S(2)}) collective-permute-start(f32[32,16,128]{2,1,0:T(8,128)S(1)} %all_to_all.10.refs_2_), channel_id=1, source_target_pairs={{0,4},{4,0},{1,5},{5,1},{2,6},{6,2},{3,7},{7,3},{8,12},{12,8},{9,1... | collective-permute-start | bytes 786440 | tf_op jit(solution)/shard_map/ppermute | solution.py:448

commit v5 on v4

--- a/solution.py
+++ b/solution.py
@@ -197,15 +197,16 @@
 def payload_kernel(keep_ref, got_ref, out_hbm, out_ref, sems):
     n_plane, _, width = keep_ref.shape
     hid = width - 128
+    first = hid // 2
     piece = n_plane // 4
     stores = []
     for i in range(4):
         part = slice(i * piece, (i + 1) * piece)
-        total = keep_ref[part, :, 0:hid] + got_ref[part, :, 0:hid].astype(F32)
-        out_ref[part, :, 0:hid] = total.astype(BF16)
+        total = keep_ref[part, :, 0:first] + got_ref[part, :, 0:first].astype(F32)
+        out_ref[part, :, 0:first] = total.astype(BF16)
         for j in range(i * piece, (i + 1) * piece):
             block = unfold(keep_ref[j, :, hid:] + fold(got_ref[j, :, hid:].astype(F32)))
-            out_ref[j, :, hid:] = block.astype(BF16)
+            out_ref[j, :, first:] = block.astype(BF16)
         part = pl.ds(i * piece, piece)
         store = pltpu.make_async_copy(out_ref.at[part], out_hbm.at[part], sems.at[i])
         store.start()
@@ -214,13 +215,36 @@
         store.wait()
 
 
+def second_half_kernel(ids, keep_ref, got_ref, own_ref, part2, part1, part3, quarters):
+    n_plane = keep_ref.shape[0]
+    first = own_ref.shape[1]
+    zhi = ids[1]
+    for n in range(n_plane):
+        total = keep_ref[n, :, first : 2 * first] + got_ref[n, :, first : 2 * first].astype(F32)
+        for z in range(4):
+            quarters[lax.rem(z + 4 - zhi, 4), 4 * n : 4 * n + 4, :] = total[4 * z : 4 * z + 4, :]
+    own_ref[...] = quarters[0]
+    part1[...] = quarters[1].astype(BF16)
+    part2[...] = quarters[2].astype(BF16)
+    part3[...] = quarters[3].astype(BF16)
+
+
+def second_total_kernel(own_ref, got2, got1, got3, out_ref, total, wide):
+    n_plane = out_ref.shape[0]
+    total[...] = own_ref[...] + got1[...].astype(F32) + got2[...].astype(F32) + got3[...].astype(F32)
+    for n in range(n_plane):
+        for j in range(4):
+            wide[n, 4 * j : 4 * j + 4, :] = total[4 * n : 4 * n + 4, 128 * j : 128 * (j + 1)]
+    out_ref[...] = wide[...].astype(BF16)
+
+
 def plane_kernel(ids, landed_ref, own_ref, small_ref, part2, part1, part3):
-    hid = own_ref.shape[1]
+    first = own_ref.shape[1]
     total = jnp.sum(landed_ref[...].astype(F32), axis=0)
-    small = fold(total[:, hid:])
+    small = fold(total[:, first:])
     small_ref[...] = small
     zhi = ids[1]
-    quarters = [total[4 * z : 4 * z + 4, 0:hid] for z in range(4)]
+    quarters = [total[4 * z : 4 * z + 4, 0:first] for z in range(4)]
 
     def quarter(which):
         out = quarters[3]
@@ -232,18 +256,18 @@
     for k, out in ((1, part1), (2, part2), (3, part3)):
         rows = quarter(lax.rem(zhi + k, 4))
         for j in range(4):
-            out[4 * j : 4 * j + 4, 0:256] = rows[:, j * 256 : (j + 1) * 256]
-        out[:, 256:384] = small
-
-
-def total_kernel(ids, own_ref, small_ref, got2, got1, got3, loss_ref, grad_ref, copies_ref):
+            out[4 * j : 4 * j + 4, 0:128] = rows[:, j * 128 : (j + 1) * 128]
+        out[:, 128:256] = small
+
+
+def total_kernel(ids, own_ref, small_ref, got2, got1, got3, loss_ref, second_ref, grad_ref, copies_ref):
     zhi = ids[1]
     for j in range(4):
-        acc = own_ref[:, j * 256 : (j + 1) * 256]
+        acc = own_ref[:, j * 128 : (j + 1) * 128]
         for got in (got1, got2, got3):
-            acc = acc + got[4 * j : 4 * j + 4, 0:256]
-        grad_ref[:, j * 256 : (j + 1) * 256] = acc
-    parts = [small_ref[...]] + [got[:, 256:384] for got in (got1, got2, got3)]
+            acc = acc + got[4 * j : 4 * j + 4, 0:128]
+        grad_ref[:, j * 128 : (j + 1) * 128] = acc
+    parts = [small_ref[...]] + [got[:, 128:256] for got in (got1, got2, got3)]
     acc = None
     for source in range(4):
         term = parts[0]
@@ -252,7 +276,12 @@
         acc = term if acc is None else acc + term
     row = lax.broadcasted_iota(jnp.int32, acc.shape, 0)
     acc = jnp.where(row == ROW_LOSS, loss_ref[0:1, :], acc)
-    copies_ref[...] = jnp.broadcast_to(acc[None], copies_ref.shape)
+    high = acc.astype(BF16)
+    low = (acc - high.astype(F32)).astype(BF16)
+    count = copies_ref.shape[0]
+    copies_ref[:, 0:16, :] = jnp.broadcast_to(high[None], (count, 16, 128))
+    copies_ref[:, 16:32, :] = jnp.broadcast_to(low[None], (count, 16, 128))
+    copies_ref[:, 32:48, :] = second_ref[...]
 
 
 def final_kernel(
@@ -269,13 +298,20 @@
         copy.start()
         stores.append(copy)
 
-    in_ref[...] = grad_ref[...] * scale
+    first = grad_ref.shape[1]
+    in_ref[:, 0:first] = grad_ref[...] * scale
+    second = jnp.sum(mine[:, 32:48, :].astype(F32), axis=0) * scale
+    for j in range(4):
+        start = first + 128 * j
+        in_ref[:, start : start + 128] = second[4 * j : 4 * j + 4, :]
     store(in_ref, in_hbm)
     for which, blocks in ((core, mine), (1 - core, theirs)):
         for part in range(4):
             start = pl.multiple_of((2 * part + which) * 16, 16)
             for j in range(8):
-                full[pl.ds(start, 16), j * 128 : (j + 1) * 128] = blocks[part * 8 + j]
+                block = blocks[part * 8 + j, 0:16, :].astype(F32)
+                block = block + blocks[part * 8 + j, 16:32, :].astype(F32)
+                full[pl.ds(start, 16), j * 128 : (j + 1) * 128] = block
     for q in range(8):
         count = min(PER_BLOCK, n_vars - PER_BLOCK * q)
         out_ref[PER_BLOCK * q : PER_BLOCK * q + count, :] = full[16 * q : 16 * q + count, :] * scale
@@ -399,7 +435,8 @@
 
     swap = [(0, 1), (1, 0)]
     got = lax.ppermute(send, "core", swap)
-    payload_shape = (n_plane, block, hid + 128)
+    first = hid // 2
+    payload_shape = (n_plane, block, first + 128)
     payload = pl.pallas_call(
         payload_kernel,
         in_specs=[whole] * 2,
@@ -409,8 +446,25 @@
         compiler_params=PARAMS,
         name="payload",
     )(keep, got)
-    payload, val2, val1, val3 = lax.optimization_barrier((payload, val2, val1, val3))
+    payload, keep, got, val2, val1, val3 = lax.optimization_barrier(
+        (payload, keep, got, val2, val1, val3)
+    )
     landed = lax.all_to_all(payload, PLANE, 0, 0, tiled=True)
+
+    n_rows = n_plane * block // 4
+    quarter = shape((n_rows, first), BF16)
+    own_second, second2, second1, second3 = pl.pallas_call(
+        second_half_kernel,
+        in_specs=[SMEM, whole, whole],
+        out_specs=[whole] * 4,
+        out_shape=[shape((n_rows, first), F32), quarter, quarter, quarter],
+        scratch_shapes=[pltpu.VMEM((4, n_rows, first), F32)],
+        compiler_params=PARAMS,
+        name="second_half",
+    )(ids, keep, got)
+    second2 = lax.ppermute(second2, "zhi", shift("zhi", 2))
+    second1 = lax.ppermute(second1, "zhi", shift("zhi", 1))
+    second3 = lax.ppermute(second3, "zhi", shift("zhi", 3))
     val2 = lax.ppermute(val2, "y", pairs_of("y", 2))
     val1 = lax.ppermute(val1, "y", pairs_of("y", 1))
     val3 = lax.ppermute(val3, "y", pairs_of("y", 3))
@@ -422,13 +476,22 @@
         compiler_params=PARAMS,
         name="loss",
     )(val0, val2, val1, val3, truth, weight)
-
-    part = shape((block, 384), F32)
+    second = pl.pallas_call(
+        second_total_kernel,
+        in_specs=[whole] * 4,
+        out_specs=whole,
+        out_shape=shape((n_plane, block, 128), BF16),
+        scratch_shapes=[pltpu.VMEM((n_rows, first), F32), pltpu.VMEM((n_plane, block, 128), F32)],
+        compiler_params=PARAMS,
+        name="second_total",
+    )(own_second, second2, second1, second3)
+
+    part = shape((block, 256), F32)
     own, small, part2, part1, part3 = pl.pallas_call(
         plane_kernel,
         in_specs=[SMEM, whole],
         out_specs=[whole] * 5,
-        out_shape=[shape((block // 4, hid), F32), shape((block, 128), F32), part, part, part],
+        out_shape=[shape((block // 4, first), F32), shape((block, 128), F32), part, part, part],
         compiler_params=PARAMS,
         name="plane_sum",
     )(ids, landed)
@@ -437,12 +500,12 @@
     part3 = lax.ppermute(part3, "zhi", shift("zhi", 3))
     grad_in, copies = pl.pallas_call(
         total_kernel,
-        in_specs=[SMEM] + [whole] * 6,
+        in_specs=[SMEM] + [whole] * 7,
         out_specs=[whole] * 2,
-        out_shape=[shape((block // 4, hid), F32), shape((n_plane, block, 128), F32)],
+        out_shape=[shape((block // 4, first), F32), shape((n_plane, 3 * block, 128), BF16)],
         compiler_params=PARAMS,
         name="total",
-    )(ids, own, small, part2, part1, part3, part_loss)
+    )(ids, own, small, part2, part1, part3, part_loss, second)
 
     mine = lax.all_to_all(copies, PLANE, 0, 0, tiled=True)
     theirs = lax.ppermute(mine, "core", swap)

time: 82.1 us -> 87.9 us (1.071)
  waiting for transfers between devices: 17.8 us -> 5.77 us
  starting transfers between devices: 32 us -> 39.7 us
  local copies, waits for them, and re-layouts: 0.01 us -> 5.48 us
  Pallas kernels: 17.5 us -> 20 us
  blocking collectives: 13.5 us -> 15.4 us
    all_to_all x1, waiting for transfers between devices: 13.4 us -> 0.01 us  [per_device(): landed = lax.all_to_all(payload, PLANE, 0, 0, tiled=True)]
    ppermute x0 -> x3, starting transfers between devices: none -> 9.59 us  [the longest x1 6.01 us: per_device(): second2 = lax.ppermute(second2, 'zhi', shift('zhi', 2))]
    unnamed x2 -> x20, local copies, waits for them, and re-layouts: 0.01 us -> 5.48 us
    ppermute x1, starting transfers between devices: 6.1 us -> 1.42 us  [per_device(): part2 = lax.ppermute(part2, 'zhi', shift('zhi', 2))]
    ppermute x1, waiting for transfers between devices: 0.01 us -> 1.92 us  [per_device(): val2 = lax.ppermute(val2, 'y', pairs_of('y', 2))]
    all_to_all x1, blocking collectives: 13.5 us -> 15.4 us  [per_device(): mine = lax.all_to_all(copies, PLANE, 0, 0, tiled=True)]
    ppermute x1, starting transfers between devices: 0.57 us -> 2.42 us  [per_device(): val3 = lax.ppermute(val3, 'y', pairs_of('y', 3))]
    pallas_call x1 -> x3, Pallas kernels: 0.58 us -> 2.23 us  [the longest x1 1.52 us: per_device(): pl.pallas_call(second_half_kernel, in_specs=[SMEM, whole, whole], out_spe...]
  transfers between devices with their start and end apart: 12 -> 15, of which waited for: 5 -> 3; matrix products, arithmetic and copies ran while one was open for 0% -> 0% of each run, Pallas kernels for 9% -> 11%
where the time goes in v5:
time: 87.9 us; the launch traced here: 87.4 us
  starting transfers between devices  39.7 us (45%)
  Pallas kernels  20 us (23%)
  blocking collectives  15.4 us (18%)
  waiting for transfers between devices  5.77 us (7%)
  local copies, waits for them, and re-layouts  5.48 us (6%)
  between operations  0.98 us (1%)
    all_to_all x1, blocking collectives, per_device(): mine = lax.all_to_all(copies, PLANE, 0, 0, tiled=True)  15.4 us
    all_to_all x1, starting transfers between devices, per_device(): landed = lax.all_to_all(payload, PLANE, 0, 0, tiled=True)  6.77 us
    pallas_call x1, Pallas kernels, per_device(): pl.pallas_call(forward_kernel, grid=(hid // cols,), in_specs=[SMEM, const...  6.26 us
    ppermute x1, starting transfers between devices, per_device(): second2 = lax.ppermute(second2, 'zhi', shift('zhi', 2))  6.01 us
    unnamed x20, local copies, waits for them, and re-layouts  5.48 us
    ppermute x1, starting transfers between devices, per_device(): theirs = lax.ppermute(mine, 'core', swap)  5.47 us
    pallas_call x1, Pallas kernels, per_device(): pl.pallas_call(backward_kernel, in_specs=[SMEM] + [whole] * 9, out_specs=...  4.07 us
    ppermute x1, starting transfers between devices, per_device(): cot2 = lax.ppermute(cot2, 'y', pairs_of('y', 2))  3.74 us
  transfers between devices with their start and end apart: 15, of which 3 were waited for; matrix products, arithmetic and copies ran while one was open for 0% of the time, Pallas kernels for 11%

profile of v5, /device:TPU:1, one launch (start us, length us, event | category | flops | bytes accessed | tf_op | source)
XLA Modules:
  0.0 87.4 jit_solution(10069750189920787005)
XLA Ops:
  0.7 3.1 %cotangent.1 = (f32[64,100]{1,0:T(8,128)S(1)}, f32[1,100]{1,0:T(1,128)S(1)}, bf16[4,64,100]{2,1,0:T(8,128)(2,1)S(1)}, bf16[4,64,100]{2,1,0:T(8,128)(2,1)S(1)}, b...) custom-call(s32[3]{0:T(128)S(1)} %pad_add_fusion.ids.refs_0_, ...), custom_call_target="tpu_custom_call" | custom-call | tf_op jit(solution)/shard_map/cotangent/pallas_call | solution.py:368
  4.5 3.7 %collective-permute-start = (bf16[4,64,100]{2,1,0:T(8,128)(2,1)S(1)}, bf16[4,64,100]{2,1,0:T(8,128)(2,1)S(1)}, u32[]{:S(2)}, u32[]{:S(2)}) collective-permute-start(bf16[4,64,100]{2,1,0:T(8,128)(2,1)S(1)} %get-tuple-element.54), channel_id=1, source_target_pairs={{0,128},{64,192},{128,0},{192,64},{1,129},{65,193},{129,1},{193,65... | collective-permute-start | bytes 153608 | tf_op jit(solution)/shard_map/ppermute | solution.py:393
  9.0 6.3 %forward.1 = (bf16[1024,1024]{1,0:T(8,128)(2,1)S(1)}, f32[1024,1024]{1,0:T(8,128)S(1)}, bf16[4,64,100]{2,1,0:T(8,128)(2,1)S(1)}, bf16[4,64,100]{2,1,0:T(8,128)(2...) custom-call(s32[3]{0:T(128)S(1)} %pad_add_fusion.ids.refs_0_, ...), custom_call_target="tpu_custom_call" | custom-call | tf_op jit(solution)/shard_map/forward/pallas_call | solution.py:399
  15.3 4.1 %backward.1 = (f32[32,16,1152]{2,1,0:T(8,128)S(1)}, bf16[32,16,1152]{2,1,0:T(8,128)(2,1)S(1)}) custom-call(s32[3]{0:T(128)S(1)} %pad_add_fusion.ids.refs_0_, bf16[4,64,100]{2,1,0:T(8,128)(2,1)S(1)} %get-tuple-element.50.got0, bf16[4,64,100]{2,1,0:T(8,128)(2,1)S(1)} %collective-permute-done.got2, bf16[4,64,100]{2,1,0:T(8,128)(2,1)S(1)} %collective-permute-done.1.got1, ...), custom_call_target="tpu_custom_call" | custom-call | tf_op jit(solution)/shard_map/backward/pallas_call | solution.py:419
  19.4 2.9 %collective-permute-start.3 = (bf16[32,16,1152]{2,1,0:T(8,128)(2,1)S(1)}, bf16[32,16,1152]{2,1,0:T(8,128)(2,1)S(1)}, u32[]{:S(2)}, u32[]{:S(2)}) collective-permute-start(bf16[32,16,1152]{2,1,0:T(8,128)(2,1)S(1)} %get-tuple-element.67), channel_id=1, source_target_pairs={{0,4},{4,0},{1,5},{5,1},{2,6},{6,2},{3,7},{7,3},{8,12},{12,8},{9,1... | collective-permute-start | bytes 3538952 | tf_op jit(solution)/shard_map/ppermute | solution.py:437
  22.3 2.5 %collective-permute-done.3.got_ref = bf16[32,16,1152]{2,1,0:T(8,128)(2,1)S(1)} collective-permute-done((bf16[32,16,1152]{2,1,0:T(8,128)(2,1)S(1)}, bf16[32,16,1152]{2,1,0:T(8,128)(2,1)S(1)}, u32[]{:S(2)}, u32[]{:S(2)}) %collective-permute-start.3) | collective-permute-done | bytes 1179680 | tf_op jit(solution)/shard_map/ppermute | solution.py:437
  24.7 1.1 %payload.1 = bf16[32,16,640]{2,1,0:T(8,128)(2,1)S(1)} custom-call(f32[32,16,1152]{2,1,0:T(8,128)S(1)} %get-tuple-element.82.keep_ref, bf16[32,16,1152]{2,1,0:T(8,128)(2,1)S(1)} %collective-permute-done.3.got_ref), custom_call_target="tpu_custom_call" | custom-call | tf_op jit(solution)/shard_map/payload/pallas_call | solution.py:440
  26.7 6.8 %all-to-all-start = ((bf16[32,16,640]{2,1,0:T(8,128)(2,1)}), bf16[32,16,640]{2,1,0:T(8,128)(2,1)}, u32[]{:S(2)}, u32[]{:S(2)}) async-start(bf16[32,16,640]{2,1,0:T(8,128)(2,1)} %copy-done), calls=%async_computation | async-start | bytes 1310720 | tf_op jit(solution)/shard_map/all_to_all | solution.py:452
  33.5 1.5 %second_half.1 = (f32[128,512]{1,0:T(8,128)S(1)}, bf16[128,512]{1,0:T(8,128)(2,1)}, bf16[128,512]{1,0:T(8,128)(2,1)}, bf16[128,512]{1,0:T(8,128)(2,1)}) custom-call(s32[3]{0:T(128)S(1)} %pad_add_fusion.ids.refs_0_, f32[32,16,1152]{2,1,0:T(8,128)S(1)} %get-tuple-element.82.keep_ref, bf16[32,16,1152]{2,1,0:T(8,128)(2,1)S(1)} %collective-permute-done.3.got_ref), custom_call_target="tpu_custom_call" | custom-call | tf_op jit(solution)/shard_map/second_half/pallas_call | solution.py:456
  35.7 6.0 %collective-permute-start.10 = (bf16[128,512]{1,0:T(8,128)(2,1)}, bf16[128,512]{1,0:T(8,128)(2,1)S(1)}, u32[]{:S(2)}, u32[]{:S(2)}) collective-permute-start(bf16[128,512]{1,0:T(8,128)(2,1)} %get-tuple-element.85), channel_id=1, source_target_pairs={{0,2},{1,3},{2,0},{3,1},{4,6},{5,7},{6,4},{7,5},{8,10},{9,11},{10,... | collective-permute-start | bytes 393224 | tf_op jit(solution)/shard_map/ppermute | solution.py:465
  41.7 1.2 %collective-permute-start.11 = (bf16[128,512]{1,0:T(8,128)(2,1)}, bf16[128,512]{1,0:T(8,128)(2,1)S(1)}, u32[]{:S(2)}, u32[]{:S(2)}) collective-permute-start(bf16[128,512]{1,0:T(8,128)(2,1)} %get-tuple-element.86), channel_id=1, source_target_pairs={{0,1},{1,2},{2,3},{3,0},{4,5},{5,6},{6,7},{7,4},{8,9},{9,10},{10,1... | collective-permute-start | bytes 393224 | tf_op jit(solution)/shard_map/ppermute | solution.py:466
  42.9 2.4 %collective-permute-start.12 = (bf16[128,512]{1,0:T(8,128)(2,1)}, bf16[128,512]{1,0:T(8,128)(2,1)S(1)}, u32[]{:S(2)}, u32[]{:S(2)}) collective-permute-start(bf16[128,512]{1,0:T(8,128)(2,1)} %get-tuple-element.87), channel_id=1, source_target_pairs={{0,3},{1,0},{2,1},{3,2},{4,7},{5,4},{6,5},{7,6},{8,11},{9,8},{10,9... | collective-permute-start | bytes 393224 | tf_op jit(solution)/shard_map/ppermute | solution.py:467
  45.3 2.7 %collective-permute-start.7 = (bf16[4,64,100]{2,1,0:T(8,128)(2,1)S(1)}, bf16[4,64,100]{2,1,0:T(8,128)(2,1)S(1)}, u32[]{:S(2)}, u32[]{:S(2)}) collective-permute-start(bf16[4,64,100]{2,1,0:T(8,128)(2,1)S(1)} %copy-done.9), channel_id=1, source_target_pairs={{0,128},{64,192},{128,0},{192,64},{1,129},{65,193},{129,1},{193,65... | collective-permute-start | bytes 153608 | tf_op jit(solution)/shard_map/ppermute | solution.py:468
  48.3 1.9 %collective-permute-done.7.got2 = bf16[4,64,100]{2,1,0:T(8,128)(2,1)S(1)} collective-permute-done((bf16[4,64,100]{2,1,0:T(8,128)(2,1)S(1)}, bf16[4,64,100]{2,1,0:T(8,128)(2,1)S(1)}, u32[]{:S(2)}, u32[]{:S(2)}) %collective-permute-start.7) | collective-permute-done | bytes 51232 | tf_op jit(solution)/shard_map/ppermute | solution.py:468
  50.2 2.4 %collective-permute-start.9 = (bf16[4,64,100]{2,1,0:T(8,128)(2,1)}, bf16[4,64,100]{2,1,0:T(8,128)(2,1)S(1)}, u32[]{:S(2)}, u32[]{:S(2)}) collective-permute-start(bf16[4,64,100]{2,1,0:T(8,128)(2,1)} %get-tuple-element.80), channel_id=1, source_target_pairs={{0,192},{64,128},{128,64},{192,0},{1,193},{65,129},{129,65},{193,1... | collective-permute-start | bytes 153608 | tf_op jit(solution)/shard_map/ppermute | solution.py:470
  52.6 1.2 %plane_sum.1 = (f32[4,512]{1,0:T(4,128)S(1)}, f32[16,128]{1,0:T(8,128)S(1)}, f32[16,256]{1,0:T(8,128)S(1)}, f32[16,256]{1,0:T(8,128)S(1)}, f32[16,256]{1,0:T(8,128)S(1)}) custom-call(s32[3]{0:T(128)S(1)} %pad_add_fusion.ids.refs_0_, bf16[32,16,640]{2,1,0:T(8,128)(2,1)} %all-to-all-done.landed_ref), custom_call_target="tpu_custom_call" | custom-call | tf_op jit(solution)/shard_map/plane_sum/pallas_call | solution.py:490
  53.9 1.4 %collective-permute-start.4 = (f32[16,256]{1,0:T(8,128)S(1)}, f32[16,256]{1,0:T(8,128)S(1)}, u32[]{:S(2)}, u32[]{:S(2)}) collective-permute-start(f32[16,256]{1,0:T(8,128)S(1)} %get-tuple-element.74), channel_id=1, source_target_pairs={{0,2},{1,3},{2,0},{3,1},{4,6},{5,7},{6,4},{7,5},{8,10},{9,11},{10,... | collective-permute-start | bytes 49160 | tf_op jit(solution)/shard_map/ppermute | solution.py:498
  55.3 1.1 %collective-permute-start.5 = (f32[16,256]{1,0:T(8,128)S(1)}, f32[16,256]{1,0:T(8,128)S(1)}, u32[]{:S(2)}, u32[]{:S(2)}) collective-permute-start(f32[16,256]{1,0:T(8,128)S(1)} %get-tuple-element.75), channel_id=1, source_target_pairs={{0,1},{1,2},{2,3},{3,0},{4,5},{5,6},{6,7},{7,4},{8,9},{9,10},{10,1... | collective-permute-start | bytes 49160 | tf_op jit(solution)/shard_map/ppermute | solution.py:499
  56.4 2.5 %collective-permute-start.6 = (f32[16,256]{1,0:T(8,128)S(1)}, f32[16,256]{1,0:T(8,128)S(1)}, u32[]{:S(2)}, u32[]{:S(2)}) collective-permute-start(f32[16,256]{1,0:T(8,128)S(1)} %get-tuple-element.76), channel_id=1, source_target_pairs={{0,3},{1,0},{2,1},{3,2},{4,7},{5,4},{6,5},{7,6},{8,11},{9,8},{10,9... | collective-permute-start | bytes 49160 | tf_op jit(solution)/shard_map/ppermute | solution.py:500
  61.9 0.9 %copy-done.2 = f32[128,512]{1,0:T(8,128)S(1)} copy-done((f32[128,512]{1,0:T(8,128)S(1)}, f32[128,512]{1,0:T(8,128)}, u32[]{:S(2)}) %copy-start.2) | copy-done | bytes 262168
  63.6 15.4 %all_to_all.10.refs_2_ = bf16[32,48,128]{2,1,0:T(8,128)(2,1)S(1)} all-to-all(bf16[32,48,128]{2,1,0:T(8,128)(2,1)S(1)} %get-tuple-element.89), channel_id=1, replica_groups=mesh['y'=4,'zlo'=2,'x'=4,'core'=2,'zhi'=4] {'y','zlo','x'}, dimensions={0} | all-to-all | bytes 786432 | tf_op jit(solution)/shard_map/all_to_all | solution.py:510
  79.0 5.5 %collective-permute-start.13 = (bf16[32,48,128]{2,1,0:T(8,128)(2,1)S(1)}, bf16[32,48,128]{2,1,0:T(8,128)(2,1)S(1)}, u32[]{:S(2)}, u32[]{:S(2)}) collective-permute-start(bf16[32,48,128]{2,1,0:T(8,128)(2,1)S(1)} %all_to_all.10.refs_2_), channel_id=1, source_target_pairs={{0,4},{4,0},{1,5},{5,1},{2,6},{6,2},{3,7},{7,3},{8,12},{12,8},{9,1... | collective-permute-start | bytes 1179656 | tf_op jit(solution)/shard_map/ppermute | solution.py:511
  84.4 1.3 %collective-permute-done.13.refs_3_ = bf16[32,48,128]{2,1,0:T(8,128)(2,1)S(1)} collective-permute-done((bf16[32,48,128]{2,1,0:T(8,128)(2,1)S(1)}, bf16[32,48,128]{2,1,0:T(8,128)(2,1)S(1)}, u32[]{:S(2)}, u32[]{:S(2)}) %collective-permute-start.13) | collective-permute-done | bytes 393248 | tf_op jit(solution)/shard_map/ppermute | solution.py:511
  85.8 1.5 %unpack.1 = (f32[4,1024]{1,0:T(4,128)}, f32[100,1024]{1,0:T(8,128)}, f32[1,1024]{1,0:T(1,128)}, f32[1,100]{1,0:T(1,128)}, f32[1,1]{1,0:T(1,128)}) custom-call(s32[3]{0:T(128)S(1)} %pad_add_fusion.ids.refs_0_, f32[4,512]{1,0:T(4,128)S(1)} %get-tuple-element.88.refs_1_, bf16[32,48,128]{2,1,0:T(8,128)(2,1)S(1)} %all_to_all.10.refs_2_, ...), custom_call_target="tpu_custom_call" | custom-call | tf_op jit(solution)/shard_map/unpack/pallas_call | solution.py:519
  (38 shorter events, 7.0 us)
Async XLA Ops:
  4.5 10.8 %collective-permute-start = (bf16[4,64,100]{2,1,0:T(8,128)(2,1)S(1)}, bf16[4,64,100]{2,1,0:T(8,128)(2,1)S(1)}, u32[]{:S(2)}, u32[]{:S(2)}) collective-permute-start(bf16[4,64,100]{2,1,0:T(8,128)(2,1)S(1)} %get-tuple-element.54), channel_id=1, source_target_pairs={{0,128},{64,192},{128,0},{192,64},{1,129},{65,193},{129,1},{193,65... | collective-permute-start | bytes 153608 | tf_op jit(solution)/shard_map/ppermute | solution.py:393
  8.2 7.1 %collective-permute-start.1 = (bf16[4,64,100]{2,1,0:T(8,128)(2,1)S(1)}, bf16[4,64,100]{2,1,0:T(8,128)(2,1)S(1)}, u32[]{:S(2)}, u32[]{:S(2)}) collective-permute-start(bf16[4,64,100]{2,1,0:T(8,128)(2,1)S(1)} %get-tuple-element.55), channel_id=1, source_target_pairs={{0,64},{64,0},{128,192},{192,128},{1,65},{65,1},{129,193},{193,129... | collective-permute-start | bytes 153608 | tf_op jit(solution)/shard_map/ppermute | solution.py:394
  8.6 6.7 %collective-permute-start.2 = (bf16[4,64,100]{2,1,0:T(8,128)(2,1)S(1)}, bf16[4,64,100]{2,1,0:T(8,128)(2,1)S(1)}, u32[]{:S(2)}, u32[]{:S(2)}) collective-permute-start(bf16[4,64,100]{2,1,0:T(8,128)(2,1)S(1)} %get-tuple-element.56), channel_id=1, source_target_pairs={{0,192},{64,128},{128,64},{192,0},{1,193},{65,129},{129,65},{193,1... | collective-permute-start | bytes 153608 | tf_op jit(solution)/shard_map/ppermute | solution.py:395
  15.2 4.1 %copy-start.3 = (bf16[4,64,100]{2,1,0:T(8,128)(2,1)}, bf16[4,64,100]{2,1,0:T(8,128)(2,1)S(1)}, u32[]{:S(2)}) copy-start(bf16[4,64,100]{2,1,0:T(8,128)(2,1)S(1)} %get-tuple-element.77.got0) | copy-start | bytes 153604
  15.2 4.1 %copy-start.8 = (bf16[4,64,100]{2,1,0:T(8,128)(2,1)}, bf16[4,64,100]{2,1,0:T(8,128)(2,1)S(1)}, u32[]{:S(2)}) copy-start(bf16[4,64,100]{2,1,0:T(8,128)(2,1)S(1)} %get-tuple-element.78) | copy-start | bytes 153604
  19.4 5.4 %collective-permute-start.3 = (bf16[32,16,1152]{2,1,0:T(8,128)(2,1)S(1)}, bf16[32,16,1152]{2,1,0:T(8,128)(2,1)S(1)}, u32[]{:S(2)}, u32[]{:S(2)}) collective-permute-start(bf16[32,16,1152]{2,1,0:T(8,128)(2,1)S(1)} %get-tuple-element.67), channel_id=1, source_target_pairs={{0,4},{4,0},{1,5},{5,1},{2,6},{6,2},{3,7},{7,3},{8,12},{12,8},{9,1... | collective-permute-start | bytes 3538952 | tf_op jit(solution)/shard_map/ppermute | solution.py:437
  25.8 0.9 %copy-start = (bf16[32,16,640]{2,1,0:T(8,128)(2,1)}, bf16[32,16,640]{2,1,0:T(8,128)(2,1)S(1)}, u32[]{:S(2)}) copy-start(bf16[32,16,640]{2,1,0:T(8,128)(2,1)S(1)} %payload.1) | copy-start | bytes 1966084
  26.7 25.9 %all-to-all-start = ((bf16[32,16,640]{2,1,0:T(8,128)(2,1)}), bf16[32,16,640]{2,1,0:T(8,128)(2,1)}, u32[]{:S(2)}, u32[]{:S(2)}) async-start(bf16[32,16,640]{2,1,0:T(8,128)(2,1)} %copy-done), calls=%async_computation | async-start | bytes 1310720 | tf_op jit(solution)/shard_map/all_to_all | solution.py:452
  33.5 11.8 %copy-start.9 = (bf16[4,64,100]{2,1,0:T(8,128)(2,1)S(1)}, bf16[4,64,100]{2,1,0:T(8,128)(2,1)}, u32[]{:S(2)}) copy-start(bf16[4,64,100]{2,1,0:T(8,128)(2,1)} %copy-done.8) | copy-start | bytes 153604
  35.0 0.7 copy-start.1
  35.7 20.7 %collective-permute-start.10 = (bf16[128,512]{1,0:T(8,128)(2,1)}, bf16[128,512]{1,0:T(8,128)(2,1)S(1)}, u32[]{:S(2)}, u32[]{:S(2)}) collective-permute-start(bf16[128,512]{1,0:T(8,128)(2,1)} %get-tuple-element.85), channel_id=1, source_target_pairs={{0,2},{1,3},{2,0},{3,1},{4,6},{5,7},{6,4},{7,5},{8,10},{9,11},{10,... | collective-permute-start | bytes 393224 | tf_op jit(solution)/shard_map/ppermute | solution.py:465
  41.7 20.1 %collective-permute-start.11 = (bf16[128,512]{1,0:T(8,128)(2,1)}, bf16[128,512]{1,0:T(8,128)(2,1)S(1)}, u32[]{:S(2)}, u32[]{:S(2)}) collective-permute-start(bf16[128,512]{1,0:T(8,128)(2,1)} %get-tuple-element.86), channel_id=1, source_target_pairs={{0,1},{1,2},{2,3},{3,0},{4,5},{5,6},{6,7},{7,4},{8,9},{9,10},{10,1... | collective-permute-start | bytes 393224 | tf_op jit(solution)/shard_map/ppermute | solution.py:466
  42.9 18.9 %collective-permute-start.12 = (bf16[128,512]{1,0:T(8,128)(2,1)}, bf16[128,512]{1,0:T(8,128)(2,1)S(1)}, u32[]{:S(2)}, u32[]{:S(2)}) collective-permute-start(bf16[128,512]{1,0:T(8,128)(2,1)} %get-tuple-element.87), channel_id=1, source_target_pairs={{0,3},{1,0},{2,1},{3,2},{4,7},{5,4},{6,5},{7,6},{8,11},{9,8},{10,9... | collective-permute-start | bytes 393224 | tf_op jit(solution)/shard_map/ppermute | solution.py:467
  45.3 4.9 %collective-permute-start.7 = (bf16[4,64,100]{2,1,0:T(8,128)(2,1)S(1)}, bf16[4,64,100]{2,1,0:T(8,128)(2,1)S(1)}, u32[]{:S(2)}, u32[]{:S(2)}) collective-permute-start(bf16[4,64,100]{2,1,0:T(8,128)(2,1)S(1)} %copy-done.9), channel_id=1, source_target_pairs={{0,128},{64,192},{128,0},{192,64},{1,129},{65,193},{129,1},{193,65... | collective-permute-start | bytes 153608 | tf_op jit(solution)/shard_map/ppermute | solution.py:468
  48.0 5.9 %collective-permute-start.8 = (bf16[4,64,100]{2,1,0:T(8,128)(2,1)}, bf16[4,64,100]{2,1,0:T(8,128)(2,1)S(1)}, u32[]{:S(2)}, u32[]{:S(2)}) collective-permute-start(bf16[4,64,100]{2,1,0:T(8,128)(2,1)} %get-tuple-element.79), channel_id=1, source_target_pairs={{0,64},{64,0},{128,192},{192,128},{1,65},{65,1},{129,193},{193,129... | collective-permute-start | bytes 153608 | tf_op jit(solution)/shard_map/ppermute | solution.py:469
  50.2 5.1 %collective-permute-start.9 = (bf16[4,64,100]{2,1,0:T(8,128)(2,1)}, bf16[4,64,100]{2,1,0:T(8,128)(2,1)S(1)}, u32[]{:S(2)}, u32[]{:S(2)}) collective-permute-start(bf16[4,64,100]{2,1,0:T(8,128)(2,1)} %get-tuple-element.80), channel_id=1, source_target_pairs={{0,192},{64,128},{128,64},{192,0},{1,193},{65,129},{129,65},{193,1... | collective-permute-start | bytes 153608 | tf_op jit(solution)/shard_map/ppermute | solution.py:470
  53.9 9.1 %collective-permute-start.4 = (f32[16,256]{1,0:T(8,128)S(1)}, f32[16,256]{1,0:T(8,128)S(1)}, u32[]{:S(2)}, u32[]{:S(2)}) collective-permute-start(f32[16,256]{1,0:T(8,128)S(1)} %get-tuple-element.74), channel_id=1, source_target_pairs={{0,2},{1,3},{2,0},{3,1},{4,6},{5,7},{6,4},{7,5},{8,10},{9,11},{10,... | collective-permute-start | bytes 49160 | tf_op jit(solution)/shard_map/ppermute | solution.py:498
  55.3 7.6 %collective-permute-start.5 = (f32[16,256]{1,0:T(8,128)S(1)}, f32[16,256]{1,0:T(8,128)S(1)}, u32[]{:S(2)}, u32[]{:S(2)}) collective-permute-start(f32[16,256]{1,0:T(8,128)S(1)} %get-tuple-element.75), channel_id=1, source_target_pairs={{0,1},{1,2},{2,3},{3,0},{4,5},{5,6},{6,7},{7,4},{8,9},{9,10},{10,1... | collective-permute-start | bytes 49160 | tf_op jit(solution)/shard_map/ppermute | solution.py:499
  56.4 6.6 %collective-permute-start.6 = (f32[16,256]{1,0:T(8,128)S(1)}, f32[16,256]{1,0:T(8,128)S(1)}, u32[]{:S(2)}, u32[]{:S(2)}) collective-permute-start(f32[16,256]{1,0:T(8,128)S(1)} %get-tuple-element.76), channel_id=1, source_target_pairs={{0,3},{1,0},{2,1},{3,2},{4,7},{5,4},{6,5},{7,6},{8,11},{9,8},{10,9... | collective-permute-start | bytes 49160 | tf_op jit(solution)/shard_map/ppermute | solution.py:500
  58.9 0.8 copy-start.4
  59.7 0.8 copy-start.5
  60.5 0.8 copy-start.7
  61.9 1.0 %copy-start.2 = (f32[128,512]{1,0:T(8,128)S(1)}, f32[128,512]{1,0:T(8,128)}, u32[]{:S(2)}) copy-start(f32[128,512]{1,0:T(8,128)} %copy-done.1) | copy-start | bytes 786436
  79.0 6.8 %collective-permute-start.13 = (bf16[32,48,128]{2,1,0:T(8,128)(2,1)S(1)}, bf16[32,48,128]{2,1,0:T(8,128)(2,1)S(1)}, u32[]{:S(2)}, u32[]{:S(2)}) collective-permute-start(bf16[32,48,128]{2,1,0:T(8,128)(2,1)S(1)} %all_to_all.10.refs_2_), channel_id=1, source_target_pairs={{0,4},{4,0},{1,5},{5,1},{2,6},{6,2},{3,7},{7,3},{8,12},{12,8},{9,1... | collective-permute-start | bytes 1179656 | tf_op jit(solution)/shard_map/ppermute | solution.py:511
  (1 other events, 0.6 us)

commit v6 on v4

--- a/solution.py
+++ b/solution.py
@@ -57,7 +57,8 @@
     pairs = [(rank_hbm, rank_ref), (obs_hbm, obs_ref), (area_hbm, area_ref), (vw_hbm, vw_ref)]
     needed = len(pairs)
     pairs += [(w_out_hbm, w_out_ref), (b_in_hbm, b_in_ref), (b_out_hbm, b_out_ref)]
-    for source, target in ((x_hbm, x_ref), (w_in_hbm, w_in_ref)):
+    first = w_in_hbm.at[:, 0 : w_in_ref.shape[1]]
+    for source, target in ((x_hbm, x_ref), (first, w_in_ref)):
         piece = source.shape[0] // 4
         for i in range(4):
             rows = pl.ds(i * piece, piece)
@@ -95,31 +96,37 @@
 
 
 def forward_kernel(
-    ids, x_ref, w_in_ref, b_in_ref, w_out_ref, b_out_ref,
-    hidden_ref, slope_ref, send0, send2, send1, send3, values,
+    ids, x_ref, w_first, w_in_hbm, b_in_ref, w_out_ref, b_out_ref,
+    hidden_ref, slope_ref, send0, send2, send1, send3, values, w_ref, sem,
 ):
     step = pl.program_id(0)
     mem_dev, sub, _ = send0.shape
-    pre = jnp.dot(x_ref[...], w_in_ref[...], preferred_element_type=F32) + b_in_ref[...]
-    square = pre * pre
-    t = jnp.tanh(pre * (GELU_C + (GELU_C * GELU_A) * square))
-    half = 0.5 + 0.5 * t
-    hidden = (pre * half).astype(BF16)
-    hidden_ref[...] = hidden
-    slope_ref[...] = half + pre * (0.5 - 0.5 * (t * t)) * (
-        GELU_C + (3.0 * GELU_A * GELU_C) * square
-    )
-    part = lax.dot_general(
-        hidden, w_out_ref[...], (((1,), (1,)), ((), ())), preferred_element_type=F32
-    )
+    cols = w_first.shape[1]
+    fetch = pltpu.make_async_copy(w_in_hbm.at[:, cols : 2 * cols], w_ref, sem)
+
+    def half(weights):
+        pre = jnp.dot(x_ref[...], weights[...], preferred_element_type=F32) + b_in_ref[...]
+        square = pre * pre
+        t = jnp.tanh(pre * (GELU_C + (GELU_C * GELU_A) * square))
+        upper = 0.5 + 0.5 * t
+        hidden = (pre * upper).astype(BF16)
+        hidden_ref[...] = hidden
+        slope_ref[...] = upper + pre * (0.5 - 0.5 * (t * t)) * (
+            GELU_C + (3.0 * GELU_A * GELU_C) * square
+        )
+        return lax.dot_general(
+            hidden, w_out_ref[...], (((1,), (1,)), ((), ())), preferred_element_type=F32
+        )
 
     @pl.when(step == 0)
     def _():
-        values[...] = part + b_out_ref[...]
-
-    @pl.when(step > 0)
+        fetch.start()
+        values[...] = half(w_first) + b_out_ref[...]
+
+    @pl.when(step == 1)
     def _():
-        values[...] += part
+        fetch.wait()
+        values[...] += half(w_ref)
 
     @pl.when(step == pl.num_programs(0) - 1)
     def _():
@@ -183,15 +190,16 @@
         send_ref[:, :, cols] = jnp.where(core == 0, second, first).astype(BF16)
 
     small[ROW_BOUT : ROW_BOUT + 1, 0:n_vars] = bout_ref[...]
-    for part in range(4):
-        start = pl.multiple_of((2 * part + core) * 16, 16)
-        rows = small[pl.ds(start, 16), :]
-        for j in range(8):
-            keep_ref[part * 8 + j, :, hid:] = rows[:, j * 128 : (j + 1) * 128]
-        start = pl.multiple_of((2 * part + 1 - core) * 16, 16)
-        rows = unfold(small[pl.ds(start, 16), :]).astype(BF16)
-        for j in range(8):
-            send_ref[part * 8 + j, :, hid:] = rows[:, j * 128 : (j + 1) * 128]
+    half = hid // 2
+    mine = pl.ds(pl.multiple_of(core * half, half), half)
+    other = pl.ds(pl.multiple_of((1 - core) * half, half), half)
+    for q in range(8):
+        rows = small[16 * q : 16 * q + 16, mine]
+        for t in range(4):
+            keep_ref[4 * q + t, :, hid:] = rows[:, t * 128 : (t + 1) * 128]
+        rows = unfold(small[16 * q : 16 * q + 16, other]).astype(BF16)
+        for t in range(4):
+            send_ref[4 * q + t, :, hid:] = rows[:, t * 128 : (t + 1) * 128]
 
 
 def payload_kernel(keep_ref, got_ref, out_hbm, out_ref, sems):
@@ -255,43 +263,68 @@
     copies_ref[...] = jnp.broadcast_to(acc[None], copies_ref.shape)
 
 
-def final_kernel(
-    scale, loss_scale, ids, grad_ref, mine, theirs,
-    in_hbm, out_hbm, bin_hbm, bout_hbm, loss_hbm,
-    full, in_ref, out_ref, bin_ref, bout_ref, loss_ref, sems,
-):
-    core = ids[2]
+def small_half(blocks, full):
+    for q in range(8):
+        for t in range(4):
+            full[16 * q : 16 * q + 16, t * 128 : (t + 1) * 128] = blocks[4 * q + t]
+
+
+def plain_rows(full, out_ref, scale):
     n_vars = out_ref.shape[0]
-    stores = []
-
-    def store(source, target):
-        copy = pltpu.make_async_copy(source, target, sems.at[len(stores)])
-        copy.start()
-        stores.append(copy)
-
-    in_ref[...] = grad_ref[...] * scale
-    store(in_ref, in_hbm)
-    for which, blocks in ((core, mine), (1 - core, theirs)):
-        for part in range(4):
-            start = pl.multiple_of((2 * part + which) * 16, 16)
-            for j in range(8):
-                full[pl.ds(start, 16), j * 128 : (j + 1) * 128] = blocks[part * 8 + j]
     for q in range(8):
         count = min(PER_BLOCK, n_vars - PER_BLOCK * q)
         out_ref[PER_BLOCK * q : PER_BLOCK * q + count, :] = full[16 * q : 16 * q + count, :] * scale
-        if q == 3:
-            store(out_ref.at[0:48, :], out_hbm.at[0:48, :])
-    store(out_ref.at[48:n_vars, :], out_hbm.at[48:n_vars, :])
+
+
+def own_kernel(
+    scale, ids, grad_ref, mine, in_hbm, out_hbm, bin_hbm, full, in_ref, out_ref, bin_ref, sems
+):
+    half = full.shape[1]
+    cols = pl.ds(pl.multiple_of(ids[2] * half, half), half)
+    in_ref[...] = grad_ref[...] * scale
+    small_half(mine, full)
+    plain_rows(full, out_ref, scale)
     bin_ref[...] = full[ROW_BIN : ROW_BIN + 1, :] * scale
-    store(bin_ref, bin_hbm)
-    bout_ref[...] = full[ROW_BOUT : ROW_BOUT + 1, 0:n_vars] * scale
-    store(bout_ref, bout_hbm)
-    total = jnp.zeros((1, 128), F32)
-    for q in range(8):
-        for j in range(8):
-            total = total + full[16 * q + ROW_LOSS : 16 * q + ROW_LOSS + 1, 128 * j : 128 * (j + 1)]
-    loss_ref[...] = total[:, 0:1] * loss_scale
-    store(loss_ref, loss_hbm)
+    stores = [
+        pltpu.make_async_copy(out_ref, out_hbm.at[:, cols], sems.at[0]),
+        pltpu.make_async_copy(in_ref, in_hbm, sems.at[1]),
+        pltpu.make_async_copy(bin_ref, bin_hbm.at[:, cols], sems.at[2]),
+    ]
+    for copy in stores:
+        copy.start()
+    for copy in stores:
+        copy.wait()
+
+
+def other_kernel(
+    scale, loss_scale, ids, out_before, bin_before, mine, theirs,
+    out_hbm, bin_hbm, bout_hbm, loss_hbm, full, out_ref, bin_ref, bout_ref, loss_ref, sems,
+):
+    core = ids[2]
+    half = full.shape[1]
+    n_vars = out_ref.shape[0]
+    cols = pl.ds(pl.multiple_of((1 - core) * half, half), half)
+    small_half(theirs, full)
+    plain_rows(full, out_ref, scale)
+    bin_ref[...] = full[ROW_BIN : ROW_BIN + 1, :] * scale
+    row = ROW_BOUT - 112
+    here, there = mine[28, row : row + 1, :], theirs[28, row : row + 1, :]
+    bout_ref[...] = jnp.where(core == 0, here, there)[:, 0:n_vars] * scale
+    totals = []
+    for blocks in (mine, theirs):
+        total = jnp.zeros((1, 128), F32)
+        for n in range(blocks.shape[0]):
+            total = total + blocks[n, ROW_LOSS : ROW_LOSS + 1, :]
+        totals.append(total)
+    loss_ref[...] = (totals[0] + totals[1])[:, 0:1] * loss_scale
+    stores = [
+        pltpu.make_async_copy(out_ref, out_hbm.at[:, cols], sems.at[0]),
+        pltpu.make_async_copy(bin_ref, bin_hbm.at[:, cols], sems.at[1]),
+        pltpu.make_async_copy(bout_ref, bout_hbm, sems.at[2]),
+        pltpu.make_async_copy(loss_ref, loss_hbm, sems.at[3]),
+    ]
+    for copy in stores:
+        copy.start()
     for copy in stores:
         copy.wait()
 
@@ -329,7 +362,7 @@
             x, w_in, b_in[None, :], w_out_t, b_out[None, :],
         )
     ]
-    weight, bout, cot0, cot2, cot1, cot3, x, w_in, b_in, w_out_t, b_out = pl.pallas_call(
+    weight, bout, cot0, cot2, cot1, cot3, x, w_first, b_in, w_out_t, b_out = pl.pallas_call(
         cotangent_kernel,
         in_specs=[SMEM] + [hbm] * 9,
         out_specs=[whole] * 11,
@@ -337,7 +370,7 @@
         + [sent] * 4
         + [
             shape((rows, width), BF16),
-            shape((width, hid), BF16),
+            shape((width, hid // 2), BF16),
             shape((1, hid), F32),
             shape((n_vars, hid), BF16),
             shape((1, n_vars), F32),
@@ -358,7 +391,7 @@
     cot1 = lax.ppermute(cot1, "y", pairs_of("y", 1))
     cot3 = lax.ppermute(cot3, "y", pairs_of("y", 3))
 
-    cols = 512
+    cols = hid // 2
     by_cols = lambda height: pl.BlockSpec((height, cols), lambda i: (0, i))
     hidden, slope, val0, val2, val1, val3 = pl.pallas_call(
         forward_kernel,
@@ -366,17 +399,22 @@
         in_specs=[
             SMEM,
             const_spec((rows, width)),
-            by_cols(width),
+            const_spec((width, cols)),
+            hbm,
             by_cols(1),
             by_cols(n_vars),
             const_spec((1, n_vars)),
         ],
         out_specs=[by_cols(rows), by_cols(rows)] + [const_spec(sent.shape)] * 4,
         out_shape=[shape((rows, hid), BF16), shape((rows, hid), F32)] + [sent] * 4,
-        scratch_shapes=[pltpu.VMEM((rows, n_vars), F32)],
+        scratch_shapes=[
+            pltpu.VMEM((rows, n_vars), F32),
+            pltpu.VMEM((width, cols), BF16),
+            pltpu.SemaphoreType.DMA,
+        ],
         compiler_params=PARAMS,
         name="forward",
-    )(ids_later, x, w_in, b_in, w_out_t, b_out)
+    )(ids_later, x, w_first, operands[5], b_in, w_out_t, b_out)
 
     n_plane = lax.axis_size(PLANE)
     block = width // (2 * n_plane)
@@ -446,24 +484,44 @@
 
     mine = lax.all_to_all(copies, PLANE, 0, 0, tiled=True)
     theirs = lax.ppermute(mine, "core", swap)
-    finals = [
-        shape((block // 4, hid), F32),
-        shape((n_vars, hid), F32),
-        shape((1, hid), F32),
-        shape((1, n_vars), F32),
-        shape((1, 1), F32),
-    ]
-    grad_in, grad_out, grad_bin, grad_bout, loss = pl.pallas_call(
-        lambda *refs: final_kernel(scale, 1.0 / (n_points * n_vars), *refs),
-        in_specs=[SMEM] + [whole] * 3,
-        out_specs=[hbm] * 5,
-        out_shape=finals,
-        scratch_shapes=[pltpu.VMEM((128, hid), F32)]
-        + [pltpu.VMEM(final.shape, F32) for final in finals]
-        + [pltpu.SemaphoreType.DMA((6,))],
-        compiler_params=PARAMS,
-        name="unpack",
-    )(ids, grad_in, mine, theirs)
+    half = hid // 2
+    in_shape = shape((block // 4, hid), F32)
+    out_shape = shape((n_vars, hid), F32)
+    bin_shape = shape((1, hid), F32)
+    bout_shape = shape((1, n_vars), F32)
+    loss_shape = shape((1, 1), F32)
+    grad_in, grad_out, grad_bin = pl.pallas_call(
+        lambda *refs: own_kernel(scale, *refs),
+        in_specs=[SMEM] + [whole] * 2,
+        out_specs=[hbm] * 3,
+        out_shape=[in_shape, out_shape, bin_shape],
+        scratch_shapes=[
+            pltpu.VMEM((128, half), F32),
+            pltpu.VMEM(in_shape.shape, F32),
+            pltpu.VMEM((n_vars, half), F32),
+            pltpu.VMEM((1, half), F32),
+            pltpu.SemaphoreType.DMA((3,)),
+        ],
+        compiler_params=PARAMS,
+        name="unpack_own",
+    )(ids, grad_in, mine)
+    grad_out, grad_bin, grad_bout, loss = pl.pallas_call(
+        lambda *refs: other_kernel(scale, 1.0 / (n_points * n_vars), *refs),
+        in_specs=[SMEM, hbm, hbm] + [whole] * 2,
+        out_specs=[hbm] * 4,
+        out_shape=[out_shape, bin_shape, bout_shape, loss_shape],
+        input_output_aliases={1: 0, 2: 1},
+        scratch_shapes=[
+            pltpu.VMEM((128, half), F32),
+            pltpu.VMEM((n_vars, half), F32),
+            pltpu.VMEM((1, half), F32),
+            pltpu.VMEM(bout_shape.shape, F32),
+            pltpu.VMEM(loss_shape.shape, F32),
+            pltpu.SemaphoreType.DMA((4,)),
+        ],
+        compiler_params=PARAMS,
+        name="unpack_other",
+    )(ids, grad_out, grad_bin, mine, theirs)
     return (loss.reshape(1), grad_in, grad_out.T, grad_bin.reshape(hid), grad_bout.reshape(n_vars))
 
 

time: 82.1 us -> 81.9 us (level)
  waiting for transfers between devices: 17.8 us -> 16.6 us
  Pallas kernels: 17.5 us -> 18.5 us
    pallas_call x1 -> x2, Pallas kernels: 1.42 us -> 2.6 us  [the longest x1 1.31 us: per_device(): pl.pallas_call(lambda *refs: other_kernel(scale, 1.0 / (n_points * n_vars...]
    ppermute x1, waiting for transfers between devices: 1.16 us -> 0.01 us  [per_device(): theirs = lax.ppermute(mine, 'core', swap)]
  transfers between devices with their start and end apart: 12 -> 12, of which waited for: 5 -> 4; matrix products, arithmetic and copies ran while one was open for 0% -> 0% of each run, Pallas kernels for 9% -> 10%
where the time goes in v6:
time: 81.9 us; the launch traced here: 81.6 us
  starting transfers between devices  32 us (39%)
  Pallas kernels  18.5 us (23%)
  waiting for transfers between devices  16.6 us (20%)
  blocking collectives  13.5 us (16%)
  between operations  0.93 us (1%)
    all_to_all x1, blocking collectives, per_device(): mine = lax.all_to_all(copies, PLANE, 0, 0, tiled=True)  13.5 us
    all_to_all x1, waiting for transfers between devices, per_device(): landed = lax.all_to_all(payload, PLANE, 0, 0, tiled=True)  13.4 us
    all_to_all x1, starting transfers between devices, per_device(): landed = lax.all_to_all(payload, PLANE, 0, 0, tiled=True)  6.66 us
    ppermute x1, starting transfers between devices, per_device(): part2 = lax.ppermute(part2, 'zhi', shift('zhi', 2))  6.1 us
    pallas_call x1, Pallas kernels, per_device(): pl.pallas_call(forward_kernel, grid=(hid // cols,), in_specs=[SMEM, const...  5.78 us
    ppermute x1, starting transfers between devices, per_device(): theirs = lax.ppermute(mine, 'core', swap)  4.41 us
    pallas_call x1, Pallas kernels, per_device(): pl.pallas_call(backward_kernel, in_specs=[SMEM] + [whole] * 9, out_specs=...  4.23 us
    ppermute x1, starting transfers between devices, per_device(): cot2 = lax.ppermute(cot2, 'y', pairs_of('y', 2))  3.83 us
  transfers between devices with their start and end apart: 12, of which 4 were waited for; matrix products, arithmetic and copies ran while one was open for 0% of the time, Pallas kernels for 10%

profile of v6, /device:TPU:1, one launch (start us, length us, event | category | flops | bytes accessed | tf_op | source)
XLA Modules:
  0.0 81.6 jit_solution(1987603280961659869)
XLA Ops:
  0.7 2.8 %cotangent.1 = (f32[64,100]{1,0:T(8,128)S(1)}, f32[1,100]{1,0:T(1,128)S(1)}, bf16[4,64,100]{2,1,0:T(8,128)(2,1)S(1)}, bf16[4,64,100]{2,1,0:T(8,128)(2,1)S(1)}, b...) custom-call(s32[3]{0:T(128)S(1)} %pad_add_fusion.ids.refs_0_, ...), custom_call_target="tpu_custom_call" | custom-call | tf_op jit(solution)/shard_map/cotangent/pallas_call | solution.py:365
  3.5 3.8 %collective-permute-start = (bf16[4,64,100]{2,1,0:T(8,128)(2,1)S(1)}, bf16[4,64,100]{2,1,0:T(8,128)(2,1)S(1)}, u32[]{:S(2)}, u32[]{:S(2)}) collective-permute-start(bf16[4,64,100]{2,1,0:T(8,128)(2,1)S(1)} %get-tuple-element.50), channel_id=1, source_target_pairs={{0,128},{64,192},{128,0},{192,64},{1,129},{65,193},{129,1},{193,65... | collective-permute-start | bytes 153608 | tf_op jit(solution)/shard_map/ppermute | solution.py:390
  7.3 0.4 collective-permute-start.1
  7.7 0.4 collective-permute-start.2
  8.1 5.8 %forward.1 = (bf16[1024,1024]{1,0:T(8,128)(2,1)S(1)}, f32[1024,1024]{1,0:T(8,128)S(1)}, bf16[4,64,100]{2,1,0:T(8,128)(2,1)S(1)}, bf16[4,64,100]{2,1,0:T(8,128)(2...) custom-call(s32[3]{0:T(128)S(1)} %pad_add_fusion.ids.refs_0_, ...), custom_call_target="tpu_custom_call" | custom-call | tf_op jit(solution)/shard_map/forward/pallas_call | solution.py:396
  13.9 4.2 %backward.1 = (f32[32,16,1152]{2,1,0:T(8,128)S(1)}, bf16[32,16,1152]{2,1,0:T(8,128)(2,1)S(1)}) custom-call(s32[3]{0:T(128)S(1)} %pad_add_fusion.ids.refs_0_, bf16[4,64,100]{2,1,0:T(8,128)(2,1)S(1)} %get-tuple-element.46.got0, bf16[4,64,100]{2,1,0:T(8,128)(2,1)S(1)} %collective-permute-done.got2, bf16[4,64,100]{2,1,0:T(8,128)(2,1)S(1)} %collective-permute-done.1.got1, ...), custom_call_target="tpu_custom_call" | custom-call | tf_op jit(solution)/shard_map/backward/pallas_call | solution.py:421
  18.2 2.9 %collective-permute-start.3 = (bf16[32,16,1152]{2,1,0:T(8,128)(2,1)S(1)}, bf16[32,16,1152]{2,1,0:T(8,128)(2,1)S(1)}, u32[]{:S(2)}, u32[]{:S(2)}) collective-permute-start(bf16[32,16,1152]{2,1,0:T(8,128)(2,1)S(1)} %get-tuple-element.63), channel_id=1, source_target_pairs={{0,4},{4,0},{1,5},{5,1},{2,6},{6,2},{3,7},{7,3},{8,12},{12,8},{9,1... | collective-permute-start | bytes 3538952 | tf_op jit(solution)/shard_map/ppermute | solution.py:439
  21.1 2.5 %collective-permute-done.3.got_ref = bf16[32,16,1152]{2,1,0:T(8,128)(2,1)S(1)} collective-permute-done((bf16[32,16,1152]{2,1,0:T(8,128)(2,1)S(1)}, bf16[32,16,1152]{2,1,0:T(8,128)(2,1)S(1)}, u32[]{:S(2)}, u32[]{:S(2)}) %collective-permute-start.3) | collective-permute-done | bytes 1179680 | tf_op jit(solution)/shard_map/ppermute | solution.py:439
  23.6 1.2 %payload.1 = bf16[32,16,1152]{2,1,0:T(8,128)(2,1)} custom-call(f32[32,16,1152]{2,1,0:T(8,128)S(1)} %get-tuple-element.62.keep_ref, bf16[32,16,1152]{2,1,0:T(8,128)(2,1)S(1)} %collective-permute-done.3.got_ref), custom_call_target="tpu_custom_call" | custom-call | tf_op jit(solution)/shard_map/payload/pallas_call | solution.py:441
  24.8 6.7 %all-to-all-start = ((bf16[32,16,1152]{2,1,0:T(8,128)(2,1)}), bf16[32,16,1152]{2,1,0:T(8,128)(2,1)S(1)}, u32[]{:S(2)}, u32[]{:S(2)}) async-start(bf16[32,16,1152]{2,1,0:T(8,128)(2,1)} %payload.1), calls=%async_computation | async-start | bytes 2359296 | tf_op jit(solution)/shard_map/all_to_all | solution.py:451
  31.4 2.8 %collective-permute-start.7 = (bf16[4,64,100]{2,1,0:T(8,128)(2,1)S(1)}, bf16[4,64,100]{2,1,0:T(8,128)(2,1)S(1)}, u32[]{:S(2)}, u32[]{:S(2)}) collective-permute-start(bf16[4,64,100]{2,1,0:T(8,128)(2,1)S(1)} %get-tuple-element.74), channel_id=1, source_target_pairs={{0,128},{64,192},{128,0},{192,64},{1,129},{65,193},{129,1},{193,65... | collective-permute-start | bytes 153608 | tf_op jit(solution)/shard_map/ppermute | solution.py:452
  34.6 0.6 collective-permute-start.9
  35.1 13.4 %all-to-all-done.landed_ref = bf16[32,16,1152]{2,1,0:T(8,128)(2,1)S(1)} async-done(((bf16[32,16,1152]{2,1,0:T(8,128)(2,1)}), bf16[32,16,1152]{2,1,0:T(8,128)(2,1)S(1)}, u32[]{:S(2)}, u32[]{:S(2)}) %all-to-all-start) | async-done | bytes 1179680 | tf_op jit(solution)/shard_map/all_to_all | solution.py:451
  48.6 0.8 plane_sum.1
  49.4 6.1 %collective-permute-start.4 = (f32[16,384]{1,0:T(8,128)S(1)}, f32[16,384]{1,0:T(8,128)S(1)}, u32[]{:S(2)}, u32[]{:S(2)}) collective-permute-start(f32[16,384]{1,0:T(8,128)S(1)} %get-tuple-element.70), channel_id=1, source_target_pairs={{0,2},{1,3},{2,0},{3,1},{4,6},{5,7},{6,4},{7,5},{8,10},{9,11},{10,... | collective-permute-start | bytes 73736 | tf_op jit(solution)/shard_map/ppermute | solution.py:473
  55.5 1.2 %collective-permute-start.5 = (f32[16,384]{1,0:T(8,128)S(1)}, f32[16,384]{1,0:T(8,128)S(1)}, u32[]{:S(2)}, u32[]{:S(2)}) collective-permute-start(f32[16,384]{1,0:T(8,128)S(1)} %get-tuple-element.71), channel_id=1, source_target_pairs={{0,1},{1,2},{2,3},{3,0},{4,5},{5,6},{6,7},{7,4},{8,9},{9,10},{10,1... | collective-permute-start | bytes 73736 | tf_op jit(solution)/shard_map/ppermute | solution.py:474
  56.6 2.4 %collective-permute-start.6 = (f32[16,384]{1,0:T(8,128)S(1)}, f32[16,384]{1,0:T(8,128)S(1)}, u32[]{:S(2)}, u32[]{:S(2)}) collective-permute-start(f32[16,384]{1,0:T(8,128)S(1)} %get-tuple-element.72), channel_id=1, source_target_pairs={{0,3},{1,0},{2,1},{3,2},{4,7},{5,4},{6,5},{7,6},{8,11},{9,8},{10,9... | collective-permute-start | bytes 73736 | tf_op jit(solution)/shard_map/ppermute | solution.py:475
  59.0 0.6 loss.1.loss_ref
  59.7 0.6 collective-permute-done.5.got1
  60.3 0.6 total.1
  60.9 13.5 %all_to_all.10.refs_2_.refs_3_ = f32[32,16,128]{2,1,0:T(8,128)S(1)} all-to-all(f32[32,16,128]{2,1,0:T(8,128)S(1)} %get-tuple-element.79), channel_id=1, replica_groups=mesh['y'=4,'zlo'=2,'x'=4,'core'=2,'zhi'=4] {'y','zlo','x'}, dimensions={0} | all-to-all | bytes 524288 | tf_op jit(solution)/shard_map/all_to_all | solution.py:485
  74.4 4.4 %collective-permute-start.10 = (f32[32,16,128]{2,1,0:T(8,128)S(1)}, f32[32,16,128]{2,1,0:T(8,128)S(1)}, u32[]{:S(2)}, u32[]{:S(2)}) collective-permute-start(f32[32,16,128]{2,1,0:T(8,128)S(1)} %all_to_all.10.refs_2_.refs_3_), channel_id=1, source_target_pairs={{0,4},{4,0},{1,5},{5,1},{2,6},{6,2},{3,7},{7,3},{8,12},{12,8},{9,1... | collective-permute-start | bytes 786440 | tf_op jit(solution)/shard_map/ppermute | solution.py:486
  78.9 1.3 %unpack_own.1 = (f32[4,1024]{1,0:T(4,128)}, f32[100,1024]{1,0:T(8,128)}, f32[1,1024]{1,0:T(1,128)}) custom-call(s32[3]{0:T(128)S(1)} %pad_add_fusion.ids.refs_0_, f32[4,1024]{1,0:T(4,128)S(1)} %get-tuple-element.78.refs_1_, f32[32,16,128]{2,1,0:T(8,128)S(1)} %all_to_all.10.refs_2_.refs_3_), custom_call_target="tpu_custom_call" | custom-call | tf_op jit(solution)/shard_map/unpack_own/pallas_call | solution.py:493
  80.2 1.3 %unpack_other.1 = (f32[100,1024]{1,0:T(8,128)}, f32[1,1024]{1,0:T(1,128)}, f32[1,100]{1,0:T(1,128)}, f32[1,1]{1,0:T(1,128)}) custom-call(s32[3]{0:T(128)S(1)} %pad_add_fusion.ids.refs_0_, f32[100,1024]{1,0:T(8,128)} %get-tuple-element.80.refs_1_, f32[1,1024]{1,0:T(1,128)} %get-tuple-element.81.refs_2_, ...), custom_call_target="tpu_custom_call", output_to_operand_aliasing={{0}: (1, {}), {1}: (2, {})} | custom-call | tf_op jit(solution)/shard_map/unpack_other/pallas_call | solution.py:508
  (13 shorter events, 0.5 us)
Async XLA Ops:
  3.5 10.4 %collective-permute-start = (bf16[4,64,100]{2,1,0:T(8,128)(2,1)S(1)}, bf16[4,64,100]{2,1,0:T(8,128)(2,1)S(1)}, u32[]{:S(2)}, u32[]{:S(2)}) collective-permute-start(bf16[4,64,100]{2,1,0:T(8,128)(2,1)S(1)} %get-tuple-element.50), channel_id=1, source_target_pairs={{0,128},{64,192},{128,0},{192,64},{1,129},{65,193},{129,1},{193,65... | collective-permute-start | bytes 153608 | tf_op jit(solution)/shard_map/ppermute | solution.py:390
  7.3 6.6 %collective-permute-start.1 = (bf16[4,64,100]{2,1,0:T(8,128)(2,1)S(1)}, bf16[4,64,100]{2,1,0:T(8,128)(2,1)S(1)}, u32[]{:S(2)}, u32[]{:S(2)}) collective-permute-start(bf16[4,64,100]{2,1,0:T(8,128)(2,1)S(1)} %get-tuple-element.51), channel_id=1, source_target_pairs={{0,64},{64,0},{128,192},{192,128},{1,65},{65,1},{129,193},{193,129... | collective-permute-start | bytes 153608 | tf_op jit(solution)/shard_map/ppermute | solution.py:391
  7.7 6.2 %collective-permute-start.2 = (bf16[4,64,100]{2,1,0:T(8,128)(2,1)S(1)}, bf16[4,64,100]{2,1,0:T(8,128)(2,1)S(1)}, u32[]{:S(2)}, u32[]{:S(2)}) collective-permute-start(bf16[4,64,100]{2,1,0:T(8,128)(2,1)S(1)} %get-tuple-element.52), channel_id=1, source_target_pairs={{0,192},{64,128},{128,64},{192,0},{1,193},{65,129},{129,65},{193,1... | collective-permute-start | bytes 153608 | tf_op jit(solution)/shard_map/ppermute | solution.py:392
  18.2 5.4 %collective-permute-start.3 = (bf16[32,16,1152]{2,1,0:T(8,128)(2,1)S(1)}, bf16[32,16,1152]{2,1,0:T(8,128)(2,1)S(1)}, u32[]{:S(2)}, u32[]{:S(2)}) collective-permute-start(bf16[32,16,1152]{2,1,0:T(8,128)(2,1)S(1)} %get-tuple-element.63), channel_id=1, source_target_pairs={{0,4},{4,0},{1,5},{5,1},{2,6},{6,2},{3,7},{7,3},{8,12},{12,8},{9,1... | collective-permute-start | bytes 3538952 | tf_op jit(solution)/shard_map/ppermute | solution.py:439
  24.7 34.3 %copy-start = (f32[1,100,64]{1,2,0:T(8,128)S(1)}, f32[1,100,64]{1,2,0:T(8,128)}, u32[]{:S(2)}) copy-start(f32[1,100,64]{1,2,0:T(8,128)} %param.15) | copy-start | bytes 76804
  24.8 23.8 %all-to-all-start = ((bf16[32,16,1152]{2,1,0:T(8,128)(2,1)}), bf16[32,16,1152]{2,1,0:T(8,128)(2,1)S(1)}, u32[]{:S(2)}, u32[]{:S(2)}) async-start(bf16[32,16,1152]{2,1,0:T(8,128)(2,1)} %payload.1), calls=%async_computation | async-start | bytes 2359296 | tf_op jit(solution)/shard_map/all_to_all | solution.py:451
  31.4 25.2 %collective-permute-start.7 = (bf16[4,64,100]{2,1,0:T(8,128)(2,1)S(1)}, bf16[4,64,100]{2,1,0:T(8,128)(2,1)S(1)}, u32[]{:S(2)}, u32[]{:S(2)}) collective-permute-start(bf16[4,64,100]{2,1,0:T(8,128)(2,1)S(1)} %get-tuple-element.74), channel_id=1, source_target_pairs={{0,128},{64,192},{128,0},{192,64},{1,129},{65,193},{129,1},{193,65... | collective-permute-start | bytes 153608 | tf_op jit(solution)/shard_map/ppermute | solution.py:452
  34.3 24.8 %collective-permute-start.8 = (bf16[4,64,100]{2,1,0:T(8,128)(2,1)S(1)}, bf16[4,64,100]{2,1,0:T(8,128)(2,1)S(1)}, u32[]{:S(2)}, u32[]{:S(2)}) collective-permute-start(bf16[4,64,100]{2,1,0:T(8,128)(2,1)S(1)} %get-tuple-element.75), channel_id=1, source_target_pairs={{0,64},{64,0},{128,192},{192,128},{1,65},{65,1},{129,193},{193,129... | collective-permute-start | bytes 153608 | tf_op jit(solution)/shard_map/ppermute | solution.py:453
  34.6 24.5 %collective-permute-start.9 = (bf16[4,64,100]{2,1,0:T(8,128)(2,1)S(1)}, bf16[4,64,100]{2,1,0:T(8,128)(2,1)S(1)}, u32[]{:S(2)}, u32[]{:S(2)}) collective-permute-start(bf16[4,64,100]{2,1,0:T(8,128)(2,1)S(1)} %get-tuple-element.76), channel_id=1, source_target_pairs={{0,192},{64,128},{128,64},{192,0},{1,193},{65,129},{129,65},{193,1... | collective-permute-start | bytes 153608 | tf_op jit(solution)/shard_map/ppermute | solution.py:454
  49.4 10.3 %collective-permute-start.4 = (f32[16,384]{1,0:T(8,128)S(1)}, f32[16,384]{1,0:T(8,128)S(1)}, u32[]{:S(2)}, u32[]{:S(2)}) collective-permute-start(f32[16,384]{1,0:T(8,128)S(1)} %get-tuple-element.70), channel_id=1, source_target_pairs={{0,2},{1,3},{2,0},{3,1},{4,6},{5,7},{6,4},{7,5},{8,10},{9,11},{10,... | collective-permute-start | bytes 73736 | tf_op jit(solution)/shard_map/ppermute | solution.py:473
  55.5 4.8 %collective-permute-start.5 = (f32[16,384]{1,0:T(8,128)S(1)}, f32[16,384]{1,0:T(8,128)S(1)}, u32[]{:S(2)}, u32[]{:S(2)}) collective-permute-start(f32[16,384]{1,0:T(8,128)S(1)} %get-tuple-element.71), channel_id=1, source_target_pairs={{0,1},{1,2},{2,3},{3,0},{4,5},{5,6},{6,7},{7,4},{8,9},{9,10},{10,1... | collective-permute-start | bytes 73736 | tf_op jit(solution)/shard_map/ppermute | solution.py:474
  56.6 3.7 %collective-permute-start.6 = (f32[16,384]{1,0:T(8,128)S(1)}, f32[16,384]{1,0:T(8,128)S(1)}, u32[]{:S(2)}, u32[]{:S(2)}) collective-permute-start(f32[16,384]{1,0:T(8,128)S(1)} %get-tuple-element.72), channel_id=1, source_target_pairs={{0,3},{1,0},{2,1},{3,2},{4,7},{5,4},{6,5},{7,6},{8,11},{9,8},{10,9... | collective-permute-start | bytes 73736 | tf_op jit(solution)/shard_map/ppermute | solution.py:475
  74.4 5.7 %collective-permute-start.10 = (f32[32,16,128]{2,1,0:T(8,128)S(1)}, f32[32,16,128]{2,1,0:T(8,128)S(1)}, u32[]{:S(2)}, u32[]{:S(2)}) collective-permute-start(f32[32,16,128]{2,1,0:T(8,128)S(1)} %all_to_all.10.refs_2_.refs_3_), channel_id=1, source_target_pairs={{0,4},{4,0},{1,5},{5,1},{2,6},{6,2},{3,7},{7,3},{8,12},{12,8},{9,1... | collective-permute-start | bytes 786440 | tf_op jit(solution)/shard_map/ppermute | solution.py:486

commit v7 on v6

--- a/solution.py
+++ b/solution.py
@@ -50,13 +50,13 @@
 
 
 def cotangent_kernel(
-    ids, rank_hbm, obs_hbm, area_hbm, vw_hbm, x_hbm, w_in_hbm, b_in_hbm, w_out_hbm, b_out_hbm,
-    weight_ref, bout_ref, send0, send2, send1, send3, x_ref, w_in_ref, b_in_ref, w_out_ref, b_out_ref,
+    ids, rank_hbm, obs_hbm, area_hbm, vw_hbm, x_hbm, w_in_hbm, b_in_hbm, b_out_hbm,
+    weight_ref, bout_ref, send0, send2, send1, send3, x_ref, w_in_ref, b_in_ref, b_out_ref,
     every, rank_ref, obs_ref, area_ref, vw_ref, sems,
 ):
     pairs = [(rank_hbm, rank_ref), (obs_hbm, obs_ref), (area_hbm, area_ref), (vw_hbm, vw_ref)]
     needed = len(pairs)
-    pairs += [(w_out_hbm, w_out_ref), (b_in_hbm, b_in_ref), (b_out_hbm, b_out_ref)]
+    pairs += [(b_in_hbm, b_in_ref), (b_out_hbm, b_out_ref)]
     first = w_in_hbm.at[:, 0 : w_in_ref.shape[1]]
     for source, target in ((x_hbm, x_ref), (first, w_in_ref)):
         piece = source.shape[0] // 4
@@ -97,11 +97,12 @@
 
 def forward_kernel(
     ids, x_ref, w_first, w_in_hbm, b_in_ref, w_out_ref, b_out_ref,
-    hidden_ref, slope_ref, send0, send2, send1, send3, values, w_ref, sem,
+    hidden_ref, slope_ref, w_out_copy, send0, send2, send1, send3, values, w_ref, sem,
 ):
     step = pl.program_id(0)
     mem_dev, sub, _ = send0.shape
     cols = w_first.shape[1]
+    w_out_copy[...] = w_out_ref[...]
     fetch = pltpu.make_async_copy(w_in_hbm.at[:, cols : 2 * cols], w_ref, sem)
 
     def half(weights):
@@ -359,20 +360,20 @@
         pltpu.with_memory_space_constraint(arr, pltpu.HBM)
         for arr in (
             ranks, obs, area[None, :], var_weight[None, :],
-            x, w_in, b_in[None, :], w_out_t, b_out[None, :],
+            x, w_in, b_in[None, :], b_out[None, :], w_out_t,
         )
     ]
-    weight, bout, cot0, cot2, cot1, cot3, x, w_first, b_in, w_out_t, b_out = pl.pallas_call(
+    w_in_hbm, w_out_hbm = operands[5], operands[8]
+    weight, bout, cot0, cot2, cot1, cot3, x, w_first, b_in, b_out = pl.pallas_call(
         cotangent_kernel,
-        in_specs=[SMEM] + [hbm] * 9,
-        out_specs=[whole] * 11,
+        in_specs=[SMEM] + [hbm] * 8,
+        out_specs=[whole] * 10,
         out_shape=[shape((sub, n_vars), F32), shape((1, n_vars), F32)]
         + [sent] * 4
         + [
             shape((rows, width), BF16),
             shape((width, hid // 2), BF16),
             shape((1, hid), F32),
-            shape((n_vars, hid), BF16),
             shape((1, n_vars), F32),
         ],
         scratch_shapes=[
@@ -381,11 +382,11 @@
             pltpu.VMEM((sub, n_vars), jnp.int32),
             pltpu.VMEM((1, sub), F32),
             pltpu.VMEM((1, n_vars), F32),
-            pltpu.SemaphoreType.DMA((15,)),
+            pltpu.SemaphoreType.DMA((14,)),
         ],
         compiler_params=PARAMS,
         name="cotangent",
-    )(ids, *operands)
+    )(ids, *operands[:8])
     ids_later, cot2, cot1, cot3 = lax.optimization_barrier((ids, cot2, cot1, cot3))
     cot2 = lax.ppermute(cot2, "y", pairs_of("y", 2))
     cot1 = lax.ppermute(cot1, "y", pairs_of("y", 1))
@@ -393,7 +394,7 @@
 
     cols = hid // 2
     by_cols = lambda height: pl.BlockSpec((height, cols), lambda i: (0, i))
-    hidden, slope, val0, val2, val1, val3 = pl.pallas_call(
+    hidden, slope, w_out_t, val0, val2, val1, val3 = pl.pallas_call(
         forward_kernel,
         grid=(hid // cols,),
         in_specs=[
@@ -405,8 +406,9 @@
             by_cols(n_vars),
             const_spec((1, n_vars)),
         ],
-        out_specs=[by_cols(rows), by_cols(rows)] + [const_spec(sent.shape)] * 4,
-        out_shape=[shape((rows, hid), BF16), shape((rows, hid), F32)] + [sent] * 4,
+        out_specs=[by_cols(rows), by_cols(rows), by_cols(n_vars)] + [const_spec(sent.shape)] * 4,
+        out_shape=[shape((rows, hid), BF16), shape((rows, hid), F32), shape((n_vars, hid), BF16)]
+        + [sent] * 4,
         scratch_shapes=[
             pltpu.VMEM((rows, n_vars), F32),
             pltpu.VMEM((width, cols), BF16),
@@ -414,7 +416,7 @@
         ],
         compiler_params=PARAMS,
         name="forward",
-    )(ids_later, x, w_first, operands[5], b_in, w_out_t, b_out)
+    )(ids_later, x, w_first, w_in_hbm, b_in, w_out_hbm, b_out)
 
     n_plane = lax.axis_size(PLANE)
     block = width // (2 * n_plane)

time: 81.9 us -> 82.3 us (level)
  transfers between devices with their start and end apart: 12 -> 12, of which waited for: 4 -> 4; matrix products, arithmetic and copies ran while one was open for 0% -> 0% of each run, Pallas kernels for 10% -> 11%
where the time goes in v7:
time: 82.3 us; the launch traced here: 82 us
  starting transfers between devices  32 us (39%)
  Pallas kernels  18.8 us (23%)
  waiting for transfers between devices  16.6 us (20%)
  blocking collectives  13.5 us (16%)
  between operations  0.93 us (1%)
    all_to_all x1, blocking collectives, per_device(): mine = lax.all_to_all(copies, PLANE, 0, 0, tiled=True)  13.5 us
    all_to_all x1, waiting for transfers between devices, per_device(): landed = lax.all_to_all(payload, PLANE, 0, 0, tiled=True)  13.4 us
    all_to_all x1, starting transfers between devices, per_device(): landed = lax.all_to_all(payload, PLANE, 0, 0, tiled=True)  6.67 us
    pallas_call x1, Pallas kernels, per_device(): pl.pallas_call(forward_kernel, grid=(hid // cols,), in_specs=[SMEM, const...  6.18 us
    ppermute x1, starting transfers between devices, per_device(): part2 = lax.ppermute(part2, 'zhi', shift('zhi', 2))  6.09 us
    ppermute x1, starting transfers between devices, per_device(): theirs = lax.ppermute(mine, 'core', swap)  4.42 us
    pallas_call x1, Pallas kernels, per_device(): pl.pallas_call(backward_kernel, in_specs=[SMEM] + [whole] * 9, out_specs=...  4.23 us
    ppermute x1, starting transfers between devices, per_device(): cot2 = lax.ppermute(cot2, 'y', pairs_of('y', 2))  3.83 us
  transfers between devices with their start and end apart: 12, of which 4 were waited for; matrix products, arithmetic and copies ran while one was open for 0% of the time, Pallas kernels for 11%

profile of v7, /device:TPU:1, one launch (start us, length us, event | category | flops | bytes accessed | tf_op | source)
XLA Modules:
  0.0 82.0 jit_solution(9307506841179377146)
XLA Ops:
  0.7 2.7 %cotangent.1 = (f32[64,100]{1,0:T(8,128)S(1)}, f32[1,100]{1,0:T(1,128)S(1)}, bf16[4,64,100]{2,1,0:T(8,128)(2,1)S(1)}, bf16[4,64,100]{2,1,0:T(8,128)(2,1)S(1)}, b...) custom-call(s32[3]{0:T(128)S(1)} %pad_add_fusion.ids.refs_0_, ...), custom_call_target="tpu_custom_call" | custom-call | tf_op jit(solution)/shard_map/cotangent/pallas_call | solution.py:367
  3.4 3.8 %collective-permute-start = (bf16[4,64,100]{2,1,0:T(8,128)(2,1)S(1)}, bf16[4,64,100]{2,1,0:T(8,128)(2,1)S(1)}, u32[]{:S(2)}, u32[]{:S(2)}) collective-permute-start(bf16[4,64,100]{2,1,0:T(8,128)(2,1)S(1)} %get-tuple-element.50), channel_id=1, source_target_pairs={{0,128},{64,192},{128,0},{192,64},{1,129},{65,193},{129,1},{193,65... | collective-permute-start | bytes 153608 | tf_op jit(solution)/shard_map/ppermute | solution.py:391
  7.3 0.4 collective-permute-start.1
  7.7 0.4 collective-permute-start.2
  8.1 6.2 %forward.1 = (bf16[1024,1024]{1,0:T(8,128)(2,1)S(1)}, f32[1024,1024]{1,0:T(8,128)S(1)}, bf16[100,1024]{1,0:T(8,128)(2,1)S(1)}, bf16[4,64,100]{2,1,0:T(8,128)(2,1...) custom-call(s32[3]{0:T(128)S(1)} %pad_add_fusion.ids.refs_0_, ...), custom_call_target="tpu_custom_call" | custom-call | tf_op jit(solution)/shard_map/forward/pallas_call | solution.py:397
  14.3 4.2 %backward.1 = (f32[32,16,1152]{2,1,0:T(8,128)S(1)}, bf16[32,16,1152]{2,1,0:T(8,128)(2,1)S(1)}) custom-call(s32[3]{0:T(128)S(1)} %pad_add_fusion.ids.refs_0_, bf16[4,64,100]{2,1,0:T(8,128)(2,1)S(1)} %get-tuple-element.46.got0, bf16[4,64,100]{2,1,0:T(8,128)(2,1)S(1)} %collective-permute-done.got2, bf16[4,64,100]{2,1,0:T(8,128)(2,1)S(1)} %collective-permute-done.1.got1, ...), custom_call_target="tpu_custom_call" | custom-call | tf_op jit(solution)/shard_map/backward/pallas_call | solution.py:423
  18.5 2.9 %collective-permute-start.3 = (bf16[32,16,1152]{2,1,0:T(8,128)(2,1)S(1)}, bf16[32,16,1152]{2,1,0:T(8,128)(2,1)S(1)}, u32[]{:S(2)}, u32[]{:S(2)}) collective-permute-start(bf16[32,16,1152]{2,1,0:T(8,128)(2,1)S(1)} %get-tuple-element.63), channel_id=1, source_target_pairs={{0,4},{4,0},{1,5},{5,1},{2,6},{6,2},{3,7},{7,3},{8,12},{12,8},{9,1... | collective-permute-start | bytes 3538952 | tf_op jit(solution)/shard_map/ppermute | solution.py:441
  21.4 2.5 %collective-permute-done.3.got_ref = bf16[32,16,1152]{2,1,0:T(8,128)(2,1)S(1)} collective-permute-done((bf16[32,16,1152]{2,1,0:T(8,128)(2,1)S(1)}, bf16[32,16,1152]{2,1,0:T(8,128)(2,1)S(1)}, u32[]{:S(2)}, u32[]{:S(2)}) %collective-permute-start.3) | collective-permute-done | bytes 1179680 | tf_op jit(solution)/shard_map/ppermute | solution.py:441
  23.9 1.2 %payload.1 = bf16[32,16,1152]{2,1,0:T(8,128)(2,1)} custom-call(f32[32,16,1152]{2,1,0:T(8,128)S(1)} %get-tuple-element.62.keep_ref, bf16[32,16,1152]{2,1,0:T(8,128)(2,1)S(1)} %collective-permute-done.3.got_ref), custom_call_target="tpu_custom_call" | custom-call | tf_op jit(solution)/shard_map/payload/pallas_call | solution.py:443
  25.1 6.7 %all-to-all-start = ((bf16[32,16,1152]{2,1,0:T(8,128)(2,1)}), bf16[32,16,1152]{2,1,0:T(8,128)(2,1)S(1)}, u32[]{:S(2)}, u32[]{:S(2)}) async-start(bf16[32,16,1152]{2,1,0:T(8,128)(2,1)} %payload.1), calls=%async_computation | async-start | bytes 2359296 | tf_op jit(solution)/shard_map/all_to_all | solution.py:453
  31.8 2.8 %collective-permute-start.7 = (bf16[4,64,100]{2,1,0:T(8,128)(2,1)S(1)}, bf16[4,64,100]{2,1,0:T(8,128)(2,1)S(1)}, u32[]{:S(2)}, u32[]{:S(2)}) collective-permute-start(bf16[4,64,100]{2,1,0:T(8,128)(2,1)S(1)} %get-tuple-element.74), channel_id=1, source_target_pairs={{0,128},{64,192},{128,0},{192,64},{1,129},{65,193},{129,1},{193,65... | collective-permute-start | bytes 153608 | tf_op jit(solution)/shard_map/ppermute | solution.py:454
  34.9 0.6 collective-permute-start.9
  35.5 13.4 %all-to-all-done.landed_ref = bf16[32,16,1152]{2,1,0:T(8,128)(2,1)S(1)} async-done(((bf16[32,16,1152]{2,1,0:T(8,128)(2,1)}), bf16[32,16,1152]{2,1,0:T(8,128)(2,1)S(1)}, u32[]{:S(2)}, u32[]{:S(2)}) %all-to-all-start) | async-done | bytes 1179680 | tf_op jit(solution)/shard_map/all_to_all | solution.py:453
  48.9 0.8 plane_sum.1
  49.7 6.1 %collective-permute-start.4 = (f32[16,384]{1,0:T(8,128)S(1)}, f32[16,384]{1,0:T(8,128)S(1)}, u32[]{:S(2)}, u32[]{:S(2)}) collective-permute-start(f32[16,384]{1,0:T(8,128)S(1)} %get-tuple-element.70), channel_id=1, source_target_pairs={{0,2},{1,3},{2,0},{3,1},{4,6},{5,7},{6,4},{7,5},{8,10},{9,11},{10,... | collective-permute-start | bytes 73736 | tf_op jit(solution)/shard_map/ppermute | solution.py:475
  55.8 1.2 %collective-permute-start.5 = (f32[16,384]{1,0:T(8,128)S(1)}, f32[16,384]{1,0:T(8,128)S(1)}, u32[]{:S(2)}, u32[]{:S(2)}) collective-permute-start(f32[16,384]{1,0:T(8,128)S(1)} %get-tuple-element.71), channel_id=1, source_target_pairs={{0,1},{1,2},{2,3},{3,0},{4,5},{5,6},{6,7},{7,4},{8,9},{9,10},{10,1... | collective-permute-start | bytes 73736 | tf_op jit(solution)/shard_map/ppermute | solution.py:476
  57.0 2.4 %collective-permute-start.6 = (f32[16,384]{1,0:T(8,128)S(1)}, f32[16,384]{1,0:T(8,128)S(1)}, u32[]{:S(2)}, u32[]{:S(2)}) collective-permute-start(f32[16,384]{1,0:T(8,128)S(1)} %get-tuple-element.72), channel_id=1, source_target_pairs={{0,3},{1,0},{2,1},{3,2},{4,7},{5,4},{6,5},{7,6},{8,11},{9,8},{10,9... | collective-permute-start | bytes 73736 | tf_op jit(solution)/shard_map/ppermute | solution.py:477
  59.4 0.6 loss.1.loss_ref
  60.0 0.6 collective-permute-done.5.got1
  60.7 0.6 total.1
  61.2 13.5 %all_to_all.10.refs_2_.refs_3_ = f32[32,16,128]{2,1,0:T(8,128)S(1)} all-to-all(f32[32,16,128]{2,1,0:T(8,128)S(1)} %get-tuple-element.79), channel_id=1, replica_groups=mesh['y'=4,'zlo'=2,'x'=4,'core'=2,'zhi'=4] {'y','zlo','x'}, dimensions={0} | all-to-all | bytes 524288 | tf_op jit(solution)/shard_map/all_to_all | solution.py:487
  74.8 4.4 %collective-permute-start.10 = (f32[32,16,128]{2,1,0:T(8,128)S(1)}, f32[32,16,128]{2,1,0:T(8,128)S(1)}, u32[]{:S(2)}, u32[]{:S(2)}) collective-permute-start(f32[32,16,128]{2,1,0:T(8,128)S(1)} %all_to_all.10.refs_2_.refs_3_), channel_id=1, source_target_pairs={{0,4},{4,0},{1,5},{5,1},{2,6},{6,2},{3,7},{7,3},{8,12},{12,8},{9,1... | collective-permute-start | bytes 786440 | tf_op jit(solution)/shard_map/ppermute | solution.py:488
  79.2 1.3 %unpack_own.1 = (f32[4,1024]{1,0:T(4,128)}, f32[100,1024]{1,0:T(8,128)}, f32[1,1024]{1,0:T(1,128)}) custom-call(s32[3]{0:T(128)S(1)} %pad_add_fusion.ids.refs_0_, f32[4,1024]{1,0:T(4,128)S(1)} %get-tuple-element.78.refs_1_, f32[32,16,128]{2,1,0:T(8,128)S(1)} %all_to_all.10.refs_2_.refs_3_), custom_call_target="tpu_custom_call" | custom-call | tf_op jit(solution)/shard_map/unpack_own/pallas_call | solution.py:495
  80.5 1.3 %unpack_other.1 = (f32[100,1024]{1,0:T(8,128)}, f32[1,1024]{1,0:T(1,128)}, f32[1,100]{1,0:T(1,128)}, f32[1,1]{1,0:T(1,128)}) custom-call(s32[3]{0:T(128)S(1)} %pad_add_fusion.ids.refs_0_, f32[100,1024]{1,0:T(8,128)} %get-tuple-element.80.refs_1_, f32[1,1024]{1,0:T(1,128)} %get-tuple-element.81.refs_2_, ...), custom_call_target="tpu_custom_call", output_to_operand_aliasing={{0}: (1, {}), {1}: (2, {})} | custom-call | tf_op jit(solution)/shard_map/unpack_other/pallas_call | solution.py:510
  (13 shorter events, 0.5 us)
Async XLA Ops:
  3.4 10.8 %collective-permute-start = (bf16[4,64,100]{2,1,0:T(8,128)(2,1)S(1)}, bf16[4,64,100]{2,1,0:T(8,128)(2,1)S(1)}, u32[]{:S(2)}, u32[]{:S(2)}) collective-permute-start(bf16[4,64,100]{2,1,0:T(8,128)(2,1)S(1)} %get-tuple-element.50), channel_id=1, source_target_pairs={{0,128},{64,192},{128,0},{192,64},{1,129},{65,193},{129,1},{193,65... | collective-permute-start | bytes 153608 | tf_op jit(solution)/shard_map/ppermute | solution.py:391
  7.3 7.0 %collective-permute-start.1 = (bf16[4,64,100]{2,1,0:T(8,128)(2,1)S(1)}, bf16[4,64,100]{2,1,0:T(8,128)(2,1)S(1)}, u32[]{:S(2)}, u32[]{:S(2)}) collective-permute-start(bf16[4,64,100]{2,1,0:T(8,128)(2,1)S(1)} %get-tuple-element.51), channel_id=1, source_target_pairs={{0,64},{64,0},{128,192},{192,128},{1,65},{65,1},{129,193},{193,129... | collective-permute-start | bytes 153608 | tf_op jit(solution)/shard_map/ppermute | solution.py:392
  7.7 6.6 %collective-permute-start.2 = (bf16[4,64,100]{2,1,0:T(8,128)(2,1)S(1)}, bf16[4,64,100]{2,1,0:T(8,128)(2,1)S(1)}, u32[]{:S(2)}, u32[]{:S(2)}) collective-permute-start(bf16[4,64,100]{2,1,0:T(8,128)(2,1)S(1)} %get-tuple-element.52), channel_id=1, source_target_pairs={{0,192},{64,128},{128,64},{192,0},{1,193},{65,129},{129,65},{193,1... | collective-permute-start | bytes 153608 | tf_op jit(solution)/shard_map/ppermute | solution.py:393
  18.5 5.4 %collective-permute-start.3 = (bf16[32,16,1152]{2,1,0:T(8,128)(2,1)S(1)}, bf16[32,16,1152]{2,1,0:T(8,128)(2,1)S(1)}, u32[]{:S(2)}, u32[]{:S(2)}) collective-permute-start(bf16[32,16,1152]{2,1,0:T(8,128)(2,1)S(1)} %get-tuple-element.63), channel_id=1, source_target_pairs={{0,4},{4,0},{1,5},{5,1},{2,6},{6,2},{3,7},{7,3},{8,12},{12,8},{9,1... | collective-permute-start | bytes 3538952 | tf_op jit(solution)/shard_map/ppermute | solution.py:441
  25.1 34.3 %copy-start = (f32[1,100,64]{1,2,0:T(8,128)S(1)}, f32[1,100,64]{1,2,0:T(8,128)}, u32[]{:S(2)}) copy-start(f32[1,100,64]{1,2,0:T(8,128)} %param.15) | copy-start | bytes 76804
  25.1 23.8 %all-to-all-start = ((bf16[32,16,1152]{2,1,0:T(8,128)(2,1)}), bf16[32,16,1152]{2,1,0:T(8,128)(2,1)S(1)}, u32[]{:S(2)}, u32[]{:S(2)}) async-start(bf16[32,16,1152]{2,1,0:T(8,128)(2,1)} %payload.1), calls=%async_computation | async-start | bytes 2359296 | tf_op jit(solution)/shard_map/all_to_all | solution.py:453
  31.8 25.2 %collective-permute-start.7 = (bf16[4,64,100]{2,1,0:T(8,128)(2,1)S(1)}, bf16[4,64,100]{2,1,0:T(8,128)(2,1)S(1)}, u32[]{:S(2)}, u32[]{:S(2)}) collective-permute-start(bf16[4,64,100]{2,1,0:T(8,128)(2,1)S(1)} %get-tuple-element.74), channel_id=1, source_target_pairs={{0,128},{64,192},{128,0},{192,64},{1,129},{65,193},{129,1},{193,65... | collective-permute-start | bytes 153608 | tf_op jit(solution)/shard_map/ppermute | solution.py:454
  34.6 24.8 %collective-permute-start.8 = (bf16[4,64,100]{2,1,0:T(8,128)(2,1)S(1)}, bf16[4,64,100]{2,1,0:T(8,128)(2,1)S(1)}, u32[]{:S(2)}, u32[]{:S(2)}) collective-permute-start(bf16[4,64,100]{2,1,0:T(8,128)(2,1)S(1)} %get-tuple-element.75), channel_id=1, source_target_pairs={{0,64},{64,0},{128,192},{192,128},{1,65},{65,1},{129,193},{193,129... | collective-permute-start | bytes 153608 | tf_op jit(solution)/shard_map/ppermute | solution.py:455
  34.9 24.5 %collective-permute-start.9 = (bf16[4,64,100]{2,1,0:T(8,128)(2,1)S(1)}, bf16[4,64,100]{2,1,0:T(8,128)(2,1)S(1)}, u32[]{:S(2)}, u32[]{:S(2)}) collective-permute-start(bf16[4,64,100]{2,1,0:T(8,128)(2,1)S(1)} %get-tuple-element.76), channel_id=1, source_target_pairs={{0,192},{64,128},{128,64},{192,0},{1,193},{65,129},{129,65},{193,1... | collective-permute-start | bytes 153608 | tf_op jit(solution)/shard_map/ppermute | solution.py:456
  49.7 10.3 %collective-permute-start.4 = (f32[16,384]{1,0:T(8,128)S(1)}, f32[16,384]{1,0:T(8,128)S(1)}, u32[]{:S(2)}, u32[]{:S(2)}) collective-permute-start(f32[16,384]{1,0:T(8,128)S(1)} %get-tuple-element.70), channel_id=1, source_target_pairs={{0,2},{1,3},{2,0},{3,1},{4,6},{5,7},{6,4},{7,5},{8,10},{9,11},{10,... | collective-permute-start | bytes 73736 | tf_op jit(solution)/shard_map/ppermute | solution.py:475
  55.8 4.8 %collective-permute-start.5 = (f32[16,384]{1,0:T(8,128)S(1)}, f32[16,384]{1,0:T(8,128)S(1)}, u32[]{:S(2)}, u32[]{:S(2)}) collective-permute-start(f32[16,384]{1,0:T(8,128)S(1)} %get-tuple-element.71), channel_id=1, source_target_pairs={{0,1},{1,2},{2,3},{3,0},{4,5},{5,6},{6,7},{7,4},{8,9},{9,10},{10,1... | collective-permute-start | bytes 73736 | tf_op jit(solution)/shard_map/ppermute | solution.py:476
  57.0 3.7 %collective-permute-start.6 = (f32[16,384]{1,0:T(8,128)S(1)}, f32[16,384]{1,0:T(8,128)S(1)}, u32[]{:S(2)}, u32[]{:S(2)}) collective-permute-start(f32[16,384]{1,0:T(8,128)S(1)} %get-tuple-element.72), channel_id=1, source_target_pairs={{0,3},{1,0},{2,1},{3,2},{4,7},{5,4},{6,5},{7,6},{8,11},{9,8},{10,9... | collective-permute-start | bytes 73736 | tf_op jit(solution)/shard_map/ppermute | solution.py:477
  74.8 5.7 %collective-permute-start.10 = (f32[32,16,128]{2,1,0:T(8,128)S(1)}, f32[32,16,128]{2,1,0:T(8,128)S(1)}, u32[]{:S(2)}, u32[]{:S(2)}) collective-permute-start(f32[32,16,128]{2,1,0:T(8,128)S(1)} %all_to_all.10.refs_2_.refs_3_), channel_id=1, source_target_pairs={{0,4},{4,0},{1,5},{5,1},{2,6},{6,2},{3,7},{7,3},{8,12},{12,8},{9,1... | collective-permute-start | bytes 786440 | tf_op jit(solution)/shard_map/ppermute | solution.py:488

commit v8 on v7

--- a/solution.py
+++ b/solution.py
@@ -95,14 +95,9 @@
         fetch.wait()
 
 
-def forward_kernel(
-    ids, x_ref, w_first, w_in_hbm, b_in_ref, w_out_ref, b_out_ref,
-    hidden_ref, slope_ref, w_out_copy, send0, send2, send1, send3, values, w_ref, sem,
-):
+def forward_kernel(x_ref, w_first, w_in_hbm, b_in_ref, hidden_ref, slope_ref, w_ref, sem):
     step = pl.program_id(0)
-    mem_dev, sub, _ = send0.shape
     cols = w_first.shape[1]
-    w_out_copy[...] = w_out_ref[...]
     fetch = pltpu.make_async_copy(w_in_hbm.at[:, cols : 2 * cols], w_ref, sem)
 
     def half(weights):
@@ -110,33 +105,35 @@
         square = pre * pre
         t = jnp.tanh(pre * (GELU_C + (GELU_C * GELU_A) * square))
         upper = 0.5 + 0.5 * t
-        hidden = (pre * upper).astype(BF16)
-        hidden_ref[...] = hidden
+        hidden_ref[...] = (pre * upper).astype(BF16)
         slope_ref[...] = upper + pre * (0.5 - 0.5 * (t * t)) * (
             GELU_C + (3.0 * GELU_A * GELU_C) * square
         )
-        return lax.dot_general(
-            hidden, w_out_ref[...], (((1,), (1,)), ((), ())), preferred_element_type=F32
-        )
 
     @pl.when(step == 0)
     def _():
         fetch.start()
-        values[...] = half(w_first) + b_out_ref[...]
+        half(w_first)
 
     @pl.when(step == 1)
     def _():
         fetch.wait()
-        values[...] += half(w_ref)
-
-    @pl.when(step == pl.num_programs(0) - 1)
-    def _():
-        y = ids[0]
-        for k, out in enumerate((send0, send1, send2, send3)):
-            dest = y ^ k
-            for m in range(mem_dev):
-                start = pl.multiple_of(m * 4 * sub + dest * sub, sub)
-                out[m] = values[pl.ds(start, sub), :].astype(BF16)
+        half(w_ref)
+
+
+def forecast_kernel(
+    ids, hidden_ref, w_out_ref, b_out_ref, send0, send2, send1, send3, values
+):
+    mem_dev, sub, _ = send0.shape
+    values[...] = b_out_ref[...] + lax.dot_general(
+        hidden_ref[...], w_out_ref[...], (((1,), (1,)), ((), ())), preferred_element_type=F32
+    )
+    y = ids[0]
+    for k, out in enumerate((send0, send1, send2, send3)):
+        dest = y ^ k
+        for m in range(mem_dev):
+            start = pl.multiple_of(m * 4 * sub + dest * sub, sub)
+            out[m] = values[pl.ds(start, sub), :].astype(BF16)
 
 
 def loss_kernel(got0, got2, got1, got3, target_ref, weight_ref, loss_ref):
@@ -360,10 +357,10 @@
         pltpu.with_memory_space_constraint(arr, pltpu.HBM)
         for arr in (
             ranks, obs, area[None, :], var_weight[None, :],
-            x, w_in, b_in[None, :], b_out[None, :], w_out_t,
+            x, w_in, b_in[None, :], b_out[None, :],
         )
     ]
-    w_in_hbm, w_out_hbm = operands[5], operands[8]
+    w_in_hbm = operands[5]
     weight, bout, cot0, cot2, cot1, cot3, x, w_first, b_in, b_out = pl.pallas_call(
         cotangent_kernel,
         in_specs=[SMEM] + [hbm] * 8,
@@ -386,37 +383,24 @@
         ],
         compiler_params=PARAMS,
         name="cotangent",
-    )(ids, *operands[:8])
-    ids_later, cot2, cot1, cot3 = lax.optimization_barrier((ids, cot2, cot1, cot3))
+    )(ids, *operands)
+    b_in_later, cot2, cot1, cot3 = lax.optimization_barrier((b_in, cot2, cot1, cot3))
     cot2 = lax.ppermute(cot2, "y", pairs_of("y", 2))
     cot1 = lax.ppermute(cot1, "y", pairs_of("y", 1))
     cot3 = lax.ppermute(cot3, "y", pairs_of("y", 3))
 
     cols = hid // 2
     by_cols = lambda height: pl.BlockSpec((height, cols), lambda i: (0, i))
-    hidden, slope, w_out_t, val0, val2, val1, val3 = pl.pallas_call(
+    hidden, slope = pl.pallas_call(
         forward_kernel,
         grid=(hid // cols,),
-        in_specs=[
-            SMEM,
-            const_spec((rows, width)),
-            const_spec((width, cols)),
-            hbm,
-            by_cols(1),
-            by_cols(n_vars),
-            const_spec((1, n_vars)),
-        ],
-        out_specs=[by_cols(rows), by_cols(rows), by_cols(n_vars)] + [const_spec(sent.shape)] * 4,
-        out_shape=[shape((rows, hid), BF16), shape((rows, hid), F32), shape((n_vars, hid), BF16)]
-        + [sent] * 4,
-        scratch_shapes=[
-            pltpu.VMEM((rows, n_vars), F32),
-            pltpu.VMEM((width, cols), BF16),
-            pltpu.SemaphoreType.DMA,
-        ],
+        in_specs=[const_spec((rows, width)), const_spec((width, cols)), hbm, by_cols(1)],
+        out_specs=[by_cols(rows), by_cols(rows)],
+        out_shape=[shape((rows, hid), BF16), shape((rows, hid), F32)],
+        scratch_shapes=[pltpu.VMEM((width, cols), BF16), pltpu.SemaphoreType.DMA],
         compiler_params=PARAMS,
         name="forward",
-    )(ids_later, x, w_first, w_in_hbm, b_in, w_out_hbm, b_out)
+    )(x, w_first, w_in_hbm, b_in_later)
 
     n_plane = lax.axis_size(PLANE)
     block = width // (2 * n_plane)
@@ -449,8 +433,17 @@
         compiler_params=PARAMS,
         name="payload",
     )(keep, got)
-    payload, val2, val1, val3 = lax.optimization_barrier((payload, val2, val1, val3))
+    payload, hidden = lax.optimization_barrier((payload, hidden))
     landed = lax.all_to_all(payload, PLANE, 0, 0, tiled=True)
+    val0, val2, val1, val3 = pl.pallas_call(
+        forecast_kernel,
+        in_specs=[SMEM] + [whole] * 3,
+        out_specs=[whole] * 4,
+        out_shape=[sent] * 4,
+        scratch_shapes=[pltpu.VMEM((rows, n_vars), F32)],
+        compiler_params=PARAMS,
+        name="forecast",
+    )(ids, hidden, w_out_t, b_out)
     val2 = lax.ppermute(val2, "y", pairs_of("y", 2))
     val1 = lax.ppermute(val1, "y", pairs_of("y", 1))
     val3 = lax.ppermute(val3, "y", pairs_of("y", 3))

time: 82.3 us -> 82.9 us (level)
  local copies, waits for them, and re-layouts: 0.01 us -> 5.61 us
  waiting for transfers between devices: 16.6 us -> 12.8 us
  starting transfers between devices: 32 us -> 30.8 us
    unnamed x2 -> x20, local copies, waits for them, and re-layouts: 0.01 us -> 5.61 us
    all_to_all x1, waiting for transfers between devices: 13.4 us -> 10.3 us  [per_device(): landed = lax.all_to_all(payload, PLANE, 0, 0, tiled=True)]
    ppermute x1, starting transfers between devices: 4.42 us -> 3.46 us  [per_device(): theirs = lax.ppermute(mine, 'core', swap)]
    pallas_call x1 -> x2, Pallas kernels: 6.18 us -> 6.79 us  [the longest x1 4.86 us: per_device(): pl.pallas_call(forward_kernel, grid=(hid // cols,), in_specs=[const_spec(...]
  transfers between devices with their start and end apart: 12 -> 12, of which waited for: 4 -> 2; matrix products, arithmetic and copies ran while one was open for 0% -> 0% of each run, Pallas kernels for 11% -> 11%
where the time goes in v8:
time: 82.9 us; the launch traced here: 82.5 us
  starting transfers between devices  30.8 us (37%)
  Pallas kernels  18.6 us (22%)
  blocking collectives  13.6 us (16%)
  waiting for transfers between devices  12.8 us (15%)
  local copies, waits for them, and re-layouts  5.61 us (7%)
  between operations  0.98 us (1%)
    all_to_all x1, blocking collectives, per_device(): mine = lax.all_to_all(copies, PLANE, 0, 0, tiled=True)  13.6 us
    all_to_all x1, waiting for transfers between devices, per_device(): landed = lax.all_to_all(payload, PLANE, 0, 0, tiled=True)  10.3 us
    all_to_all x1, starting transfers between devices, per_device(): landed = lax.all_to_all(payload, PLANE, 0, 0, tiled=True)  6.66 us
    ppermute x1, starting transfers between devices, per_device(): part2 = lax.ppermute(part2, 'zhi', shift('zhi', 2))  6.09 us
    unnamed x20, local copies, waits for them, and re-layouts  5.61 us
    pallas_call x1, Pallas kernels, per_device(): pl.pallas_call(forward_kernel, grid=(hid // cols,), in_specs=[const_spec(...  4.86 us
    pallas_call x1, Pallas kernels, per_device(): pl.pallas_call(backward_kernel, in_specs=[SMEM] + [whole] * 9, out_specs=...  4 us
    ppermute x1, starting transfers between devices, per_device(): cot2 = lax.ppermute(cot2, 'y', pairs_of('y', 2))  3.74 us
  transfers between devices with their start and end apart: 12, of which 2 were waited for; matrix products, arithmetic and copies ran while one was open for 0% of the time, Pallas kernels for 11%

profile of v8, /device:TPU:1, one launch (start us, length us, event | category | flops | bytes accessed | tf_op | source)
XLA Modules:
  0.0 82.5 jit_solution(7124985541551380749)
XLA Ops:
  0.7 2.7 %cotangent.1 = (f32[64,100]{1,0:T(8,128)S(1)}, f32[1,100]{1,0:T(1,128)S(1)}, bf16[4,64,100]{2,1,0:T(8,128)(2,1)S(1)}, bf16[4,64,100]{2,1,0:T(8,128)(2,1)S(1)}, b...) custom-call(s32[3]{0:T(128)S(1)} %pad_add_fusion.ids.refs_0_, ...), custom_call_target="tpu_custom_call" | custom-call | tf_op jit(solution)/shard_map/cotangent/pallas_call | solution.py:364
  4.6 3.7 %collective-permute-start = (bf16[4,64,100]{2,1,0:T(8,128)(2,1)S(1)}, bf16[4,64,100]{2,1,0:T(8,128)(2,1)S(1)}, u32[]{:S(2)}, u32[]{:S(2)}) collective-permute-start(bf16[4,64,100]{2,1,0:T(8,128)(2,1)S(1)} %get-tuple-element.48), channel_id=1, source_target_pairs={{0,128},{64,192},{128,0},{192,64},{1,129},{65,193},{129,1},{193,65... | collective-permute-start | bytes 153608 | tf_op jit(solution)/shard_map/ppermute | solution.py:388
  9.1 4.9 %forward.1 = (bf16[1024,1024]{1,0:T(8,128)(2,1)S(1)}, f32[1024,1024]{1,0:T(8,128)S(1)}) custom-call(bf16[1024,1024]{1,0:T(8,128)(2,1)S(1)} %get-tuple-element.51.x_ref, bf16[1024,512]{1,0:T(8,128)(2,1)S(1)} %get-tuple-element.52.w_first, bf16[1024,1024]{1,0:T(8,128)(2,1)} %w_in_hbm.3, f32[1,1024]{1,0:T(1,128)S(1)} %get-tuple-element.53.b_in_ref), custom_call_target="tpu_custom_call" | custom-call | tf_op jit(solution)/shard_map/forward/pallas_call | solution.py:394
  14.0 4.0 %backward.1 = (f32[32,16,1152]{2,1,0:T(8,128)S(1)}, bf16[32,16,1152]{2,1,0:T(8,128)(2,1)S(1)}) custom-call(s32[3]{0:T(128)S(1)} %pad_add_fusion.ids.refs_0_, bf16[4,64,100]{2,1,0:T(8,128)(2,1)S(1)} %get-tuple-element.43.got0, bf16[4,64,100]{2,1,0:T(8,128)(2,1)S(1)} %collective-permute-done.got2, bf16[4,64,100]{2,1,0:T(8,128)(2,1)S(1)} %collective-permute-done.1.got1, ...), custom_call_target="tpu_custom_call" | custom-call | tf_op jit(solution)/shard_map/backward/pallas_call | solution.py:407
  18.0 2.9 %collective-permute-start.3 = (bf16[32,16,1152]{2,1,0:T(8,128)(2,1)S(1)}, bf16[32,16,1152]{2,1,0:T(8,128)(2,1)S(1)}, u32[]{:S(2)}, u32[]{:S(2)}) collective-permute-start(bf16[32,16,1152]{2,1,0:T(8,128)(2,1)S(1)} %get-tuple-element.58), channel_id=1, source_target_pairs={{0,4},{4,0},{1,5},{5,1},{2,6},{6,2},{3,7},{7,3},{8,12},{12,8},{9,1... | collective-permute-start | bytes 3538952 | tf_op jit(solution)/shard_map/ppermute | solution.py:425
  20.9 2.5 %collective-permute-done.3.got_ref = bf16[32,16,1152]{2,1,0:T(8,128)(2,1)S(1)} collective-permute-done((bf16[32,16,1152]{2,1,0:T(8,128)(2,1)S(1)}, bf16[32,16,1152]{2,1,0:T(8,128)(2,1)S(1)}, u32[]{:S(2)}, u32[]{:S(2)}) %collective-permute-start.3) | collective-permute-done | bytes 1179680 | tf_op jit(solution)/shard_map/ppermute | solution.py:425
  24.0 1.0 %copy-done = bf16[32,16,1152]{2,1,0:T(8,128)(2,1)} copy-done((bf16[32,16,1152]{2,1,0:T(8,128)(2,1)}, bf16[32,16,1152]{2,1,0:T(8,128)(2,1)S(1)}, u32[]{:S(2)}) %copy-start) | copy-done | bytes 1179672
  25.0 6.7 %all-to-all-start = ((bf16[32,16,1152]{2,1,0:T(8,128)(2,1)}), bf16[32,16,1152]{2,1,0:T(8,128)(2,1)S(1)}, u32[]{:S(2)}, u32[]{:S(2)}) async-start(bf16[32,16,1152]{2,1,0:T(8,128)(2,1)} %copy-done), calls=%async_computation | async-start | bytes 2359296 | tf_op jit(solution)/shard_map/all_to_all | solution.py:437
  31.7 0.6 copy-done.6
  32.3 0.7 copy-done.9
  33.0 1.9 %forecast.1 = (bf16[4,64,100]{2,1,0:T(8,128)(2,1)S(1)}, bf16[4,64,100]{2,1,0:T(8,128)(2,1)}, bf16[4,64,100]{2,1,0:T(8,128)(2,1)}, bf16[4,64,100]{2,1,0:T(8,128)(2,1)}) custom-call(s32[3]{0:T(128)S(1)} %copy-done.6, bf16[1024,1024]{1,0:T(8,128)(2,1)S(1)} %get-tuple-element.65.hidden_ref, bf16[100,1024]{1,0:T(8,128)(2,1)S(1)} %bitcast.23, f32[1,100]{1,0:T(1,128)S(1)} %copy-done.9), custom_call_target="tpu_custom_call" | custom-call | tf_op jit(solution)/shard_map/forecast/pallas_call | solution.py:438
  34.9 2.7 %collective-permute-start.7 = (bf16[4,64,100]{2,1,0:T(8,128)(2,1)}, bf16[4,64,100]{2,1,0:T(8,128)(2,1)S(1)}, u32[]{:S(2)}, u32[]{:S(2)}) collective-permute-start(bf16[4,64,100]{2,1,0:T(8,128)(2,1)} %get-tuple-element.68), channel_id=1, source_target_pairs={{0,128},{64,192},{128,0},{192,64},{1,129},{65,193},{129,1},{193,65... | collective-permute-start | bytes 153608 | tf_op jit(solution)/shard_map/ppermute | solution.py:447
  38.5 10.3 %all-to-all-done.landed_ref = bf16[32,16,1152]{2,1,0:T(8,128)(2,1)S(1)} async-done(((bf16[32,16,1152]{2,1,0:T(8,128)(2,1)}), bf16[32,16,1152]{2,1,0:T(8,128)(2,1)S(1)}, u32[]{:S(2)}, u32[]{:S(2)}) %all-to-all-start) | async-done | bytes 1179680 | tf_op jit(solution)/shard_map/all_to_all | solution.py:437
  48.8 0.7 copy-done.7
  49.5 0.8 plane_sum.1
  50.3 6.1 %collective-permute-start.4 = (f32[16,384]{1,0:T(8,128)S(1)}, f32[16,384]{1,0:T(8,128)S(1)}, u32[]{:S(2)}, u32[]{:S(2)}) collective-permute-start(f32[16,384]{1,0:T(8,128)S(1)} %get-tuple-element.62), channel_id=1, source_target_pairs={{0,2},{1,3},{2,0},{3,1},{4,6},{5,7},{6,4},{7,5},{8,10},{9,11},{10,... | collective-permute-start | bytes 73736 | tf_op jit(solution)/shard_map/ppermute | solution.py:468
  56.3 1.2 %collective-permute-start.5 = (f32[16,384]{1,0:T(8,128)S(1)}, f32[16,384]{1,0:T(8,128)S(1)}, u32[]{:S(2)}, u32[]{:S(2)}) collective-permute-start(f32[16,384]{1,0:T(8,128)S(1)} %get-tuple-element.63), channel_id=1, source_target_pairs={{0,1},{1,2},{2,3},{3,0},{4,5},{5,6},{6,7},{7,4},{8,9},{9,10},{10,1... | collective-permute-start | bytes 73736 | tf_op jit(solution)/shard_map/ppermute | solution.py:469
  57.5 2.4 %collective-permute-start.6 = (f32[16,384]{1,0:T(8,128)S(1)}, f32[16,384]{1,0:T(8,128)S(1)}, u32[]{:S(2)}, u32[]{:S(2)}) collective-permute-start(f32[16,384]{1,0:T(8,128)S(1)} %get-tuple-element.64), channel_id=1, source_target_pairs={{0,3},{1,0},{2,1},{3,2},{4,7},{5,4},{6,5},{7,6},{8,11},{9,8},{10,9... | collective-permute-start | bytes 73736 | tf_op jit(solution)/shard_map/ppermute | solution.py:470
  59.9 0.8 copy-done.2
  60.7 0.8 copy-done.4
  62.7 13.6 %all_to_all.10.refs_2_.refs_3_ = f32[32,16,128]{2,1,0:T(8,128)S(1)} all-to-all(f32[32,16,128]{2,1,0:T(8,128)S(1)} %get-tuple-element.73), channel_id=1, replica_groups=mesh['y'=4,'zlo'=2,'x'=4,'core'=2,'zhi'=4] {'y','zlo','x'}, dimensions={0} | all-to-all | bytes 524288 | tf_op jit(solution)/shard_map/all_to_all | solution.py:480
  76.3 3.5 %collective-permute-start.10 = (f32[32,16,128]{2,1,0:T(8,128)S(1)}, f32[32,16,128]{2,1,0:T(8,128)S(1)}, u32[]{:S(2)}, u32[]{:S(2)}) collective-permute-start(f32[32,16,128]{2,1,0:T(8,128)S(1)} %all_to_all.10.refs_2_.refs_3_), channel_id=1, source_target_pairs={{0,4},{4,0},{1,5},{5,1},{2,6},{6,2},{3,7},{7,3},{8,12},{12,8},{9,1... | collective-permute-start | bytes 786440 | tf_op jit(solution)/shard_map/ppermute | solution.py:481
  79.8 1.3 %unpack_own.1 = (f32[4,1024]{1,0:T(4,128)}, f32[100,1024]{1,0:T(8,128)}, f32[1,1024]{1,0:T(1,128)}) custom-call(s32[3]{0:T(128)S(1)} %copy-done.7, f32[4,1024]{1,0:T(4,128)S(1)} %get-tuple-element.72.refs_1_, f32[32,16,128]{2,1,0:T(8,128)S(1)} %all_to_all.10.refs_2_.refs_3_), custom_call_target="tpu_custom_call" | custom-call | tf_op jit(solution)/shard_map/unpack_own/pallas_call | solution.py:488
  81.1 1.3 %unpack_other.1 = (f32[100,1024]{1,0:T(8,128)}, f32[1,1024]{1,0:T(1,128)}, f32[1,100]{1,0:T(1,128)}, f32[1,1]{1,0:T(1,128)}) custom-call(s32[3]{0:T(128)S(1)} %copy-done.7, f32[100,1024]{1,0:T(8,128)} %get-tuple-element.74.refs_1_, f32[1,1024]{1,0:T(1,128)} %get-tuple-element.75.refs_2_, ...), custom_call_target="tpu_custom_call", output_to_operand_aliasing={{0}: (1, {}), {1}: (2, {})} | custom-call | tf_op jit(solution)/shard_map/unpack_other/pallas_call | solution.py:503
  (32 shorter events, 4.6 us)
Async XLA Ops:
  0.7 13.3 %copy-start.5 = (s32[3]{0:T(128)}, s32[3]{0:T(128)S(1)}, u32[]{:S(2)}) copy-start(s32[3]{0:T(128)S(1)} %pad_add_fusion.ids.refs_0_) | copy-start | bytes 40
  3.4 0.6 copy-start.3
  4.1 0.5 copy-start.8
  4.6 9.4 %collective-permute-start = (bf16[4,64,100]{2,1,0:T(8,128)(2,1)S(1)}, bf16[4,64,100]{2,1,0:T(8,128)(2,1)S(1)}, u32[]{:S(2)}, u32[]{:S(2)}) collective-permute-start(bf16[4,64,100]{2,1,0:T(8,128)(2,1)S(1)} %get-tuple-element.48), channel_id=1, source_target_pairs={{0,128},{64,192},{128,0},{192,64},{1,129},{65,193},{129,1},{193,65... | collective-permute-start | bytes 153608 | tf_op jit(solution)/shard_map/ppermute | solution.py:388
  8.3 5.7 %collective-permute-start.1 = (bf16[4,64,100]{2,1,0:T(8,128)(2,1)S(1)}, bf16[4,64,100]{2,1,0:T(8,128)(2,1)S(1)}, u32[]{:S(2)}, u32[]{:S(2)}) collective-permute-start(bf16[4,64,100]{2,1,0:T(8,128)(2,1)S(1)} %get-tuple-element.49), channel_id=1, source_target_pairs={{0,64},{64,0},{128,192},{192,128},{1,65},{65,1},{129,193},{193,129... | collective-permute-start | bytes 153608 | tf_op jit(solution)/shard_map/ppermute | solution.py:389
  8.7 5.3 %collective-permute-start.2 = (bf16[4,64,100]{2,1,0:T(8,128)(2,1)S(1)}, bf16[4,64,100]{2,1,0:T(8,128)(2,1)S(1)}, u32[]{:S(2)}, u32[]{:S(2)}) collective-permute-start(bf16[4,64,100]{2,1,0:T(8,128)(2,1)S(1)} %get-tuple-element.50), channel_id=1, source_target_pairs={{0,192},{64,128},{128,64},{192,0},{1,193},{65,129},{129,65},{193,1... | collective-permute-start | bytes 153608 | tf_op jit(solution)/shard_map/ppermute | solution.py:390
  9.1 4.9 %copy-start.1 = (bf16[1024,100]{0,1:T(8,128)(2,1)S(1)}, bf16[1024,100]{0,1:T(8,128)(2,1)}, u32[]{:S(2)}) copy-start(bf16[1024,100]{0,1:T(8,128)(2,1)} %param.13) | copy-start | bytes 614404
  18.0 5.4 %collective-permute-start.3 = (bf16[32,16,1152]{2,1,0:T(8,128)(2,1)S(1)}, bf16[32,16,1152]{2,1,0:T(8,128)(2,1)S(1)}, u32[]{:S(2)}, u32[]{:S(2)}) collective-permute-start(bf16[32,16,1152]{2,1,0:T(8,128)(2,1)S(1)} %get-tuple-element.58), channel_id=1, source_target_pairs={{0,4},{4,0},{1,5},{5,1},{2,6},{6,2},{3,7},{7,3},{8,12},{12,8},{9,1... | collective-permute-start | bytes 3538952 | tf_op jit(solution)/shard_map/ppermute | solution.py:425
  24.0 1.0 %copy-start = (bf16[32,16,1152]{2,1,0:T(8,128)(2,1)}, bf16[32,16,1152]{2,1,0:T(8,128)(2,1)S(1)}, u32[]{:S(2)}) copy-start(bf16[32,16,1152]{2,1,0:T(8,128)(2,1)S(1)} %payload.1) | copy-start | bytes 3538948
  25.0 23.8 %all-to-all-start = ((bf16[32,16,1152]{2,1,0:T(8,128)(2,1)}), bf16[32,16,1152]{2,1,0:T(8,128)(2,1)S(1)}, u32[]{:S(2)}, u32[]{:S(2)}) async-start(bf16[32,16,1152]{2,1,0:T(8,128)(2,1)} %copy-done), calls=%async_computation | async-start | bytes 2359296 | tf_op jit(solution)/shard_map/all_to_all | solution.py:437
  31.7 0.7 copy-start.6
  32.3 0.7 copy-start.9
  34.9 22.6 %collective-permute-start.7 = (bf16[4,64,100]{2,1,0:T(8,128)(2,1)}, bf16[4,64,100]{2,1,0:T(8,128)(2,1)S(1)}, u32[]{:S(2)}, u32[]{:S(2)}) collective-permute-start(bf16[4,64,100]{2,1,0:T(8,128)(2,1)} %get-tuple-element.68), channel_id=1, source_target_pairs={{0,128},{64,192},{128,0},{192,64},{1,129},{65,193},{129,1},{193,65... | collective-permute-start | bytes 153608 | tf_op jit(solution)/shard_map/ppermute | solution.py:447
  37.7 22.3 %collective-permute-start.8 = (bf16[4,64,100]{2,1,0:T(8,128)(2,1)}, bf16[4,64,100]{2,1,0:T(8,128)(2,1)S(1)}, u32[]{:S(2)}, u32[]{:S(2)}) collective-permute-start(bf16[4,64,100]{2,1,0:T(8,128)(2,1)} %get-tuple-element.69), channel_id=1, source_target_pairs={{0,64},{64,0},{128,192},{192,128},{1,65},{65,1},{129,193},{193,129... | collective-permute-start | bytes 153608 | tf_op jit(solution)/shard_map/ppermute | solution.py:448
  38.0 22.0 %collective-permute-start.9 = (bf16[4,64,100]{2,1,0:T(8,128)(2,1)}, bf16[4,64,100]{2,1,0:T(8,128)(2,1)S(1)}, u32[]{:S(2)}, u32[]{:S(2)}) collective-permute-start(bf16[4,64,100]{2,1,0:T(8,128)(2,1)} %get-tuple-element.70), channel_id=1, source_target_pairs={{0,192},{64,128},{128,64},{192,0},{1,193},{65,129},{129,65},{193,1... | collective-permute-start | bytes 153608 | tf_op jit(solution)/shard_map/ppermute | solution.py:449
  48.8 0.7 copy-start.7
  50.3 11.8 %collective-permute-start.4 = (f32[16,384]{1,0:T(8,128)S(1)}, f32[16,384]{1,0:T(8,128)S(1)}, u32[]{:S(2)}, u32[]{:S(2)}) collective-permute-start(f32[16,384]{1,0:T(8,128)S(1)} %get-tuple-element.62), channel_id=1, source_target_pairs={{0,2},{1,3},{2,0},{3,1},{4,6},{5,7},{6,4},{7,5},{8,10},{9,11},{10,... | collective-permute-start | bytes 73736 | tf_op jit(solution)/shard_map/ppermute | solution.py:468
  56.3 5.7 %collective-permute-start.5 = (f32[16,384]{1,0:T(8,128)S(1)}, f32[16,384]{1,0:T(8,128)S(1)}, u32[]{:S(2)}, u32[]{:S(2)}) collective-permute-start(f32[16,384]{1,0:T(8,128)S(1)} %get-tuple-element.63), channel_id=1, source_target_pairs={{0,1},{1,2},{2,3},{3,0},{4,5},{5,6},{6,7},{7,4},{8,9},{9,10},{10,1... | collective-permute-start | bytes 73736 | tf_op jit(solution)/shard_map/ppermute | solution.py:469
  57.5 4.5 %collective-permute-start.6 = (f32[16,384]{1,0:T(8,128)S(1)}, f32[16,384]{1,0:T(8,128)S(1)}, u32[]{:S(2)}, u32[]{:S(2)}) collective-permute-start(f32[16,384]{1,0:T(8,128)S(1)} %get-tuple-element.64), channel_id=1, source_target_pairs={{0,3},{1,0},{2,1},{3,2},{4,7},{5,4},{6,5},{7,6},{8,11},{9,8},{10,9... | collective-permute-start | bytes 73736 | tf_op jit(solution)/shard_map/ppermute | solution.py:470
  59.9 0.8 copy-start.2
  60.7 0.8 copy-start.4
  76.3 4.8 %collective-permute-start.10 = (f32[32,16,128]{2,1,0:T(8,128)S(1)}, f32[32,16,128]{2,1,0:T(8,128)S(1)}, u32[]{:S(2)}, u32[]{:S(2)}) collective-permute-start(f32[32,16,128]{2,1,0:T(8,128)S(1)} %all_to_all.10.refs_2_.refs_3_), channel_id=1, source_target_pairs={{0,4},{4,0},{1,5},{5,1},{2,6},{6,2},{3,7},{7,3},{8,12},{12,8},{9,1... | collective-permute-start | bytes 786440 | tf_op jit(solution)/shard_map/ppermute | solution.py:481
